TPU v7x, 32 devices: a whole 2x2x4 slice. The times are simulated.
32 devices in a mesh: ctx: 8 (over y, x, core), fsdp: 4 (over z).
Axes of the slice: x: 2, y: 2, z: 4, core: 2. Of those that a mesh axis runs over, the one named last changes fastest.
Arguments:
- hidden_in: bfloat16 [4, 2048, 2048], P('fsdp', 'ctx'), may hold values from -6 to 6
- out_grad: bfloat16 [4, 2048, 2048], P('fsdp', 'ctx'), may hold values from -6 to 6
- seq_lengths: int32 [4, 3], P('fsdp'), may hold values from 1 to 1024, as said below
- block_perm: int32 [16], replicated, may hold values from 0 to 15, as said below
- first_gain: bfloat16 [2048], P('fsdp'), may hold values from 0.5 to 1.5
- query_weight: bfloat16 [2048, 2048], P(None, 'fsdp'), may hold values from -0.125 to 0.125
- key_matrix: bfloat16 [2048, 1024], P(None, 'fsdp'), may hold values from -0.125 to 0.125
- value_matrix: bfloat16 [2048, 1024], P(None, 'fsdp'), may hold values from -0.125 to 0.125
- output_weight: bfloat16 [2048, 2048], P(None, 'fsdp'), may hold values from -3 to 3
- second_gain: bfloat16 [2048], P('fsdp'), may hold values from 0.5 to 1.5
- gate_weight: bfloat16 [2048, 8192], P(None, 'fsdp'), may hold values from -0.125 to 0.125
- up_weight: bfloat16 [2048, 8192], P(None, 'fsdp'), may hold values from -0.125 to 0.125
- down_weight: bfloat16 [8192, 2048], P(None, 'fsdp'), may hold values from -0.0625 to 0.0625
- clip_limit: float32 [16], replicated, may hold values from 2 to 12
Outputs:
- layer_output: bfloat16 [4, 2048, 2048], P('fsdp', 'ctx')
- input_grad: bfloat16 [4, 2048, 2048], P('fsdp', 'ctx')
- first_gain_grad: float32 [2048], P(('ctx', 'fsdp'))
- query_grad: float32 [2048, 2048], P('ctx', 'fsdp')
- key_grad: float32 [2048, 1024], P('ctx', 'fsdp')
- value_grad: float32 [2048, 1024], P('ctx', 'fsdp')
- output_grad: float32 [2048, 2048], P('ctx', 'fsdp')
- second_gain_grad: float32 [2048], P(('ctx', 'fsdp'))
- gate_grad: float32 [2048, 8192], P('ctx', 'fsdp')
- up_grad: float32 [2048, 8192], P('ctx', 'fsdp')
- down_grad: float32 [8192, 2048], P('ctx', 'fsdp')
- head_max: float32 [16], replicated
- query_clipped: bfloat16 [2048, 2048], P(None, 'fsdp')
- key_clipped: bfloat16 [2048, 1024], P(None, 'fsdp')
Inputs may be any that keep to these rules, and one draw needn't show every extreme that they name: `seq_lengths`: in each row the first length is 1024, and the later ones come in consecutive pairs that sum to 1024; each row sums to 2048. `block_perm`: A permutation; slots d * 2 to d * 2 + 1 lie on ctx index d. Block b lies in slot number b // 8 of its device; the blocks of one round b // 8 go to distinct devices, even rounds in one order of the devices and odd rounds in the reverse of that order.
All inputs are finite; a program needn't handle non-finite values.
Results may differ from a plain program's by a relative error of at most 0.02.
Values may be sent and summed in bfloat16 or wider, within the bound.
A program may use at most 576 MiB of HBM per device.

v0:
```python
import math

import jax
import jax.numpy as jnp
from jax import lax
from jax.sharding import PartitionSpec as P

QUERY_HEADS = 16
KEY_VALUE_HEADS = 8
HEAD_SIZE = 128


epsilon = 1e-06
rope_base = 1000000.0
hidden_fill_value = -1e30


def token_layout(length_row, block_slots, block_size):
    count_blocks = block_slots.shape[0]
    owner_block = (
        jnp.zeros((count_blocks,), jnp.int32)
        .at[block_slots]
        .set(jnp.arange(count_blocks, dtype=jnp.int32))
    )
    row_index = jnp.arange(count_blocks * block_size, dtype=jnp.int32)
    plain_order = jnp.repeat(owner_block, block_size) * block_size + row_index % block_size
    seq_ends = jnp.cumsum(length_row)
    seq_starts = seq_ends - length_row
    document_list = jnp.sum((plain_order[:, None] >= seq_ends[None, :]).astype(jnp.int32), 1)
    matches = document_list[:, None] == jnp.arange(length_row.shape[0], dtype=jnp.int32)[None, :]
    begins = jnp.sum(jnp.where(matches, seq_starts[None, :], 0), 1)
    return (plain_order, document_list, plain_order - begins)


def rope_tables(positions, head_dim):
    half_dim = head_dim // 2
    exponent = jnp.arange(half_dim, dtype=jnp.float32) * (2.0 / head_dim)
    inverse = rope_base ** (-exponent)
    angles = positions.astype(jnp.float32)[:, None] * inverse[None, :]
    return (jnp.cos(angles), jnp.sin(angles))


def apply_rotation(value_tensor, cosine_table, sine_values):
    half_dim = value_tensor.shape[-1] // 2
    first_half = value_tensor[..., :half_dim]
    second_half = value_tensor[..., half_dim:]
    cos_rows = cosine_table[:, None, :]
    sin_rows = sine_values[:, None, :]
    return jnp.concatenate(
        [
            first_half * cos_rows - second_half * sin_rows,
            second_half * cos_rows + first_half * sin_rows,
        ],
        -1,
    )


def reverse_rotation(value_tensor, cosine_table, sine_values):
    half_dim = value_tensor.shape[-1] // 2
    first_half = value_tensor[..., :half_dim]
    second_half = value_tensor[..., half_dim:]
    cos_rows = cosine_table[:, None, :]
    sin_rows = sine_values[:, None, :]
    return jnp.concatenate(
        [
            first_half * cos_rows + second_half * sin_rows,
            second_half * cos_rows - first_half * sin_rows,
        ],
        -1,
    )


def rms_scale(value_tensor):
    return lax.rsqrt(jnp.mean(value_tensor * value_tensor, -1, keepdims=True) + epsilon)


def norm_back(grad_unit, unit_rows, scale_rows):
    return scale_rows * (grad_unit - unit_rows * jnp.mean(grad_unit * unit_rows, -1, keepdims=True))


def matrix_product(left_side, right_side):
    return jnp.dot(left_side, right_side, preferred_element_type=jnp.float32)


def matmul_t(left_side, right_side):
    return lax.dot_general(
        left_side, right_side, (((1,), (1,)), ((), ())), preferred_element_type=jnp.float32
    )


def over_rows(left_side, right_side):
    return lax.dot_general(
        left_side, right_side, (((0,), (0,)), ((), ())), preferred_element_type=jnp.float32
    )


def keep_state(carried):
    return carried


def over_keys(step_fn, running, pieces):
    total_quantity = pieces[0].shape[0]
    block_len = math.gcd(total_quantity, 1024)
    turn_count = total_quantity // block_len
    stacked = tuple(
        (
            piece_rows.reshape((turn_count, block_len) + piece_rows.shape[1:])
            for piece_rows in pieces
        )
    )

    def advance(carried, scan_item):
        turn_index, sub_pieces = scan_item
        return (step_fn(carried, sub_pieces, turn_index * block_len), None)

    finished, unused = lax.scan(
        advance, running, (jnp.arange(turn_count, dtype=jnp.int32), stacked)
    )
    return finished


def gather_weights(
    first_gain,
    query_weight,
    key_matrix,
    value_matrix,
    output_weight,
    second_gain,
    gate_weight,
    up_weight,
    down_weight,
):
    return (
        lax.all_gather(first_gain, "fsdp", axis=0, tiled=True),
        lax.all_gather(query_weight, "fsdp", axis=1, tiled=True),
        lax.all_gather(key_matrix, "fsdp", axis=1, tiled=True),
        lax.all_gather(value_matrix, "fsdp", axis=1, tiled=True),
        lax.all_gather(output_weight, "fsdp", axis=1, tiled=True),
        lax.all_gather(second_gain, "fsdp", axis=0, tiled=True),
        lax.all_gather(gate_weight, "fsdp", axis=1, tiled=True),
        lax.all_gather(up_weight, "fsdp", axis=1, tiled=True),
        lax.all_gather(down_weight, "fsdp", axis=1, tiled=True),
    )


def clipped(weight, multiplier):
    columns = weight.shape[1]
    head_index = (
        lax.axis_index("fsdp") * columns + jnp.arange(columns, dtype=jnp.int32)
    ) // HEAD_SIZE
    matches = head_index[:, None] == jnp.arange(multiplier.shape[0], dtype=jnp.int32)[None, :]
    column_factor = jnp.sum(jnp.where(matches, multiplier[None, :], 0.0), 1)
    return (weight.astype(jnp.float32) * column_factor[None, :]).astype(jnp.bfloat16)


def on_device(
    hidden_in,
    out_grad,
    seq_lengths,
    block_perm,
    first_gain,
    query_weight,
    key_matrix,
    value_matrix,
    output_weight,
    second_gain,
    gate_weight,
    up_weight,
    down_weight,
    clip_limit,
):
    nearby_rows = hidden_in.shape[1]
    model_width = hidden_in.shape[2]
    rows_in_group = nearby_rows * lax.axis_size("ctx")
    block_size = rows_in_group // block_perm.shape[0]
    repeat_count = QUERY_HEADS // KEY_VALUE_HEADS
    scale_of_score = 1.0 / math.sqrt(HEAD_SIZE)
    plain_order, document_list, positions = token_layout(seq_lengths[0], block_perm, block_size)
    first_row = lax.axis_index("ctx") * nearby_rows
    query_natural = lax.dynamic_slice_in_dim(plain_order, first_row, nearby_rows)
    query_docs = lax.dynamic_slice_in_dim(document_list, first_row, nearby_rows)
    query_positions = lax.dynamic_slice_in_dim(positions, first_row, nearby_rows)
    cosine_table, sine_values = rope_tables(query_positions, HEAD_SIZE)

    def allowed_for(offset, total_quantity):
        key_natural = lax.dynamic_slice_in_dim(plain_order, offset, total_quantity)
        key_docs = lax.dynamic_slice_in_dim(document_list, offset, total_quantity)
        return (query_docs[:, None] == key_docs[None, :]) & (
            key_natural[None, :] <= query_natural[:, None]
        )

    tokens = hidden_in.reshape(nearby_rows, model_width).astype(jnp.float32)
    full_weights = gather_weights(
        first_gain,
        query_weight,
        key_matrix,
        value_matrix,
        output_weight,
        second_gain,
        gate_weight,
        up_weight,
        down_weight,
    )
    (
        full_first,
        full_query,
        full_key,
        full_value,
        full_output,
        full_second,
        full_gate,
        full_up,
        full_down,
    ) = full_weights
    scale_one = rms_scale(tokens)
    unit_one = tokens * scale_one
    normalized = (unit_one * full_first.astype(jnp.float32)).astype(jnp.bfloat16)
    query_lin = matrix_product(normalized, full_query)
    key_linear = matrix_product(normalized, full_key)
    values_local = matrix_product(normalized, full_value).astype(jnp.bfloat16)
    query_matrix = (
        apply_rotation(
            query_lin.reshape(nearby_rows, QUERY_HEADS, HEAD_SIZE), cosine_table, sine_values
        )
        .astype(jnp.bfloat16)
        .reshape(nearby_rows, KEY_VALUE_HEADS, repeat_count, HEAD_SIZE)
    )
    keys_local = (
        apply_rotation(
            key_linear.reshape(nearby_rows, KEY_VALUE_HEADS, HEAD_SIZE), cosine_table, sine_values
        )
        .astype(jnp.bfloat16)
        .reshape(nearby_rows, KEY_VALUE_HEADS * HEAD_SIZE)
    )

    def score_block(key_portion, allowed):
        total_quantity = key_portion.shape[0]
        score_matrix = (
            jnp.einsum(
                "pzjw,vzw->zjpv",
                query_matrix,
                key_portion.reshape(total_quantity, KEY_VALUE_HEADS, HEAD_SIZE),
                preferred_element_type=jnp.float32,
            )
            * scale_of_score
        )
        return jnp.where(allowed, score_matrix, hidden_fill_value)

    def stats_step(running, pieces, offset):
        allowed = allowed_for(offset, pieces[0].shape[0])

        def stats_update(carried):
            row_best, row_total = carried
            score_matrix = score_block(pieces[0], allowed)
            newest = jnp.maximum(row_best, jnp.max(score_matrix, -1))
            exps = jnp.where(allowed, jnp.exp(score_matrix - newest[..., None]), 0.0)
            return (newest, row_total * jnp.exp(row_best - newest) + jnp.sum(exps, -1))

        return lax.cond(jnp.any(allowed), stats_update, keep_state, running)

    stats_start = (
        jnp.full((KEY_VALUE_HEADS, repeat_count, nearby_rows), hidden_fill_value, jnp.float32),
        jnp.zeros((KEY_VALUE_HEADS, repeat_count, nearby_rows), jnp.float32),
    )
    row_best, row_total = over_keys(
        stats_step, stats_start, (lax.all_gather(keys_local, "ctx", axis=0, tiled=True),)
    )
    log_total = row_best + jnp.log(row_total)
    head_max = lax.pmax(jnp.max(row_best, -1).reshape(QUERY_HEADS), ("ctx", "fsdp"))

    def value_step(running, pieces, offset):
        key_portion, value_portion = pieces
        total_quantity = key_portion.shape[0]
        allowed = allowed_for(offset, total_quantity)

        def value_update(carried):
            score_matrix = score_block(key_portion, allowed)
            softmax_probs = jnp.where(
                allowed, jnp.exp(score_matrix - log_total[..., None]), 0.0
            ).astype(jnp.bfloat16)
            return carried + jnp.einsum(
                "jzxn,njo->jzxo",
                softmax_probs,
                value_portion.reshape(total_quantity, KEY_VALUE_HEADS, HEAD_SIZE),
                preferred_element_type=jnp.float32,
            )

        return lax.cond(jnp.any(allowed), value_update, keep_state, running)

    merged_heads = over_keys(
        value_step,
        jnp.zeros((KEY_VALUE_HEADS, repeat_count, nearby_rows, HEAD_SIZE), jnp.float32),
        (
            lax.all_gather(keys_local, "ctx", axis=0, tiled=True),
            lax.all_gather(values_local, "ctx", axis=0, tiled=True),
        ),
    )
    attended = (
        merged_heads.transpose(2, 0, 1, 3)
        .reshape(nearby_rows, QUERY_HEADS * HEAD_SIZE)
        .astype(jnp.bfloat16)
    )
    residual = tokens + matrix_product(attended, full_output)
    scale_two = rms_scale(residual)
    unit_two = residual * scale_two
    normed_two = (unit_two * full_second.astype(jnp.float32)).astype(jnp.bfloat16)
    gate_act = matrix_product(normed_two, full_gate)
    up_proj = matrix_product(normed_two, full_up)
    hidden = (jax.nn.silu(gate_act) * up_proj).astype(jnp.bfloat16)
    result = (residual + matrix_product(hidden, full_down)).astype(jnp.bfloat16)
    back_weights = gather_weights(
        first_gain,
        query_weight,
        key_matrix,
        value_matrix,
        output_weight,
        second_gain,
        gate_weight,
        up_weight,
        down_weight,
    )
    (
        back_first,
        back_query,
        back_key,
        back_value,
        back_output,
        back_second,
        back_gate,
        back_up,
        back_down,
    ) = back_weights
    rows_normed, rows_attended, rows_two, rows_hidden = (
        lax.all_gather(normalized, "fsdp", axis=0, tiled=True),
        lax.all_gather(attended, "fsdp", axis=0, tiled=True),
        lax.all_gather(normed_two, "fsdp", axis=0, tiled=True),
        lax.all_gather(hidden, "fsdp", axis=0, tiled=True),
    )
    grad_out = out_grad.reshape(nearby_rows, model_width)
    grad_hidden = matmul_t(grad_out, back_down)
    sigmoid_gate = jax.nn.sigmoid(gate_act)
    grad_gate = (
        grad_hidden * up_proj * sigmoid_gate * (1.0 + gate_act * (1.0 - sigmoid_gate))
    ).astype(jnp.bfloat16)
    grad_up = (grad_hidden * gate_act * sigmoid_gate).astype(jnp.bfloat16)
    gate_cols, up_cols, out_cols = (
        lax.all_to_all(grad_gate, "fsdp", split_axis=1, concat_axis=0, tiled=True),
        lax.all_to_all(grad_up, "fsdp", split_axis=1, concat_axis=0, tiled=True),
        lax.all_to_all(grad_out, "fsdp", split_axis=1, concat_axis=0, tiled=True),
    )
    gate_rows, up_rows, down_rows = (
        lax.psum_scatter(
            over_rows(rows_two, gate_cols).astype(jnp.bfloat16),
            "ctx",
            scatter_dimension=0,
            tiled=True,
        ).astype(jnp.float32),
        lax.psum_scatter(
            over_rows(rows_two, up_cols).astype(jnp.bfloat16),
            "ctx",
            scatter_dimension=0,
            tiled=True,
        ).astype(jnp.float32),
        lax.psum_scatter(
            over_rows(rows_hidden, out_cols).astype(jnp.bfloat16),
            "ctx",
            scatter_dimension=0,
            tiled=True,
        ).astype(jnp.float32),
    )
    grad_normed_two = matmul_t(grad_gate, back_gate) + matmul_t(grad_up, back_up)
    second_term = jnp.sum(grad_normed_two * unit_two, 0)
    grad_residual = grad_out.astype(jnp.float32) + norm_back(
        grad_normed_two * back_second.astype(jnp.float32), unit_two, scale_two
    )
    grad_branch = grad_residual.astype(jnp.bfloat16)
    attended_gradient = matmul_t(grad_branch, back_output).astype(jnp.bfloat16)
    head_gradient = attended_gradient.reshape(nearby_rows, KEY_VALUE_HEADS, repeat_count, HEAD_SIZE)
    delta_terms = jnp.einsum("njel,jenl->jen", head_gradient.astype(jnp.float32), merged_heads)

    def grad_step(running, pieces, offset):
        key_portion, value_portion = pieces
        total_quantity = key_portion.shape[0]
        allowed = allowed_for(offset, total_quantity)

        def grad_update(carried):
            grad_query, grad_keys = carried
            heads_of_key = key_portion.reshape(total_quantity, KEY_VALUE_HEADS, HEAD_SIZE)
            heads_of_value = value_portion.reshape(total_quantity, KEY_VALUE_HEADS, HEAD_SIZE)
            score_matrix = score_block(key_portion, allowed)
            softmax_probs = jnp.where(allowed, jnp.exp(score_matrix - log_total[..., None]), 0.0)
            grad_probs = jnp.einsum(
                "pzjw,vzw->zjpv", head_gradient, heads_of_value, preferred_element_type=jnp.float32
            )
            score_gradient = (softmax_probs * (grad_probs - delta_terms[..., None])).astype(
                jnp.bfloat16
            )
            grad_query = (
                grad_query
                + jnp.einsum(
                    "jzxn,njo->jzxo",
                    score_gradient,
                    heads_of_key,
                    preferred_element_type=jnp.float32,
                )
                * scale_of_score
            )
            key_delta_sum = (
                jnp.einsum(
                    "zpjy,jzpq->yzq",
                    score_gradient,
                    query_matrix,
                    preferred_element_type=jnp.float32,
                )
                * scale_of_score
            )
            value_delta_sum = jnp.einsum(
                "zpjy,jzpq->yzq",
                softmax_probs.astype(jnp.bfloat16),
                head_gradient,
                preferred_element_type=jnp.float32,
            )
            changes = jnp.stack(
                [
                    key_delta_sum.reshape(total_quantity, KEY_VALUE_HEADS * HEAD_SIZE),
                    value_delta_sum.reshape(total_quantity, KEY_VALUE_HEADS * HEAD_SIZE),
                ],
                1,
            )
            current = lax.dynamic_slice_in_dim(grad_keys, offset, total_quantity, 0)
            grad_keys = lax.dynamic_update_slice_in_dim(grad_keys, current + changes, offset, 0)
            return (grad_query, grad_keys)

        return lax.cond(jnp.any(allowed), grad_update, keep_state, running)

    grad_start = (
        jnp.zeros((KEY_VALUE_HEADS, repeat_count, nearby_rows, HEAD_SIZE), jnp.float32),
        jnp.zeros((rows_in_group, 2, KEY_VALUE_HEADS * HEAD_SIZE), jnp.float32),
    )
    grad_query, grad_keys = over_keys(
        grad_step,
        grad_start,
        (
            lax.all_gather(keys_local, "ctx", axis=0, tiled=True),
            lax.all_gather(values_local, "ctx", axis=0, tiled=True),
        ),
    )
    local_gradients = lax.psum_scatter(
        grad_keys.astype(jnp.bfloat16), "ctx", scatter_dimension=0, tiled=True
    ).astype(jnp.float32)
    key_grad = (
        reverse_rotation(
            local_gradients[:, 0].reshape(nearby_rows, KEY_VALUE_HEADS, HEAD_SIZE),
            cosine_table,
            sine_values,
        )
        .reshape(nearby_rows, KEY_VALUE_HEADS * HEAD_SIZE)
        .astype(jnp.bfloat16)
    )
    value_grad = local_gradients[:, 1].astype(jnp.bfloat16)
    query_grad = (
        reverse_rotation(
            grad_query.transpose(2, 0, 1, 3).reshape(nearby_rows, QUERY_HEADS, HEAD_SIZE),
            cosine_table,
            sine_values,
        )
        .reshape(nearby_rows, QUERY_HEADS * HEAD_SIZE)
        .astype(jnp.bfloat16)
    )
    query_cols, key_cols, value_cols, branch_cols = (
        lax.all_to_all(query_grad, "fsdp", split_axis=1, concat_axis=0, tiled=True),
        lax.all_to_all(key_grad, "fsdp", split_axis=1, concat_axis=0, tiled=True),
        lax.all_to_all(value_grad, "fsdp", split_axis=1, concat_axis=0, tiled=True),
        lax.all_to_all(grad_branch, "fsdp", split_axis=1, concat_axis=0, tiled=True),
    )
    grad_normed_one = (
        matmul_t(query_grad, back_query)
        + matmul_t(key_grad, back_key)
        + matmul_t(value_grad, back_value)
    )
    first_term = jnp.sum(grad_normed_one * unit_one, 0)
    grad_input = grad_residual + norm_back(
        grad_normed_one * back_first.astype(jnp.float32), unit_one, scale_one
    )
    query_rows, rows_of_key, value_rows, output_rows = (
        lax.psum_scatter(
            over_rows(rows_normed, query_cols).astype(jnp.bfloat16),
            "ctx",
            scatter_dimension=0,
            tiled=True,
        ).astype(jnp.float32),
        lax.psum_scatter(
            over_rows(rows_normed, key_cols).astype(jnp.bfloat16),
            "ctx",
            scatter_dimension=0,
            tiled=True,
        ).astype(jnp.float32),
        lax.psum_scatter(
            over_rows(rows_normed, value_cols).astype(jnp.bfloat16),
            "ctx",
            scatter_dimension=0,
            tiled=True,
        ).astype(jnp.float32),
        lax.psum_scatter(
            over_rows(rows_attended, branch_cols).astype(jnp.bfloat16),
            "ctx",
            scatter_dimension=0,
            tiled=True,
        ).astype(jnp.float32),
    )
    first_rows, second_rows = (
        lax.psum_scatter(first_term, ("ctx", "fsdp"), scatter_dimension=0, tiled=True),
        lax.psum_scatter(second_term, ("ctx", "fsdp"), scatter_dimension=0, tiled=True),
    )
    multiplier = jnp.sqrt(clip_limit / jnp.maximum(head_max, clip_limit))
    key_value_ratio = jnp.min(multiplier.reshape(KEY_VALUE_HEADS, repeat_count), 1)
    query_clipped = clipped(query_weight, multiplier)
    key_clipped = clipped(key_matrix, key_value_ratio)
    return (
        result.reshape(1, nearby_rows, model_width),
        grad_input.astype(jnp.bfloat16).reshape(1, nearby_rows, model_width),
        first_rows,
        query_rows,
        rows_of_key,
        value_rows,
        output_rows,
        second_rows,
        gate_rows,
        up_rows,
        down_rows,
        head_max,
        query_clipped,
        key_clipped,
    )


def solution(mesh):
    placed = (
        P("fsdp", "ctx", None),
        P("fsdp", "ctx", None),
        P("fsdp", None),
        P(),
        P("fsdp"),
        P(None, "fsdp"),
        P(None, "fsdp"),
        P(None, "fsdp"),
        P(None, "fsdp"),
        P("fsdp"),
        P(None, "fsdp"),
        P(None, "fsdp"),
        P(None, "fsdp"),
        P(),
    )
    return jax.shard_map(
        on_device,
        mesh=mesh,
        in_specs=placed,
        out_specs=(
            P("fsdp", "ctx", None),
            P("fsdp", "ctx", None),
            P(("ctx", "fsdp")),
            P("ctx", "fsdp"),
            P("ctx", "fsdp"),
            P("ctx", "fsdp"),
            P("ctx", "fsdp"),
            P(("ctx", "fsdp")),
            P("ctx", "fsdp"),
            P("ctx", "fsdp"),
            P("ctx", "fsdp"),
            P(),
            P(None, "fsdp"),
            P(None, "fsdp"),
        ),
        check_vma=False,
    )
```

profile of v0, /device:TPU:0, one launch (start us, length us, event | category | flops | bytes accessed | tf_op | source)
XLA Modules:
  0.0 3738.4 jit_solution(4472810882910343752)
XLA Ops:
  24.9 68.0 %all-gather.16.cloned.1.call-done = bf16[2048,1024]{1,0:T(8,128)(2,1)} async-done(((bf16[2048,256]{1,0:T(8,128)(2,1)}), bf16[2048,1024]{1,0:T(8,128)(2,1)}) %all-gather.16.cloned.1.call-update) | async-done | bytes 4194320 | tf_op jit(solution)/shard_map/all_gather | solution.py:136
  104.9 68.3 %all-gather.22.cloned.1.call-done = bf16[2048,1024]{1,0:T(8,128)(2,1)} async-done(((bf16[2048,256]{1,0:T(8,128)(2,1)}), bf16[2048,1024]{1,0:T(8,128)(2,1)}) %all-gather.22.cloned.1.call-update) | async-done | bytes 4194320 | tf_op jit(solution)/shard_map/all_gather | solution.py:137
  193.2 129.6 %all-gather.20.cloned.1.call-done = bf16[2048,2048]{1,0:T(8,128)(2,1)} async-done(((bf16[2048,512]{1,0:T(8,128)(2,1)}), bf16[2048,2048]{1,0:T(8,128)(2,1)}) %all-gather.20.cloned.1.call-update) | async-done | bytes 8388624 | tf_op jit(solution)/shard_map/all_gather | solution.py:135
  366.3 32.8 all-gather.24.cloned.1.call-done
  405.3 25.1 while.37
  432.6 39.4 %while.38 = (s32[]{:T(128)}, f32[8,2,256,128]{3,2,1,0:T(8,128)}, s32[256]{0:T(256)S(1)}, s32[2]{0:T(128)S(1)}, s32[2048]{0:T(1024)S(1)}, /*index=5*/s32[2048]{0:...) while((s32[]{:T(128)}, f32[8,2,256,128]{3,2,1,0:T(8,128)}, ...), condition=%wide.region_16.17_spmd, body=%wide.region_12.16_spmd.sunk | while | flops 2170028032 | bytes 18393368 | solution.py:116
  474.6 75.6 %all-gather.26.cloned.1.call-done = bf16[2048,2048]{1,0:T(8,128)(2,1)} async-done(((bf16[2048,512]{1,0:T(8,128)(2,1)}), bf16[2048,2048]{1,0:T(8,128)(2,1)}) %all-gather.26.cloned.1.call-update) | async-done | bytes 8388624 | tf_op jit(solution)/shard_map/all_gather | solution.py:138
  556.6 554.7 %all-gather.28.cloned.1.call-done = bf16[2048,8192]{1,0:T(8,128)(2,1)} async-done(((bf16[2048,2048]{1,0:T(8,128)(2,1)}), bf16[2048,8192]{1,0:T(8,128)(2,1)}) %all-gather.28.cloned.1.call-update) | async-done | bytes 33554448 | tf_op jit(solution)/shard_map/all_gather | solution.py:140
  1111.4 22.9 fusion.69
  1134.2 538.3 %all-gather.30.cloned.1.call-done = bf16[2048,8192]{1,0:T(8,128)(2,1)} async-done(((bf16[2048,2048]{1,0:T(8,128)(2,1)}), bf16[2048,8192]{1,0:T(8,128)(2,1)}) %all-gather.30.cloned.1.call-update) | async-done | bytes 33554448 | tf_op jit(solution)/shard_map/all_gather | solution.py:141
  1672.6 22.7 fusion.70
  1695.3 538.5 %all-gather.32.cloned.1.call-done = bf16[8192,2048]{1,0:T(8,128)(2,1)} async-done(((bf16[8192,512]{1,0:T(8,128)(2,1)}), bf16[8192,2048]{1,0:T(8,128)(2,1)}) %all-gather.32.cloned.1.call-update) | async-done | bytes 33554448 | tf_op jit(solution)/shard_map/all_gather | solution.py:142
  2233.8 23.1 multiply_convert_fusion
  2320.8 197.0 %while.39 = (s32[]{:T(128)}, f32[8,2,256,128]{3,2,1,0:T(8,128)}, f32[2048,2,1024]{0,2,1:T(8,128)}, s32[256]{0:T(256)S(1)}, s32[2]{0:T(128)S(1)}, /*index=5*/s32[...) while((s32[]{:T(128)}, f32[8,2,256,128]{3,2,1,0:T(8,128)}, ...), condition=%wide.region_23.24_spmd, body=%wide.region_19.23_spmd.sunk | while | flops 5426380800 | bytes 187509216 | solution.py:116
  2324.5 95.9 %conditional.8 = ((f32[8,2,256,128]{3,2,1,0:T(8,128)}, f32[2048,2,1024]{0,2,1:T(8,128)})) conditional(s32[]{:T(128)} %convert_element_type.345, (f32[8,2,256,128]{3,2,1,0:T(8,128)}, f32[2048,2,1024]{0,2,1:T(8,128)}) %tuple.130, (pred[256,1024]{0,1:T(8,128)(4,1)S(1)}, bf16[2,1024,1024]{1,2,0:T(8,128)(2,1)}, s32[]{:T(128)}, ...), branch_computations={%region_21.21_spmd, %region_22.22_spmd} | conditional | flops 5425332224 | bytes 187220096 | solution.py:434
  2372.6 39.8 %dynamic_update_slice.4 = f32[2048,2,1024]{0,2,1:T(8,128)} dynamic-update-slice(f32[2048,2,1024]{0,2,1:T(8,128)} %get-tuple-element.356, f32[1024,2,1024]{0,2,1:T(8,128)} %maximum_add_fusion, s32[]{:T(128)S(6)} %select_n.86, s32[]{:T(128)} %constant.165.clone, s32[]{:T(128)} %constant.165.clone) | dynamic-update-slice | bytes 16777220 | tf_op jit(solution)/shard_map/while/body/eval_jaxpr/cond/branch_1_fun/dynamic_update_slice | solution.py:431
  2423.6 94.1 %conditional.8 = ((f32[8,2,256,128]{3,2,1,0:T(8,128)}, f32[2048,2,1024]{0,2,1:T(8,128)})) conditional(s32[]{:T(128)} %convert_element_type.345, (f32[8,2,256,128]{3,2,1,0:T(8,128)}, f32[2048,2,1024]{0,2,1:T(8,128)}) %tuple.130, (pred[256,1024]{0,1:T(8,128)(4,1)S(1)}, bf16[2,1024,1024]{1,2,0:T(8,128)(2,1)}, s32[]{:T(128)}, ...), branch_computations={%region_21.21_spmd, %region_22.22_spmd} | conditional | flops 5425332224 | bytes 187220096 | solution.py:434
  2471.1 38.6 %dynamic_update_slice.4 = f32[2048,2,1024]{0,2,1:T(8,128)} dynamic-update-slice(f32[2048,2,1024]{0,2,1:T(8,128)} %get-tuple-element.356, f32[1024,2,1024]{0,2,1:T(8,128)} %maximum_add_fusion, s32[]{:T(128)S(6)} %select_n.86, s32[]{:T(128)} %constant.165.clone, s32[]{:T(128)} %constant.165.clone) | dynamic-update-slice | bytes 16777220 | tf_op jit(solution)/shard_map/while/body/eval_jaxpr/cond/branch_1_fun/dynamic_update_slice | solution.py:431
  2538.4 22.2 all-to-all-done.3
  2564.1 32.5 reduce-scatter.9.cloned.1.call-done
  2603.6 84.9 %all-gather.36.cloned.1.call-done = bf16[1024,2048]{0,1:T(8,128)(2,1)} async-done(((bf16[256,2048]{0,1:T(8,128)(2,1)}), bf16[1024,2048]{0,1:T(8,128)(2,1)}) %all-gather.36.cloned.1.call-update) | async-done | bytes 4194320 | tf_op jit(solution)/shard_map/all_gather | solution.py:335
  2704.2 23.2 all-to-all-done.2
  2732.3 118.1 %all-gather.34.cloned.1.call-done = bf16[1024,2048]{1,0:T(8,128)(2,1)} async-done(((bf16[256,2048]{1,0:T(8,128)(2,1)}), bf16[1024,2048]{1,0:T(8,128)(2,1)}) %all-gather.34.cloned.1.call-update) | async-done | bytes 4194320 | tf_op jit(solution)/shard_map/all_gather | solution.py:334
  2866.1 72.5 %all-gather.38.cloned.1.call-done = bf16[1024,2048]{1,0:T(8,128)(2,1)} async-done(((bf16[256,2048]{1,0:T(8,128)(2,1)}), bf16[1024,2048]{1,0:T(8,128)(2,1)}) %all-gather.38.cloned.1.call-update) | async-done | bytes 4194320 | tf_op jit(solution)/shard_map/all_gather | solution.py:336
  2955.8 201.4 %all_to_all.124 = bf16[256,4,2048]{2,0,1:T(8,128)(2,1)S(1)} all-to-all(bf16[256,4,2048]{2,0,1:T(8,128)(2,1)S(1)} %bitcast.277), channel_id=1, replica_groups=mesh['ctx'=8,'fsdp'=4] {'fsdp'}, dimensions={1} | all-to-all | bytes 8388608 | tf_op jit(solution)/shard_map/all_to_all | solution.py:348
  3170.4 65.2 %all_to_all.125 = bf16[256,4,512]{0,2,1:T(8,128)(2,1)S(1)} all-to-all(bf16[256,4,512]{0,2,1:T(8,128)(2,1)S(1)} %bitcast.295), channel_id=1, replica_groups=mesh['ctx'=8,'fsdp'=4] {'fsdp'}, dimensions={1} | all-to-all | bytes 2097152 | tf_op jit(solution)/shard_map/all_to_all | solution.py:349
  3236.1 101.0 %all-gather.40.cloned.1.call-done = bf16[1024,8192]{1,0:T(8,128)(2,1)} async-done(((bf16[256,8192]{1,0:T(8,128)(2,1)}), bf16[1024,8192]{1,0:T(8,128)(2,1)}) %all-gather.40.cloned.1.call-update) | async-done | bytes 16777232 | tf_op jit(solution)/shard_map/all_gather | solution.py:337
  3355.4 38.2 %pmax.7 = f32[16]{0:T(128)S(1)} all-reduce(f32[16]{0:T(128)S(1)} %reshape.358), channel_id=1, replica_groups=mesh['ctx'=8,'fsdp'=4] {'ctx','fsdp'}, use_global_device_ids=true, to_apply=%region_38.39 | all-reduce | flops 16 | bytes 128 | tf_op jit(solution)/shard_map/pmax | solution.py:269
  3434.5 40.8 %all-reduce.2 = (f32[2048]{0:T(1024)S(1)}, f32[2048]{0:T(1024)S(1)}) all-reduce(f32[2048]{0:T(1024)S(1)} %get-tuple-element.611, f32[2048]{0:T(1024)S(1)} %copy-done.41), channel_id=3, replica_groups=mesh['ctx'=8,'fsdp'=4] {'ctx','fsdp'}, use_global_device_ids=true, to_apply=%region_27.28.clone | all-reduce | flops 4096 | bytes 32768
  3505.2 73.6 %reduce-scatter.19.cloned.1.call-done = bf16[256,2048]{1,0:T(8,128)(2,1)} async-done(((bf16[2048,2048]{1,0:T(8,128)(2,1)}), bf16[256,2048]{1,0:T(8,128)(2,1)}) %reduce-scatter.19.cloned.1.call-update) | async-done | bytes 1048592 | tf_op jit(solution)/shard_map/reduce_scatter | solution.py:352
  3581.6 71.8 %reduce-scatter.21.cloned.1.call-done = bf16[256,2048]{1,0:T(8,128)(2,1)} async-done(((bf16[2048,2048]{1,0:T(8,128)(2,1)}), bf16[256,2048]{1,0:T(8,128)(2,1)}) %reduce-scatter.21.cloned.1.call-update) | async-done | bytes 1048592 | tf_op jit(solution)/shard_map/reduce_scatter | solution.py:358
  3656.2 72.4 %reduce-scatter.23.cloned.1.call-done = bf16[1024,512]{1,0:T(8,128)(2,1)} async-done(((bf16[8192,512]{1,0:T(8,128)(2,1)}), bf16[1024,512]{1,0:T(8,128)(2,1)}) %reduce-scatter.23.cloned.1.call-update) | async-done | bytes 1048592 | tf_op jit(solution)/shard_map/reduce_scatter | solution.py:364
  (322 shorter events, 595.0 us)
Async XLA Ops:
  7.2 85.7 %all-gather.16.cloned.1.call-start = ((), (), s32[]{:S(2)}) async-start(), calls=%async_computation.15 | async-start | bytes 5242880 | tf_op jit(solution)/shard_map/all_gather | solution.py:136
  8.0 165.3 %all-gather.22.cloned.1.call-start = ((), (), s32[]{:S(2)}) async-start(), calls=%async_computation.18 | async-start | bytes 5242880 | tf_op jit(solution)/shard_map/all_gather | solution.py:137
  8.7 314.0 %all-gather.20.cloned.1.call-start = ((), (), s32[]{:S(2)}) async-start(), calls=%async_computation.17 | async-start | bytes 10485760 | tf_op jit(solution)/shard_map/all_gather | solution.py:135
  9.4 350.6 %all-gather.18.cloned.1.call-start = ((), (), s32[]{:S(2)}) async-start(), calls=%async_computation.16 | async-start | bytes 4718592 | tf_op jit(solution)/shard_map/all_gather | solution.py:294
  24.9 316.0 %copy-start.22 = (f32[256,64]{0,1:T(8,128)}, f32[256,64]{0,1:T(8,128)S(1)}, u32[]{:S(2)}) copy-start(f32[256,64]{0,1:T(8,128)S(1)} %get-tuple-element.712) | copy-start | bytes 196612
  24.9 316.0 %copy-start.24 = (f32[256,64]{0,1:T(8,128)}, f32[256,64]{0,1:T(8,128)S(1)}, u32[]{:S(2)}) copy-start(f32[256,64]{0,1:T(8,128)S(1)} %get-tuple-element.713) | copy-start | bytes 196612
  104.6 294.5 %all-gather.24.cloned.1.call-start = ((), (), s32[]{:S(2)}) async-start(), calls=%async_computation.19 | async-start | bytes 4718592 | tf_op jit(solution)/shard_map/all_gather | solution.py:295
  177.5 372.6 %all-gather.26.cloned.1.call-start = ((), (), s32[]{:S(2)}) async-start(), calls=%async_computation.20 | async-start | bytes 10485760 | tf_op jit(solution)/shard_map/all_gather | solution.py:138
  178.1 933.3 %all-gather.28.cloned.1.call-start = ((), (), s32[]{:S(2)}) async-start(), calls=%async_computation.21 | async-start | bytes 41943040 | tf_op jit(solution)/shard_map/all_gather | solution.py:140
  178.9 1493.7 %all-gather.30.cloned.1.call-start = ((), (), s32[]{:S(2)}) async-start(), calls=%async_computation.22 | async-start | bytes 41943040 | tf_op jit(solution)/shard_map/all_gather | solution.py:141
  179.6 2054.2 %all-gather.32.cloned.1.call-start = ((), (), s32[]{:S(2)}) async-start(), calls=%async_computation.23 | async-start | bytes 41943040 | tf_op jit(solution)/shard_map/all_gather | solution.py:142
  180.3 2416.3 %reduce-scatter.9.cloned.1.call-start = ((), (), s32[]{:S(2)}) async-start(), calls=%async_computation.24 | async-start | bytes 9437184 | tf_op jit(solution)/shard_map/reduce_scatter | solution.py:448
  556.3 1736.2 %copy-start.3 = (f32[256,2048]{1,0:T(8,128)}, f32[256,2048]{1,0:T(8,128)S(1)}, u32[]{:S(2)}) copy-start(f32[256,2048]{1,0:T(8,128)S(1)} %get-tuple-element.715) | copy-start | bytes 6291460
  556.4 1736.2 %copy-start.32 = (f32[256]{0:T(256)}, f32[256]{0:T(256)S(1)}, u32[]{:S(2)}) copy-start(f32[256]{0:T(256)S(1)} %add_rsqrt_fusion) | copy-start | bytes 3076
  556.6 554.7 %copy-start.14 = (bf16[256,2048]{1,0:T(8,128)(2,1)}, bf16[256,2048]{1,0:T(8,128)(2,1)S(1)}, u32[]{:S(2)}) copy-start(bf16[256,2048]{1,0:T(8,128)(2,1)S(1)} %multiply_convert_fusion.5) | copy-start | bytes 3145732
  1134.2 1099.5 %copy-start.9 = (bf16[1,256,2048]{2,1,0:T(8,128)(2,1)S(1)}, bf16[1,256,2048]{2,1,0:T(8,128)(2,1)}, u32[]{:S(2)}) copy-start(bf16[1,256,2048]{2,1,0:T(8,128)(2,1)} %param.27) | copy-start | bytes 3145732
  2527.0 161.5 %all-gather.36.cloned.1.call-start = ((), (), s32[]{:S(2)}) async-start(), calls=%async_computation.29 | async-start | bytes 5242880 | tf_op jit(solution)/shard_map/all_gather | solution.py:335
  2527.8 322.6 %all-gather.34.cloned.1.call-start = ((), (), s32[]{:S(2)}) async-start(), calls=%async_computation.25 | async-start | bytes 5242880 | tf_op jit(solution)/shard_map/all_gather | solution.py:334
  2528.3 410.3 %all-gather.38.cloned.1.call-start = ((), (), s32[]{:S(2)}) async-start(), calls=%async_computation.31 | async-start | bytes 5242880 | tf_op jit(solution)/shard_map/all_gather | solution.py:336
  2529.1 808.1 %all-gather.40.cloned.1.call-start = ((), (), s32[]{:S(2)}) async-start(), calls=%async_computation.34 | async-start | bytes 20971520 | tf_op jit(solution)/shard_map/all_gather | solution.py:337
  2530.8 29.8 all-to-all-start.3
  2560.6 38.4 %all-to-all-start = ((bf16[256,4,512]{2,0,1:T(8,128)(2,1)}), bf16[256,4,512]{2,0,1:T(8,128)(2,1)S(1)}, u32[]{:S(2)}, u32[]{:S(2)}) async-start(bf16[256,4,512]{2,0,1:T(8,128)(2,1)} %copy.187), calls=%async_computation.1 | async-start | bytes 2097152 | tf_op jit(solution)/shard_map/all_to_all | solution.py:471
  2599.0 96.7 %all-to-all-start.1 = ((bf16[256,4,256]{2,0,1:T(8,128)(2,1)}), bf16[256,4,256]{2,0,1:T(8,128)(2,1)S(1)}, u32[]{:S(2)}, u32[]{:S(2)}) async-start(bf16[256,4,256]{2,0,1:T(8,128)(2,1)} %copy.188), calls=%async_computation.3 | async-start | bytes 1048576 | tf_op jit(solution)/shard_map/all_to_all | solution.py:472
  2603.6 818.4 %reduce-scatter.17.cloned.1.call-start = ((), (), s32[]{:S(2)}) async-start(), calls=%async_computation.30 | async-start | bytes 2359296 | tf_op jit(solution)/shard_map/reduce_scatter | solution.py:504
  2695.6 31.7 all-to-all-start.2
  2727.3 211.3 %all-to-all-start.4 = ((bf16[256,4,2048]{2,0,1:T(8,128)(2,1)}), bf16[256,4,2048]{2,0,1:T(8,128)(2,1)}, u32[]{:S(2)}, u32[]{:S(2)}) async-start(bf16[256,4,2048]{2,0,1:T(8,128)(2,1)} %bitcast.276), calls=%async_computation.9 | async-start | bytes 8388608 | tf_op jit(solution)/shard_map/all_to_all | solution.py:347
  2732.2 692.5 %reduce-scatter.11.cloned.1.call-start = ((), (), s32[]{:S(2)}) async-start(), calls=%async_computation.26 | async-start | bytes 2359296 | tf_op jit(solution)/shard_map/reduce_scatter | solution.py:486
  2856.2 625.0 %reduce-scatter.13.cloned.1.call-start = ((), (), s32[]{:S(2)}) async-start(), calls=%async_computation.27 | async-start | bytes 1179648 | tf_op jit(solution)/shard_map/reduce_scatter | solution.py:492
  2861.3 642.3 %reduce-scatter.15.cloned.1.call-start = ((), (), s32[]{:S(2)}) async-start(), calls=%async_computation.28 | async-start | bytes 1179648 | tf_op jit(solution)/shard_map/reduce_scatter | solution.py:498
  2866.0 712.7 %reduce-scatter.19.cloned.1.call-start = ((), (), s32[]{:S(2)}) async-start(), calls=%async_computation.32 | async-start | bytes 9437184 | tf_op jit(solution)/shard_map/reduce_scatter | solution.py:352
  2952.9 700.5 %reduce-scatter.21.cloned.1.call-start = ((), (), s32[]{:S(2)}) async-start(), calls=%async_computation.33 | async-start | bytes 9437184 | tf_op jit(solution)/shard_map/reduce_scatter | solution.py:358
  3168.7 559.8 %reduce-scatter.23.cloned.1.call-start = ((), (), s32[]{:S(2)}) async-start(), calls=%async_computation.35 | async-start | bytes 9437184 | tf_op jit(solution)/shard_map/reduce_scatter | solution.py:364
  (46 other events, 1756.0 us)
Sparse Core Ops, SparseCore 0:
  9.6 83.2 all-gather.15
  94.5 78.7 all-gather.21
  174.8 147.8 all-gather.19
  325.1 34.8 all-gather.17
  362.3 36.7 all-gather.23
  400.5 149.6 all-gather.25
  551.7 559.5 all-gather.27
  1112.9 559.5 all-gather.29
  1674.2 559.5 all-gather.31
  2527.1 69.4 reduce-scatter.8
  2598.8 89.6 all-gather.35
  2690.0 160.2 all-gather.33
  2852.5 86.0 all-gather.37
  2940.1 397.0 all-gather.39
  3340.7 39.6 reduce-scatter.16
  3383.5 41.1 reduce-scatter.10
  3428.1 36.1 reduce-scatter.12
  3467.6 35.9 reduce-scatter.14
  3507.5 71.2 reduce-scatter.18
  3582.1 71.2 reduce-scatter.20
  3657.2 71.2 reduce-scatter.22
where the time goes:
time: 3750 us; the launch traced here: 3740 us
  waiting for transfers between devices  2720 us (73%)
  blocking collectives  371 us (10%)
  matrix products  344 us (9%)
  local copies, waits for them, and re-layouts  173 us (5%)
  other arithmetic  80.1 us (2%)
    all_gather x1, waiting for transfers between devices, gather_weights(): lax.all_gather(gate_weight, 'fsdp', axis=1, tiled=True)  555 us
    all_gather x1, waiting for transfers between devices, gather_weights(): lax.all_gather(down_weight, 'fsdp', axis=1, tiled=True)  539 us
    all_gather x1, waiting for transfers between devices, gather_weights(): lax.all_gather(up_weight, 'fsdp', axis=1, tiled=True)  538 us
    all_to_all x1, blocking collectives, on_device(): lax.all_to_all(grad_up, 'fsdp', split_axis=1, concat_axis=0, tiled=True)  201 us
    all_gather x1, waiting for transfers between devices, gather_weights(): lax.all_gather(query_weight, 'fsdp', axis=1, tiled=True)  130 us
    all_gather x1, waiting for transfers between devices, on_device(): lax.all_gather(normalized, 'fsdp', axis=0, tiled=True)  118 us
    all_gather x1, waiting for transfers between devices, on_device(): lax.all_gather(hidden, 'fsdp', axis=0, tiled=True)  101 us
    all_gather x1, waiting for transfers between devices, on_device(): lax.all_gather(attended, 'fsdp', axis=0, tiled=True)  84.9 us
  transfers between devices with their start and end apart: 26, of which 21 were waited for; matrix products, arithmetic and copies ran while one was open for 8% of the time, Pallas kernels for 0%

commit v1 on v0

v1 whole, which is shorter than its diff:
```python
import functools
import math

import jax
import jax.numpy as jnp
from jax import lax
from jax.experimental import pallas as pl
from jax.experimental.pallas import tpu as pltpu
from jax.sharding import PartitionSpec as P

QUERY_HEADS = 16
KEY_VALUE_HEADS = 8
HEAD_SIZE = 128
REPEAT = QUERY_HEADS // KEY_VALUE_HEADS
UNIT = (REPEAT + 2) * HEAD_SIZE

epsilon = 1e-06
rope_base = 1000000.0
hidden_fill_value = -1e30
bf16 = jnp.bfloat16
f32 = jnp.float32
SCALE = 1.0 / math.sqrt(HEAD_SIZE)


def swap(value, axis, mask):
    size = lax.axis_size(axis)
    return lax.ppermute(value, axis, [(i, i ^ mask) for i in range(size)])


def bits_down(size):
    mask = size // 2
    while mask:
        yield mask
        mask //= 2


def by_place(items, me):
    mask = 1
    while mask < len(items):
        odd = (me & mask) != 0
        items = [jnp.where(odd, items[j ^ mask], items[j]) for j in range(len(items))]
        mask *= 2
    return items


def add_rounded(left, right):
    return (left.astype(f32) + right.astype(f32)).astype(bf16)


def gather_ctx(block):
    size = lax.axis_size("ctx")
    if size != 8:
        whole = block[None]
        mask = 1
        while mask < size:
            whole = jnp.concatenate([whole, swap(whole, "ctx", mask)], 0)
            mask *= 2
        return [whole]
    half = block.shape[0] // 2
    over_x = swap(block, "ctx", 2)
    over_y = swap(block, "ctx", 4)
    other = swap(block, "ctx", 1)
    low = swap(over_x[:half], "ctx", 4)
    high = swap(over_y[half:], "ctx", 2)
    far = jnp.concatenate([low, high], 0)
    slots = [
        block,
        other,
        over_x,
        swap(over_x, "ctx", 1),
        over_y,
        swap(over_y, "ctx", 1),
        far,
        swap(far, "ctx", 1),
    ]
    return [slot[None] for slot in slots]


def sum_planes(even):
    s0, s2, s4, s6 = even
    half = s0.shape[0] // 2
    from_x = swap(s6[:half], "ctx", 2)
    from_y = swap(s6[half:], "ctx", 4)
    low2 = swap(s2[:half], "ctx", 2)
    high4 = swap(s4[half:], "ctx", 4)
    low4 = swap(add_rounded(s4[:half], from_x), "ctx", 4)
    high2 = swap(add_rounded(s2[half:], from_y), "ctx", 2)
    low = s0[:half].astype(f32) + low2.astype(f32) + low4.astype(f32)
    high = s0[half:].astype(f32) + high2.astype(f32) + high4.astype(f32)
    return jnp.concatenate([low, high], 0)


def sum_halving(slots, axis):
    for mask in bits_down(slots.shape[0]):
        keep = slots[:mask].astype(f32)
        slots = (keep + swap(slots[mask:], axis, mask).astype(f32)).astype(slots.dtype)
    return slots[0].astype(f32)


def sum_fsdp(pieces):
    total = pieces[0].astype(f32)
    for d in range(1, len(pieces)):
        total = total + swap(pieces[d].astype(bf16), "fsdp", d).astype(f32)
    return total


def params(flops, bytes_accessed):
    return dict(
        compiler_params=pltpu.CompilerParams(vmem_limit_bytes=48 * 2**20),
        cost_estimate=pl.CostEstimate(
            flops=flops, bytes_accessed=bytes_accessed, transcendentals=0
        ),
    )


def rotate(value, cosine, sine):
    return value * cosine + pltpu.roll(value, HEAD_SIZE // 2, 1) * sine


def slot_matmul_body(n_slots, parts, depth, rope, me_ref, x_ref, *refs):
    slot_refs = refs[:n_slots]
    out_ref = refs[-1]
    total = None
    for j in range(n_slots):
        for q in range(parts):
            owner = me_ref[0] ^ (j * parts + q)
            cols = pl.ds(pl.multiple_of(owner * depth, depth), depth)
            term = jnp.dot(x_ref[:, cols], slot_refs[j][q], preferred_element_type=f32)
            total = term if total is None else total + term
    if rope:
        cosine, sine = refs[n_slots][...], refs[n_slots + 1][...]
        parts_out = [
            rotate(total[:, i * HEAD_SIZE : (i + 1) * HEAD_SIZE], cosine, sine)
            for i in range(REPEAT + 1)
        ]
        total = jnp.concatenate(parts_out + [total[:, (REPEAT + 1) * HEAD_SIZE :]], 1)
    out_ref[...] = total.astype(out_ref.dtype)


def in_order(slots, me):
    whole = jnp.concatenate(slots, 0)
    whole = whole[me ^ jnp.arange(whole.shape[0], dtype=jnp.int32)]
    return whole.reshape(-1, whole.shape[2])


def slot_matmul(x, slots, me, tile, out_dtype, tables=None):
    rows = x.shape[0]
    parts, depth, width = slots[0].shape
    if depth % 128:
        total = product(x, in_order(slots, me))
        if tables is None:
            return total.astype(out_dtype)
        total = total.reshape(rows, width // UNIT, REPEAT + 2, HEAD_SIZE)
        cosine, sine = (t[:, None, None] for t in tables)
        turned = total[:, :, : REPEAT + 1]
        turned = turned * cosine + jnp.roll(turned, HEAD_SIZE // 2, -1) * sine
        total = jnp.concatenate([turned, total[:, :, REPEAT + 1 :]], 2)
        return total.reshape(rows, width).astype(out_dtype)
    extra = [] if tables is None else list(tables)
    body = functools.partial(
        slot_matmul_body, len(slots), parts, depth, tables is not None
    )
    return pl.pallas_call(
        body,
        out_shape=jax.ShapeDtypeStruct((rows, width), out_dtype),
        grid_spec=pltpu.PrefetchScalarGridSpec(
            num_scalar_prefetch=1,
            grid=(width // tile,),
            in_specs=[pl.BlockSpec(x.shape, lambda i, me: (0, 0))]
            + [pl.BlockSpec((parts, depth, tile), lambda i, me: (0, 0, i))] * len(slots)
            + [pl.BlockSpec(e.shape, lambda i, me: (0, 0)) for e in extra],
            out_specs=pl.BlockSpec((rows, tile), lambda i, me: (0, i)),
        ),
        **params(2 * rows * x.shape[1] * width, 2 * x.shape[1] * width),
    )(me, x, *slots, *extra)


def slot_matmul_t_body(n_slots, parts, depth, me_ref, x_ref, *refs):
    slot_refs = refs[:n_slots]
    out_ref, total_ref = refs[n_slots], refs[n_slots + 1]
    step = pl.program_id(0)

    @pl.when(step == 0)
    def _():
        total_ref[...] = jnp.zeros_like(total_ref)

    x = x_ref[...]
    for j in range(n_slots):
        for q in range(parts):
            owner = me_ref[0] ^ (j * parts + q)
            cols = pl.ds(pl.multiple_of(owner * depth, depth), depth)
            total_ref[:, cols] += lax.dot_general(
                x, slot_refs[j][q], (((1,), (1,)), ((), ())), preferred_element_type=f32
            )

    @pl.when(step == pl.num_programs(0) - 1)
    def _():
        out_ref[...] = total_ref[...].astype(out_ref.dtype)


def slot_matmul_t(x, slots, me, tile, out_dtype):
    rows, width = x.shape
    parts, depth, _ = slots[0].shape
    height = parts * depth * len(slots)
    if depth % 128:
        return product_t(x, in_order(slots, me)).astype(out_dtype)
    return pl.pallas_call(
        functools.partial(slot_matmul_t_body, len(slots), parts, depth),
        out_shape=jax.ShapeDtypeStruct((rows, height), out_dtype),
        grid_spec=pltpu.PrefetchScalarGridSpec(
            num_scalar_prefetch=1,
            grid=(width // tile,),
            in_specs=[pl.BlockSpec((rows, tile), lambda i, me: (0, i))]
            + [pl.BlockSpec((parts, depth, tile), lambda i, me: (0, 0, i))]
            * len(slots),
            out_specs=pl.BlockSpec((rows, height), lambda i, me: (0, 0)),
            scratch_shapes=[pltpu.VMEM((rows, height), f32)],
        ),
        **params(2 * rows * height * width, 2 * height * width),
    )(me, x, *slots)


def keys_of(slot_refs):
    def column(i):
        parts = [
            r[:, :, i * HEAD_SIZE : (i + 1) * HEAD_SIZE].reshape(-1, HEAD_SIZE)
            for r in slot_refs
        ]
        return parts[0] if len(parts) == 1 else jnp.concatenate(parts, 0)

    return column(0), column(1)


def scores_of(qkv_ref, keys, natural_ref, start_ref, key_natural_ref):
    blk = qkv_ref.shape[0]
    query = jnp.concatenate(
        [qkv_ref[:, i * HEAD_SIZE : (i + 1) * HEAD_SIZE] for i in range(REPEAT)], 0
    )
    scores = (
        lax.dot_general(
            query, keys, (((1,), (1,)), ((), ())), preferred_element_type=f32
        )
        * SCALE
    )
    key_natural = key_natural_ref[0]
    allowed = (key_natural >= start_ref[...]) & (key_natural <= natural_ref[...])
    allowed = jnp.concatenate([allowed] * REPEAT, 0)
    scores = jnp.where(allowed, scores, hidden_fill_value)
    best = jnp.max(scores, 1, keepdims=True)
    exps = jnp.exp(scores - best)
    return query, exps / jnp.sum(exps, 1, keepdims=True), best, blk


def attend_body(n_slots, natural_ref, start_ref, key_natural_ref, qkv_ref, *refs):
    slot_refs, (out_ref, best_ref) = refs[:n_slots], refs[n_slots:]
    keys, values = keys_of(slot_refs)
    _, probs, best, blk = scores_of(qkv_ref, keys, natural_ref, start_ref, key_natural_ref)
    heads = jnp.dot(probs.astype(bf16), values, preferred_element_type=f32)
    out_ref[...] = jnp.concatenate(
        [heads[i * blk : (i + 1) * blk] for i in range(REPEAT)], 1
    ).astype(bf16)
    tops = [
        jnp.broadcast_to(jnp.max(best[i * blk : (i + 1) * blk], 0, keepdims=True), (1, 128))
        for i in range(REPEAT)
    ]
    best_ref[0, 0] = jnp.concatenate(tops + [jnp.zeros((8 - REPEAT, 128), f32)], 0)


def attend_back_body(
    n_slots, natural_ref, start_ref, key_natural_ref, cosine_ref, sine_ref, qkv_ref, grad_ref, *refs
):
    slot_refs, (dq_ref, *dkv_refs) = refs[:n_slots], refs[n_slots:]
    keys, values = keys_of(slot_refs)
    query, probs, _, blk = scores_of(qkv_ref, keys, natural_ref, start_ref, key_natural_ref)
    grad = jnp.concatenate(
        [grad_ref[:, i * HEAD_SIZE : (i + 1) * HEAD_SIZE] for i in range(REPEAT)], 0
    )
    low = probs.astype(bf16)
    grad_probs = lax.dot_general(
        grad, values, (((1,), (1,)), ((), ())), preferred_element_type=f32
    )
    delta = jnp.sum(low.astype(f32) * grad_probs, 1, keepdims=True)
    score_grad = (probs * (grad_probs - delta)).astype(bf16)
    query_grad = jnp.dot(score_grad, keys, preferred_element_type=f32) * SCALE
    cosine, sine = cosine_ref[...], sine_ref[...]
    dq_ref[...] = jnp.concatenate(
        [
            rotate(query_grad[i * blk : (i + 1) * blk], cosine, -sine)
            for i in range(REPEAT)
        ],
        1,
    ).astype(bf16)
    over_rows = (((0,), (0,)), ((), ()))
    key_grad = (
        lax.dot_general(score_grad, query, over_rows, preferred_element_type=f32) * SCALE
    ).astype(bf16)
    value_grad = lax.dot_general(low, grad, over_rows, preferred_element_type=f32).astype(
        bf16
    )
    both = jnp.concatenate([key_grad, value_grad], 1)
    rows = both.shape[0] // n_slots
    for j, ref in enumerate(dkv_refs):
        ref[...] = both[j * rows : (j + 1) * rows].reshape(ref.shape)


def attention_specs(slots, blk, keys):
    parts = slots[0].shape[0]
    column = pl.BlockSpec((blk, 1), lambda r, h: (r, 0))
    slot = pl.BlockSpec((parts, blk, 2 * HEAD_SIZE), lambda r, h: (0, r, h))
    return (
        [column, column, pl.BlockSpec((1, 1, keys), lambda r, h: (r, 0, 0))],
        pl.BlockSpec((blk, UNIT), lambda r, h: (r, h)),
        pl.BlockSpec((blk, REPEAT * HEAD_SIZE), lambda r, h: (r, h)),
        slot,
    )


def attend(natural, start, key_natural, qkv, slots):
    rows = qkv.shape[0]
    rounds, _, keys = key_natural.shape
    blk = rows // rounds
    meta, unit, pair, slot = attention_specs(slots, blk, keys)
    return pl.pallas_call(
        functools.partial(attend_body, len(slots)),
        grid=(rounds, KEY_VALUE_HEADS),
        in_specs=meta + [unit] + [slot] * len(slots),
        out_specs=[pair, pl.BlockSpec((1, 1, 8, 128), lambda r, h: (r, h, 0, 0))],
        out_shape=[
            jax.ShapeDtypeStruct((rows, QUERY_HEADS * HEAD_SIZE), bf16),
            jax.ShapeDtypeStruct((rounds, KEY_VALUE_HEADS, 8, 128), f32),
        ],
        **params(4 * rows * keys * QUERY_HEADS * HEAD_SIZE, 12 * 2**20),
    )(natural, start, key_natural, qkv, *slots)


def attend_back(natural, start, key_natural, cosine, sine, qkv, grad, slots):
    rows = qkv.shape[0]
    rounds, _, keys = key_natural.shape
    blk = rows // rounds
    meta, unit, pair, slot = attention_specs(slots, blk, keys)
    table = pl.BlockSpec((blk, HEAD_SIZE), lambda r, h: (r, 0))
    return pl.pallas_call(
        functools.partial(attend_back_body, len(slots)),
        grid=(rounds, KEY_VALUE_HEADS),
        in_specs=meta + [table, table, unit, pair] + [slot] * len(slots),
        out_specs=[pair] + [slot] * len(slots),
        out_shape=[jax.ShapeDtypeStruct((rows, QUERY_HEADS * HEAD_SIZE), bf16)]
        + [jax.ShapeDtypeStruct(s.shape, bf16) for s in slots],
        **params(10 * rows * keys * QUERY_HEADS * HEAD_SIZE, 20 * 2**20),
    )(natural, start, key_natural, cosine, sine, qkv, grad, *slots)


def token_layout(length_row, block_slots, block_size):
    count_blocks = block_slots.shape[0]
    owner_block = jnp.argmax(
        block_slots[None, :] == jnp.arange(count_blocks, dtype=jnp.int32)[:, None], 1
    ).astype(jnp.int32)
    row_index = jnp.arange(count_blocks * block_size, dtype=jnp.int32)
    plain_order = jnp.repeat(owner_block, block_size) * block_size + row_index % block_size
    seq_ends = jnp.cumsum(length_row)
    seq_starts = seq_ends - length_row
    document_list = jnp.sum((plain_order[:, None] >= seq_ends[None, :]).astype(jnp.int32), 1)
    matches = document_list[:, None] == jnp.arange(length_row.shape[0], dtype=jnp.int32)[None, :]
    begins = jnp.sum(jnp.where(matches, seq_starts[None, :], 0), 1)
    return plain_order, begins


def rms_scale(value):
    return lax.rsqrt(jnp.mean(value * value, -1, keepdims=True) + epsilon)


def norm_back(grad_unit, unit_rows, scale_rows):
    return scale_rows * (grad_unit - unit_rows * jnp.mean(grad_unit * unit_rows, -1, keepdims=True))


def product(left, right):
    return jnp.dot(left, right, preferred_element_type=f32)


def product_t(left, right):
    return lax.dot_general(left, right, (((1,), (1,)), ((), ())), preferred_element_type=f32)


def over_rows(left, right):
    return lax.dot_general(left, right, (((0,), (0,)), ((), ())), preferred_element_type=f32)


def column_blocks(value, count, places):
    width = value.shape[1] // count
    return jnp.concatenate(
        [lax.dynamic_slice_in_dim(value, place * width, width, 1) for place in places], 1
    )


def gather_rows(piece, fsdp_place, ctx_count):
    count = lax.axis_size("fsdp")
    parts = [piece] + [swap(piece, "fsdp", d) for d in range(1, count)]
    return jnp.concatenate(by_place(parts, fsdp_place), 1)


def weight_grad_sum(left, right, me, count):
    depth = left.shape[1] // count
    if count == 8:
        sent = over_rows(column_blocks(left, 8, [me ^ j for j in (1, 3, 5, 7)]), right)
        kept = over_rows(column_blocks(left, 8, [me ^ j for j in (0, 2, 4, 6)]), right)
        both = add_rounded(kept.astype(bf16), swap(sent.astype(bf16), "ctx", 1))
        return sum_planes([both[i * depth : (i + 1) * depth] for i in range(4)])
    full = over_rows(column_blocks(left, count, [me ^ j for j in range(count)]), right)
    return sum_halving(full.astype(bf16).reshape(count, depth, right.shape[1]), "ctx")


def down_grad_sum(hidden, grad, me, count, fsdp_count):
    bands = count // fsdp_count
    band, column = me // fsdp_count, me % fsdp_count
    depth = hidden.shape[1] // bands
    width = grad.shape[1] // fsdp_count
    left = column_blocks(hidden, bands, [band ^ j for j in range(bands)])
    if count == 8:
        sent = over_rows(left, column_blocks(grad, 4, [column ^ 1, column ^ 3])).astype(bf16)
        kept = over_rows(left, column_blocks(grad, 4, [column, column ^ 2])).astype(bf16)
        both = add_rounded(kept, swap(sent, "ctx", 1))
        return sum_planes(
            [
                both[r * depth : (r + 1) * depth, s * width : (s + 1) * width]
                for r in range(2)
                for s in range(2)
            ]
        )
    right = column_blocks(grad, fsdp_count, [column ^ j for j in range(fsdp_count)])
    full = over_rows(left, right).astype(bf16).reshape(bands, depth, fsdp_count, width)
    return sum_halving(full.transpose(0, 2, 1, 3).reshape(count, depth, width), "ctx")


def clipped(weight, multiplier):
    columns = weight.shape[1]
    head_index = (
        lax.axis_index("fsdp") * columns + jnp.arange(columns, dtype=jnp.int32)
    ) // HEAD_SIZE
    matches = head_index[:, None] == jnp.arange(multiplier.shape[0], dtype=jnp.int32)[None, :]
    column_factor = jnp.sum(jnp.where(matches, multiplier[None, :], 0.0), 1)
    return (weight.astype(f32) * column_factor[None, :]).astype(bf16)


def gain_sum(term, me, place, count, fsdp_count):
    table = term.reshape(count, fsdp_count, -1)
    table = jnp.stack(by_place([table[i] for i in range(count)], me))
    mine = sum_halving(table, "ctx")
    mine = jnp.stack(by_place([mine[i] for i in range(fsdp_count)], place))
    return sum_halving(mine, "fsdp")


def on_device(
    hidden_in,
    out_grad,
    seq_lengths,
    block_perm,
    first_gain,
    query_weight,
    key_matrix,
    value_matrix,
    output_weight,
    second_gain,
    gate_weight,
    up_weight,
    down_weight,
    clip_limit,
):
    rows, model = hidden_in.shape[1], hidden_in.shape[2]
    count, fsdp_count = lax.axis_size("ctx"), lax.axis_size("fsdp")
    me, place = lax.axis_index("ctx"), lax.axis_index("fsdp")
    me_ref = me.astype(jnp.int32).reshape(1)
    depth = model // count
    blocks = block_perm.shape[0]
    rounds = blocks // count
    blk = rows // rounds
    shard_heads = KEY_VALUE_HEADS // fsdp_count

    def own_rows(weight):
        return lax.dynamic_slice_in_dim(weight, me * depth, depth, 0)

    unit_rows = jnp.concatenate(
        [
            own_rows(query_weight).reshape(depth, shard_heads, REPEAT, HEAD_SIZE),
            own_rows(key_matrix).reshape(depth, shard_heads, 1, HEAD_SIZE),
            own_rows(value_matrix).reshape(depth, shard_heads, 1, HEAD_SIZE),
        ],
        2,
    ).reshape(depth, shard_heads * UNIT)
    unit_rows = gather_rows(unit_rows, place, count)
    unit_slots = gather_ctx(unit_rows)
    gains = jnp.stack([first_gain, second_gain])
    gains = jnp.concatenate(
        by_place([gains] + [swap(gains, "fsdp", d) for d in range(1, fsdp_count)], place), 1
    ).astype(f32)
    first_full, second_full = gains[0], gains[1]
    output_rows = gather_rows(own_rows(output_weight), place, count)
    output_slots = gather_ctx(output_rows)

    hidden_width = gate_weight.shape[1]
    down_depth = hidden_width // count

    def down_piece(d):
        first = (place ^ d) * hidden_width + me * down_depth
        return lax.dynamic_slice_in_dim(down_weight, first, down_depth, 0)

    down_rows = [down_piece(0)] + [
        swap(down_piece(d), "fsdp", d) for d in range(1, fsdp_count)
    ]
    down_slots = gather_ctx(jnp.concatenate(by_place(down_rows, place), 1))

    plain_order, begins = token_layout(seq_lengths[0], block_perm, blk)
    first_row = me * rows
    natural = lax.dynamic_slice_in_dim(plain_order, first_row, rows)
    begin = lax.dynamic_slice_in_dim(begins, first_row, rows)
    half_dim = HEAD_SIZE // 2
    exponent = jnp.arange(half_dim, dtype=f32) * (2.0 / HEAD_SIZE)
    inverse = rope_base ** (-exponent)
    angles = (natural - begin).astype(f32)[:, None] * inverse[None, :]
    cosine = jnp.concatenate([jnp.cos(angles)] * 2, 1)
    sine = jnp.concatenate([-jnp.sin(angles), jnp.sin(angles)], 1)
    slot_order = plain_order.reshape(count, rounds, blk)
    slot_order = jnp.stack(by_place([slot_order[i] for i in range(count)], me), 1)
    key_natural = slot_order.reshape(rounds, 1, count * blk)
    natural_column, begin_column = natural[:, None], begin[:, None]

    tokens = hidden_in.reshape(rows, model).astype(f32)
    scale_one = rms_scale(tokens)
    unit_one = tokens * scale_one
    normalized = (unit_one * first_full).astype(bf16)
    qkv = slot_matmul(normalized, unit_slots, me_ref, UNIT, bf16, (cosine, sine))
    kv_local = qkv.reshape(rows, KEY_VALUE_HEADS, UNIT)[:, :, REPEAT * HEAD_SIZE :].reshape(
        rows, KEY_VALUE_HEADS * 2 * HEAD_SIZE
    )
    kv_slots = gather_ctx(kv_local)
    attended, best = attend(natural_column, begin_column, key_natural, qkv, kv_slots)
    head_max = jnp.max(best[:, :, :REPEAT, 0], 0).reshape(QUERY_HEADS)
    for mask in bits_down(count):
        head_max = jnp.maximum(head_max, swap(head_max, "ctx", mask))
    for mask in bits_down(fsdp_count):
        head_max = jnp.maximum(head_max, swap(head_max, "fsdp", mask))
    residual = tokens + slot_matmul(attended, output_slots, me_ref, 512, f32)
    scale_two = rms_scale(residual)
    unit_two = residual * scale_two
    normed_two = (unit_two * second_full).astype(bf16)

    grad_out = out_grad.reshape(rows, model)
    others = range(1, fsdp_count)
    grads = [grad_out] + [swap(grad_out, "fsdp", d) for d in others]
    normed = [normed_two] + [swap(normed_two, "fsdp", d) for d in others]
    hidden_parts, gate_parts, up_parts, sums, backs = [], [], [], [], []
    for d in range(fsdp_count):
        grad_hidden = slot_matmul_t(grads[d], down_slots, me_ref, 512, f32)
        gate_act = product(normed[d], gate_weight)
        up_proj = product(normed[d], up_weight)
        sigmoid = jax.nn.sigmoid(gate_act)
        hidden = (gate_act * sigmoid * up_proj).astype(bf16)
        grad_gate = (
            grad_hidden * up_proj * sigmoid * (1.0 + gate_act * (1.0 - sigmoid))
        ).astype(bf16)
        grad_up = (grad_hidden * gate_act * sigmoid).astype(bf16)
        hidden_parts.append(hidden)
        gate_parts.append(grad_gate)
        up_parts.append(grad_up)
        backs.append(product_t(grad_gate, gate_weight) + product_t(grad_up, up_weight))
        sums.append(slot_matmul(hidden, down_slots, me_ref, 512, f32 if d == 0 else bf16))
    grad_normed_two = sum_fsdp(backs)
    result = (residual + sum_fsdp(sums)).astype(bf16)

    second_term = jnp.sum(grad_normed_two * unit_two, 0)
    grad_residual = grad_out.astype(f32) + norm_back(
        grad_normed_two * second_full, unit_two, scale_two
    )
    grad_branch = grad_residual.astype(bf16)
    head_grad = slot_matmul_t(grad_branch, output_slots, me_ref, 512, bf16)
    query_grad, *dkv_slots = attend_back(
        natural_column, begin_column, key_natural, cosine, sine, qkv, head_grad, kv_slots
    )
    if count == 8:
        even = [
            add_rounded(dkv_slots[j][0], swap(dkv_slots[j + 1][0], "ctx", 1))
            for j in (0, 2, 4, 6)
        ]
        dkv = sum_planes(even)
    else:
        dkv = sum_halving(dkv_slots[0], "ctx")
    dkv = dkv.reshape(rows, KEY_VALUE_HEADS, 2, HEAD_SIZE)
    grad_key = dkv[:, :, 0]
    first, second = grad_key[..., :half_dim], grad_key[..., half_dim:]
    cos, sin = cosine[:, None, :half_dim], sine[:, None, half_dim:]
    grad_key = jnp.concatenate([first * cos + second * sin, second * cos - first * sin], -1)
    dqkv = jnp.concatenate(
        [
            query_grad.reshape(rows, KEY_VALUE_HEADS, REPEAT, HEAD_SIZE),
            grad_key[:, :, None].astype(bf16),
            dkv[:, :, 1:].astype(bf16),
        ],
        2,
    ).reshape(rows, KEY_VALUE_HEADS * UNIT)
    grad_normed_one = slot_matmul_t(dqkv, unit_slots, me_ref, 512, f32)
    first_term = jnp.sum(grad_normed_one * unit_one, 0)
    grad_input = grad_residual + norm_back(grad_normed_one * first_full, unit_one, scale_one)

    hidden_all = jnp.concatenate(hidden_parts, 0)
    normed_all = jnp.concatenate(normed, 0)
    grads_all = jnp.concatenate(grads, 0)
    down_sum = down_grad_sum(hidden_all, grads_all, me, count, fsdp_count).astype(bf16)
    bands = count // fsdp_count
    places = [
        (c * fsdp_count + f, (bands * f + c // fsdp_count) * fsdp_count + c % fsdp_count)
        for c in range(count)
        for f in range(fsdp_count)
    ]
    down_grad = lax.ppermute(down_sum, ("ctx", "fsdp"), places).astype(f32)
    gate_grad = weight_grad_sum(normed_all, jnp.concatenate(gate_parts, 0), me, count)
    up_grad = weight_grad_sum(normed_all, jnp.concatenate(up_parts, 0), me, count)

    def over_fsdp(summed):
        width = summed.shape[1] // fsdp_count
        return sum_fsdp(
            [
                lax.dynamic_slice_in_dim(summed, (place ^ d) * width, width, 1)
                for d in range(fsdp_count)
            ]
        )

    output_grad = over_fsdp(weight_grad_sum(attended, grad_branch, me, count))
    unit_grad = over_fsdp(weight_grad_sum(normalized, dqkv, me, count))
    unit_grad = unit_grad.reshape(depth, shard_heads, REPEAT + 2, HEAD_SIZE)
    query_out = unit_grad[:, :, :REPEAT].reshape(depth, -1)
    key_out = unit_grad[:, :, REPEAT].reshape(depth, -1)
    value_out = unit_grad[:, :, REPEAT + 1].reshape(depth, -1)

    first_out = gain_sum(first_term, me, place, count, fsdp_count)
    second_out = gain_sum(second_term, me, place, count, fsdp_count)
    multiplier = jnp.sqrt(clip_limit / jnp.maximum(head_max, clip_limit))
    key_ratio = jnp.min(multiplier.reshape(KEY_VALUE_HEADS, REPEAT), 1)
    return (
        result.reshape(1, rows, model),
        grad_input.astype(bf16).reshape(1, rows, model),
        first_out,
        query_out,
        key_out,
        value_out,
        output_grad,
        second_out,
        gate_grad,
        up_grad,
        down_grad,
        head_max,
        clipped(query_weight, multiplier),
        clipped(key_matrix, key_ratio),
    )


def solution(mesh):
    shard, whole = P(None, "fsdp"), P()
    token, block = P("fsdp", "ctx", None), P("ctx", "fsdp")
    gain = P(("ctx", "fsdp"))
    return jax.shard_map(
        on_device,
        mesh=mesh,
        in_specs=(token, token, P("fsdp", None), whole, P("fsdp"))
        + (shard,) * 4
        + (P("fsdp"),)
        + (shard,) * 3
        + (whole,),
        out_specs=(token, token, gain)
        + (block,) * 4
        + (gain,)
        + (block,) * 3
        + (whole, shard, shard),
        check_vma=False,
    )
```

time: 3750 us -> 1150 us (0.31)
  waiting for transfers between devices: 2720 us -> 577 us
  blocking collectives: 371 us -> 0 us
  matrix products: 344 us -> 146 us
  Pallas kernels: 0 us -> 127 us
  starting transfers between devices: 21.1 us -> 113 us
  local copies, waits for them, and re-layouts: 173 us -> 98.2 us
    all_gather x13 -> x0, waiting for transfers between devices: 2400 us -> none  [the longest x1 555 us: gather_weights(): lax.all_gather(gate_weight, 'fsdp', axis=1, tiled=True)]
    ppermute x0 -> x123, waiting for transfers between devices: none -> 577 us  [the longest x122 577 us: swap(): return lax.ppermute(value, axis, [(i, i ^ mask) for i in range(size)])]
    reduce_scatter x8 -> x0, waiting for transfers between devices: 272 us -> none  [the longest x1 73.6 us: on_device(): lax.psum_scatter(over_rows(rows_two, gate_cols).astype(jnp.bfloat16), 'ct...]
    all_to_all x2 -> x0, blocking collectives: 267 us -> none  [the longest x1 201 us: on_device(): lax.all_to_all(grad_up, 'fsdp', split_axis=1, concat_axis=0, tiled=True)]
    dot_general x35 -> x26, matrix products: 344 us -> 146 us  [the longest x10 60.6 us: over_rows(): lax.dot_general(left, right, (((0,), (0,)), ((), ())), preferred_element_...]
    pallas_call x0 -> x14, Pallas kernels: none -> 127 us  [the longest x6 46.9 us: slot_matmul_t(): pl.pallas_call(functools.partial(slot_matmul_t_body, len(slots), parts, d...]
    ppermute x0 -> x123, starting transfers between devices: none -> 113 us  [the longest x122 112 us: swap(): return lax.ppermute(value, axis, [(i, i ^ mask) for i in range(size)])]
    dynamic_update_slice x2 -> x0, local copies, waits for them, and re-layouts: 78.5 us -> none  [grad_update(): lax.dynamic_update_slice_in_dim(grad_keys, current + changes, offset, 0)]
  transfers between devices with their start and end apart: 26 -> 123, of which waited for: 21 -> 48; matrix products, arithmetic and copies ran while one was open for 8% -> 25% of each run, Pallas kernels for 0% -> 11%
where the time goes in v1:
time: 1150 us
  waiting for transfers between devices  577 us (50%)
  matrix products  146 us (13%)
  Pallas kernels  127 us (11%)
  starting transfers between devices  113 us (10%)
  local copies, waits for them, and re-layouts  98.2 us (9%)
  other arithmetic  82.8 us (7%)
    ppermute x122, waiting for transfers between devices, swap(): return lax.ppermute(value, axis, [(i, i ^ mask) for i in range(size)])  577 us
    ppermute x122, starting transfers between devices, swap(): return lax.ppermute(value, axis, [(i, i ^ mask) for i in range(size)])  112 us
    dot_general x10, matrix products, over_rows(): lax.dot_general(left, right, (((0,), (0,)), ((), ())), preferred_element_...  60.6 us
    pallas_call x6, Pallas kernels, slot_matmul_t(): pl.pallas_call(functools.partial(slot_matmul_t_body, len(slots), parts, d...  46.9 us
    dot_general x8, matrix products, product(): return jnp.dot(left, right, preferred_element_type=f32)  43.1 us
    dot_general x8, matrix products, product_t(): lax.dot_general(left, right, (((1,), (1,)), ((), ())), preferred_element_...  42.1 us
    pallas_call x6, Pallas kernels, slot_matmul(): pl.pallas_call(body, out_shape=jax.ShapeDtypeStruct((rows, width), out_dt...  40.2 us
    unnamed x340, local copies, waits for them, and re-layouts  31.5 us
  transfers between devices with their start and end apart: 123, of which 48 were waited for; matrix products, arithmetic and copies ran while one was open for 25% of the time, Pallas kernels for 11%

profile of v1, /device:TPU:0, one launch (start us, length us, event | category | flops | bytes accessed | tf_op | source)
XLA Modules:
  0.0 1148.0 jit_solution(8186305743951163626)
XLA Ops:
  10.3 12.3 %collective-permute-done.3 = bf16[256,1024]{1,0:T(8,128)(2,1)S(1)} collective-permute-done((bf16[256,1024]{1,0:T(8,128)(2,1)S(1)}, bf16[256,1024]{1,0:T(8,128)(2,1)S(1)}, u32[]{:S(2)}, u32[]{:S(2)}) %collective-permute-start.3) | collective-permute-done | bytes 524320 | tf_op jit(solution)/shard_map/ppermute | solution.py:27
  22.5 31.9 %collective-permute-done.4 = bf16[256,1024]{1,0:T(8,128)(2,1)S(1)} collective-permute-done((bf16[256,1024]{1,0:T(8,128)(2,1)S(1)}, bf16[256,1024]{1,0:T(8,128)(2,1)S(1)}, u32[]{:S(2)}, u32[]{:S(2)}) %collective-permute-start.4) | collective-permute-done | bytes 524320 | tf_op jit(solution)/shard_map/ppermute | solution.py:27
  69.8 34.3 %collective-permute-done.7 = bf16[256,4096]{1,0:T(8,128)(2,1)S(1)} collective-permute-done((bf16[256,4096]{1,0:T(8,128)(2,1)}, bf16[256,4096]{1,0:T(8,128)(2,1)S(1)}, u32[]{:S(2)}, u32[]{:S(2)}) %collective-permute-start.7) | collective-permute-done | bytes 2097184 | tf_op jit(solution)/shard_map/ppermute | solution.py:27
  116.2 12.8 %collective-permute-done.11 = bf16[128,4096]{1,0:T(8,128)(2,1)} collective-permute-done((bf16[128,4096]{1,0:T(8,128)(2,1)}, bf16[128,4096]{1,0:T(8,128)(2,1)}, u32[]{:S(2)}, u32[]{:S(2)}) %collective-permute-start.11) | collective-permute-done | bytes 1048608 | tf_op jit(solution)/shard_map/ppermute | solution.py:27
  137.1 8.4 collective-permute-done.33
  149.1 11.4 collective-permute-done.34
  177.9 10.4 shard_map.245.qkv_ref
  196.5 62.2 %collective-permute-done.52.x_ref = bf16[256,2048]{1,0:T(8,128)(2,1)S(1)} collective-permute-done((bf16[256,2048]{1,0:T(8,128)(2,1)}, bf16[256,2048]{1,0:T(8,128)(2,1)S(1)}, u32[]{:S(2)}, u32[]{:S(2)}) %collective-permute-start.52) | collective-permute-done | bytes 1048608 | tf_op jit(solution)/shard_map/ppermute | solution.py:27
  266.0 16.2 %collective-permute-done.15 = bf16[256,2048]{1,0:T(8,128)(2,1)} collective-permute-done((bf16[256,2048]{1,0:T(8,128)(2,1)}, bf16[256,2048]{1,0:T(8,128)(2,1)}, u32[]{:S(2)}, u32[]{:S(2)}) %collective-permute-start.15) | collective-permute-done | bytes 1048608 | tf_op jit(solution)/shard_map/ppermute | solution.py:27
  307.0 10.0 collective-permute-done.19
  361.2 16.0 %shard_map.246 = (bf16[256,2048]{1,0:T(8,128)(2,1)S(1)}, f32[2,8,8,128]{3,2,1,0:T(8,128)S(1)}) custom-call(s32[256,1]{1,0:T(8,128)S(1)} %copy.63.natural_ref, s32[256,1]{1,0:T(8,128)S(1)} %copy.64.start_ref, s32[2,1,1024]{2,1,0:T(1,128)S(1)} %bitcast.203, bf16[256,4096]{1,0:T(8,128)(2,1)} %copy-done.2, bf16[1,256,2048]{2,1,0:T(8,128)(2,1)S(1)} %copy-done.11, ...), custom_call_target="tpu_custom_call" | custom-call | flops 2147483648 | bytes 12582912 | tf_op jit(solution)/shard_map/pallas_call | solution.py:323
  424.6 54.5 %collective-permute-done.121 = f32[16]{0:T(128)S(1)} collective-permute-done((f32[16]{0:T(128)S(1)}, f32[16]{0:T(128)S(1)}, u32[]{:S(2)}, u32[]{:S(2)}) %collective-permute-start.121) | collective-permute-done | bytes 96 | tf_op jit(solution)/shard_map/ppermute | solution.py:27
  597.3 26.8 %collective-permute-done.53 = bf16[256,2048]{1,0:T(8,128)(2,1)} collective-permute-done((bf16[256,2048]{1,0:T(8,128)(2,1)}, bf16[256,2048]{1,0:T(8,128)(2,1)}, u32[]{:S(2)}, u32[]{:S(2)}) %collective-permute-start.53) | collective-permute-done | bytes 1048608 | tf_op jit(solution)/shard_map/ppermute | solution.py:27
  654.0 24.1 %shard_map.257 = (bf16[256,2048]{1,0:T(8,128)(2,1)S(1)}, bf16[1,256,2048]{2,1,0:T(8,128)(2,1)S(1)}, bf16[1,256,2048]{2,1,0:T(8,128)(2,1)S(1)}, bf16[1,256,2048]{...) custom-call(s32[256,1]{1,0:T(8,128)S(1)} %copy-done.39, ...), custom_call_target="tpu_custom_call" | custom-call | flops 5368709120 | bytes 20971520 | tf_op jit(solution)/shard_map/pallas_call | solution.py:342
  708.8 7.7 collective-permute-done.61
  731.5 10.0 collective-permute-done.62
  758.8 11.3 shard_map.258
  802.6 8.4 add_convert_fusion.3
  816.1 8.7 add_convert_fusion.1
  829.4 8.6 add_convert_fusion.2
  846.8 10.1 collective-permute-done.105
  872.5 10.5 collective-permute-done.99
  895.0 10.4 collective-permute-done.106
  930.5 8.6 collective-permute-done.85
  943.4 29.4 %collective-permute-done.75 = bf16[128,4096]{1,0:T(8,128)(2,1)S(1)} collective-permute-done((bf16[128,4096]{1,0:T(8,128)(2,1)S(1)}, bf16[128,4096]{1,0:T(8,128)(2,1)S(1)}, u32[]{:S(2)}, u32[]{:S(2)}) %collective-permute-start.75) | collective-permute-done | bytes 1048608 | tf_op jit(solution)/shard_map/ppermute | solution.py:27
  975.2 8.9 collective-permute-done.87
  991.5 15.0 %collective-permute-done.77 = bf16[128,4096]{1,0:T(8,128)(2,1)S(1)} collective-permute-done((bf16[128,4096]{1,0:T(8,128)(2,1)S(1)}, bf16[128,4096]{1,0:T(8,128)(2,1)S(1)}, u32[]{:S(2)}, u32[]{:S(2)}) %collective-permute-start.77) | collective-permute-done | bytes 1048608 | tf_op jit(solution)/shard_map/ppermute | solution.py:27
  1011.1 43.0 %collective-permute-done.76 = bf16[128,4096]{1,0:T(8,128)(2,1)S(1)} collective-permute-done((bf16[128,4096]{1,0:T(8,128)(2,1)S(1)}, bf16[128,4096]{1,0:T(8,128)(2,1)S(1)}, u32[]{:S(2)}, u32[]{:S(2)}) %collective-permute-start.76) | collective-permute-done | bytes 1048608 | tf_op jit(solution)/shard_map/ppermute | solution.py:27
  1058.1 18.6 %collective-permute-done.108 = bf16[128,2048]{1,0:T(8,128)(2,1)S(1)} collective-permute-done((bf16[128,2048]{1,0:T(8,128)(2,1)S(1)}, bf16[128,2048]{1,0:T(8,128)(2,1)S(1)}, u32[]{:S(2)}, u32[]{:S(2)}) %collective-permute-start.108) | collective-permute-done | bytes 524320 | tf_op jit(solution)/shard_map/ppermute | solution.py:27
  1082.2 11.3 collective-permute-done.72
  1101.7 10.7 collective-permute-done.88
  1114.9 27.4 %collective-permute-done.79 = bf16[256,1024]{1,0:T(8,128)(2,1)S(1)} collective-permute-done((bf16[256,1024]{1,0:T(8,128)(2,1)S(1)}, bf16[256,1024]{1,0:T(8,128)(2,1)S(1)}, u32[]{:S(2)}, u32[]{:S(2)}) %collective-permute-start.79) | collective-permute-done | bytes 524320 | tf_op jit(solution)/shard_map/ppermute | solution.py:27
  (782 shorter events, 554.7 us)
Async XLA Ops:
  60.3 51.3 %collective-permute-start = (bf16[2,512]{1,0:T(2,128)(2,1)S(1)}, bf16[2,512]{1,0:T(2,128)(2,1)S(1)}, u32[]{:S(2)}, u32[]{:S(2)}) collective-permute-start(bf16[2,512]{1,0:T(2,128)(2,1)S(1)} %pad_maximum_fusion.32), channel_id=1, source_target_pairs={{0,3},{1,2},{2,1},{3,0},{4,7},{5,6},{6,5},{7,4},{8,11},{9,10},{10,... | collective-permute-start | bytes 6152 | tf_op jit(solution)/shard_map/ppermute | solution.py:27
  62.9 51.1 %collective-permute-start.1 = (bf16[2,512]{1,0:T(2,128)(2,1)S(1)}, bf16[2,512]{1,0:T(2,128)(2,1)S(1)}, u32[]{:S(2)}, u32[]{:S(2)}) collective-permute-start(bf16[2,512]{1,0:T(2,128)(2,1)S(1)} %pad_maximum_fusion.32), channel_id=1, source_target_pairs={{0,2},{1,3},{2,0},{3,1},{4,6},{5,7},{6,4},{7,5},{8,10},{9,11},{10,... | collective-permute-start | bytes 6152 | tf_op jit(solution)/shard_map/ppermute | solution.py:27
  62.9 51.1 %collective-permute-start.2 = (bf16[2,512]{1,0:T(2,128)(2,1)S(1)}, bf16[2,512]{1,0:T(2,128)(2,1)S(1)}, u32[]{:S(2)}, u32[]{:S(2)}) collective-permute-start(bf16[2,512]{1,0:T(2,128)(2,1)S(1)} %pad_maximum_fusion.32), channel_id=1, source_target_pairs={{0,1},{1,0},{2,3},{3,2},{4,5},{5,4},{6,7},{7,6},{8,9},{9,8},{10,11... | collective-permute-start | bytes 6152 | tf_op jit(solution)/shard_map/ppermute | solution.py:27
  169.9 88.7 %collective-permute-start.52 = (bf16[256,2048]{1,0:T(8,128)(2,1)}, bf16[256,2048]{1,0:T(8,128)(2,1)S(1)}, u32[]{:S(2)}, u32[]{:S(2)}) collective-permute-start(bf16[256,2048]{1,0:T(8,128)(2,1)} %bitcast.62.x_ref), channel_id=1, source_target_pairs={{0,2},{1,3},{2,0},{3,1},{4,6},{5,7},{6,4},{7,5},{8,10},{9,11},{10,... | collective-permute-start | bytes 3145736 | tf_op jit(solution)/shard_map/ppermute | solution.py:27
  171.8 88.4 %collective-permute-start.26 = (bf16[256,2048]{1,0:T(8,128)(2,1)}, bf16[256,2048]{1,0:T(8,128)(2,1)}, u32[]{:S(2)}, u32[]{:S(2)}) collective-permute-start(bf16[256,2048]{1,0:T(8,128)(2,1)} %get-tuple-element.183), channel_id=1, source_target_pairs={{0,8},{4,12},{8,0},{12,4},{16,24},{20,28},{24,16},{28,20},{1,9},{5... | collective-permute-start | bytes 3145736 | tf_op jit(solution)/shard_map/ppermute | solution.py:27
  175.8 84.9 %collective-permute-start.37 = (bf16[256,2048]{1,0:T(8,128)(2,1)}, bf16[256,2048]{1,0:T(8,128)(2,1)S(1)}, u32[]{:S(2)}, u32[]{:S(2)}) collective-permute-start(bf16[256,2048]{1,0:T(8,128)(2,1)} %get-tuple-element.181), channel_id=1, source_target_pairs={{0,8},{4,12},{8,0},{12,4},{16,24},{20,28},{24,16},{28,20},{1,9},{5... | collective-permute-start | bytes 3145736 | tf_op jit(solution)/shard_map/ppermute | solution.py:27
  176.6 84.1 %collective-permute-start.39 = (bf16[256,2048]{1,0:T(8,128)(2,1)}, bf16[256,2048]{1,0:T(8,128)(2,1)S(1)}, u32[]{:S(2)}, u32[]{:S(2)}) collective-permute-start(bf16[256,2048]{1,0:T(8,128)(2,1)} %get-tuple-element.181), channel_id=1, source_target_pairs={{0,16},{4,20},{8,24},{12,28},{16,0},{20,4},{24,8},{28,12},{1,17},{... | collective-permute-start | bytes 3145736 | tf_op jit(solution)/shard_map/ppermute | solution.py:27
  196.0 68.5 %collective-permute-start.28 = (bf16[256,2048]{1,0:T(8,128)(2,1)}, bf16[256,2048]{1,0:T(8,128)(2,1)}, u32[]{:S(2)}, u32[]{:S(2)}) collective-permute-start(bf16[256,2048]{1,0:T(8,128)(2,1)} %get-tuple-element.183), channel_id=1, source_target_pairs={{0,16},{4,20},{8,24},{12,28},{16,0},{20,4},{24,8},{28,12},{1,17},{... | collective-permute-start | bytes 3145736 | tf_op jit(solution)/shard_map/ppermute | solution.py:27
  322.8 54.4 %collective-permute-start.25 = (bf16[256,2048]{1,0:T(8,128)(2,1)}, bf16[256,2048]{1,0:T(8,128)(2,1)}, u32[]{:S(2)}, u32[]{:S(2)}) collective-permute-start(bf16[256,2048]{1,0:T(8,128)(2,1)} %get-tuple-element.183), channel_id=1, source_target_pairs={{0,4},{4,0},{8,12},{12,8},{16,20},{20,16},{24,28},{28,24},{1,5},{5... | collective-permute-start | bytes 3145736 | tf_op jit(solution)/shard_map/ppermute | solution.py:27
  323.3 54.0 %collective-permute-start.27 = (bf16[256,2048]{1,0:T(8,128)(2,1)}, bf16[256,2048]{1,0:T(8,128)(2,1)}, u32[]{:S(2)}, u32[]{:S(2)}) collective-permute-start(bf16[256,2048]{1,0:T(8,128)(2,1)} %collective-permute-done.26), channel_id=1, source_target_pairs={{0,4},{4,0},{8,12},{12,8},{16,20},{20,16},{24,28},{28,24},{1,5},{5... | collective-permute-start | bytes 3145736 | tf_op jit(solution)/shard_map/ppermute | solution.py:27
  323.4 53.9 %collective-permute-start.29 = (bf16[256,2048]{1,0:T(8,128)(2,1)}, bf16[256,2048]{1,0:T(8,128)(2,1)}, u32[]{:S(2)}, u32[]{:S(2)}) collective-permute-start(bf16[256,2048]{1,0:T(8,128)(2,1)} %collective-permute-done.28), channel_id=1, source_target_pairs={{0,4},{4,0},{8,12},{12,8},{16,20},{20,16},{24,28},{28,24},{1,5},{5... | collective-permute-start | bytes 3145736 | tf_op jit(solution)/shard_map/ppermute | solution.py:27
  323.8 53.5 %collective-permute-start.32 = (bf16[256,2048]{1,0:T(8,128)(2,1)}, bf16[256,2048]{1,0:T(8,128)(2,1)}, u32[]{:S(2)}, u32[]{:S(2)}) collective-permute-start(bf16[256,2048]{1,0:T(8,128)(2,1)} %constant_dynamic-update-slice_fusion.4), channel_id=1, source_target_pairs={{0,4},{4,0},{8,12},{12,8},{16,20},{20,16},{24,28},{28,24},{1,5},{5... | collective-permute-start | bytes 3145736 | tf_op jit(solution)/shard_map/ppermute | solution.py:27
  387.4 100.5 %collective-permute-start.48 = (bf16[256,2048]{1,0:T(8,128)(2,1)}, bf16[256,2048]{1,0:T(8,128)(2,1)}, u32[]{:S(2)}, u32[]{:S(2)}) collective-permute-start(bf16[256,2048]{1,0:T(8,128)(2,1)} %multiply_convert_fusion.14), channel_id=1, source_target_pairs={{0,3},{1,2},{2,1},{3,0},{4,7},{5,6},{6,5},{7,4},{8,11},{9,10},{10,... | collective-permute-start | bytes 3145736 | tf_op jit(solution)/shard_map/ppermute | solution.py:27
  389.5 121.3 %collective-permute-start.46 = (bf16[256,2048]{1,0:T(8,128)(2,1)}, bf16[256,2048]{1,0:T(8,128)(2,1)}, u32[]{:S(2)}, u32[]{:S(2)}) collective-permute-start(bf16[256,2048]{1,0:T(8,128)(2,1)} %multiply_convert_fusion.14), channel_id=1, source_target_pairs={{0,2},{1,3},{2,0},{3,1},{4,6},{5,7},{6,4},{7,5},{8,10},{9,11},{10,... | collective-permute-start | bytes 3145736 | tf_op jit(solution)/shard_map/ppermute | solution.py:27
  389.5 142.1 %collective-permute-start.44 = (bf16[256,2048]{1,0:T(8,128)(2,1)}, bf16[256,2048]{1,0:T(8,128)(2,1)}, u32[]{:S(2)}, u32[]{:S(2)}) collective-permute-start(bf16[256,2048]{1,0:T(8,128)(2,1)} %multiply_convert_fusion.14), channel_id=1, source_target_pairs={{0,1},{1,0},{2,3},{3,2},{4,5},{5,4},{6,7},{7,6},{8,9},{9,8},{10,11... | collective-permute-start | bytes 3145736 | tf_op jit(solution)/shard_map/ppermute | solution.py:27
  417.7 61.5 %collective-permute-start.121 = (f32[16]{0:T(128)S(1)}, f32[16]{0:T(128)S(1)}, u32[]{:S(2)}, u32[]{:S(2)}) collective-permute-start(f32[16]{0:T(128)S(1)} %max.20), channel_id=1, source_target_pairs={{0,2},{1,3},{2,0},{3,1},{4,6},{5,7},{6,4},{7,5},{8,10},{9,11},{10,... | collective-permute-start | bytes 200 | tf_op jit(solution)/shard_map/ppermute | solution.py:27
  508.8 88.5 %collective-permute-start.55 = (bf16[256,2048]{1,0:T(8,128)(2,1)}, bf16[256,2048]{1,0:T(8,128)(2,1)}, u32[]{:S(2)}, u32[]{:S(2)}) collective-permute-start(bf16[256,2048]{1,0:T(8,128)(2,1)} %fusion.6), channel_id=1, source_target_pairs={{0,3},{1,2},{2,1},{3,0},{4,7},{5,6},{6,5},{7,4},{8,11},{9,10},{10,... | collective-permute-start | bytes 3145736 | tf_op jit(solution)/shard_map/ppermute | solution.py:27
  531.6 92.5 %collective-permute-start.53 = (bf16[256,2048]{1,0:T(8,128)(2,1)}, bf16[256,2048]{1,0:T(8,128)(2,1)}, u32[]{:S(2)}, u32[]{:S(2)}) collective-permute-start(bf16[256,2048]{1,0:T(8,128)(2,1)} %fusion.5), channel_id=1, source_target_pairs={{0,2},{1,3},{2,0},{3,1},{4,6},{5,7},{6,4},{7,5},{8,10},{9,11},{10,... | collective-permute-start | bytes 3145736 | tf_op jit(solution)/shard_map/ppermute | solution.py:27
  552.6 71.5 %collective-permute-start.51 = (bf16[256,2048]{1,0:T(8,128)(2,1)}, bf16[256,2048]{1,0:T(8,128)(2,1)}, u32[]{:S(2)}, u32[]{:S(2)}) collective-permute-start(bf16[256,2048]{1,0:T(8,128)(2,1)} %fusion.4), channel_id=1, source_target_pairs={{0,1},{1,0},{2,3},{3,2},{4,5},{5,4},{6,7},{7,6},{8,9},{9,8},{10,11... | collective-permute-start | bytes 3145736 | tf_op jit(solution)/shard_map/ppermute | solution.py:27
  560.7 228.5 %collective-permute-start.49 = (bf16[256,2048]{1,0:T(8,128)(2,1)}, bf16[256,2048]{1,0:T(8,128)(2,1)}, u32[]{:S(2)}, u32[]{:S(2)}) collective-permute-start(bf16[256,2048]{1,0:T(8,128)(2,1)} %shard_map.251), channel_id=1, source_target_pairs={{0,3},{1,2},{2,1},{3,0},{4,7},{5,6},{6,5},{7,4},{8,11},{9,10},{10,... | collective-permute-start | bytes 3145736 | tf_op jit(solution)/shard_map/ppermute | solution.py:27
  727.7 61.9 %collective-permute-start.47 = (bf16[256,2048]{1,0:T(8,128)(2,1)}, bf16[256,2048]{1,0:T(8,128)(2,1)}, u32[]{:S(2)}, u32[]{:S(2)}) collective-permute-start(bf16[256,2048]{1,0:T(8,128)(2,1)} %shard_map.250), channel_id=1, source_target_pairs={{0,2},{1,3},{2,0},{3,1},{4,6},{5,7},{6,4},{7,5},{8,10},{9,11},{10,... | collective-permute-start | bytes 3145736 | tf_op jit(solution)/shard_map/ppermute | solution.py:27
  731.5 58.2 %collective-permute-start.45 = (bf16[256,2048]{1,0:T(8,128)(2,1)S(1)}, bf16[256,2048]{1,0:T(8,128)(2,1)}, u32[]{:S(2)}, u32[]{:S(2)}) collective-permute-start(bf16[256,2048]{1,0:T(8,128)(2,1)S(1)} %copy-done.32), channel_id=1, source_target_pairs={{0,1},{1,0},{2,3},{3,2},{4,5},{5,4},{6,7},{7,6},{8,9},{9,8},{10,11... | collective-permute-start | bytes 3145736 | tf_op jit(solution)/shard_map/ppermute | solution.py:27
  741.5 61.1 %collective-permute-start.96 = (bf16[1024,2048]{1,0:T(8,128)(2,1)}, bf16[1024,2048]{1,0:T(8,128)(2,1)}, u32[]{:S(2)}, u32[]{:S(2)}) collective-permute-start(bf16[1024,2048]{1,0:T(8,128)(2,1)} %convolution_convert_fusion.4), channel_id=1, source_target_pairs={{0,4},{4,0},{8,12},{12,8},{16,20},{20,16},{24,28},{28,24},{1,5},{5... | collective-permute-start | bytes 12582920 | tf_op jit(solution)/shard_map/ppermute | solution.py:27
  789.6 69.2 %collective-permute-start.81 = (bf16[1024,2048]{1,0:T(8,128)(2,1)}, bf16[1024,2048]{1,0:T(8,128)(2,1)}, u32[]{:S(2)}, u32[]{:S(2)}) collective-permute-start(bf16[1024,2048]{1,0:T(8,128)(2,1)} %convolution_convert_fusion.1), channel_id=1, source_target_pairs={{0,4},{4,0},{8,12},{12,8},{16,20},{20,16},{24,28},{28,24},{1,5},{5... | collective-permute-start | bytes 12582920 | tf_op jit(solution)/shard_map/ppermute | solution.py:27
  802.0 106.6 %collective-permute-start.71 = (bf16[1024,4096]{1,0:T(8,128)(2,1)S(1)}, bf16[1024,4096]{1,0:T(8,128)(2,1)S(1)}, u32[]{:S(2)}, u32[]{:S(2)}) collective-permute-start(bf16[1024,4096]{1,0:T(8,128)(2,1)S(1)} %convolution_convert_fusion), channel_id=1, source_target_pairs={{0,4},{4,0},{8,12},{12,8},{16,20},{20,16},{24,28},{28,24},{1,5},{5... | collective-permute-start | bytes 25165832 | tf_op jit(solution)/shard_map/ppermute | solution.py:27
  814.1 126.0 %collective-permute-start.102 = (bf16[128,2048]{1,0:T(8,128)(2,1)}, bf16[128,2048]{1,0:T(8,128)(2,1)S(1)}, u32[]{:S(2)}, u32[]{:S(2)}) collective-permute-start(bf16[128,2048]{1,0:T(8,128)(2,1)} %get-tuple-element.116), channel_id=1, source_target_pairs={{0,16},{4,20},{8,24},{12,28},{16,0},{20,4},{24,8},{28,12},{1,17},{... | collective-permute-start | bytes 1572872 | tf_op jit(solution)/shard_map/ppermute | solution.py:27
  918.7 56.0 %collective-permute-start.116 = (bf16[512,512]{1,0:T(8,128)(2,1)S(1)}, bf16[512,512]{1,0:T(8,128)(2,1)S(1)}, u32[]{:S(2)}, u32[]{:S(2)}) collective-permute-start(bf16[512,512]{1,0:T(8,128)(2,1)S(1)} %copy-done.122), channel_id=1, source_target_pairs={{0,16},{4,20},{8,24},{12,28},{16,0},{20,4},{24,8},{28,12},{1,17},{... | collective-permute-start | bytes 1572872 | tf_op jit(solution)/shard_map/ppermute | solution.py:27
  985.6 68.6 %collective-permute-start.76 = (bf16[128,4096]{1,0:T(8,128)(2,1)S(1)}, bf16[128,4096]{1,0:T(8,128)(2,1)S(1)}, u32[]{:S(2)}, u32[]{:S(2)}) collective-permute-start(bf16[128,4096]{1,0:T(8,128)(2,1)S(1)} %add_convert_fusion.5), channel_id=1, source_target_pairs={{0,8},{4,12},{8,0},{12,4},{16,24},{20,28},{24,16},{28,20},{1,9},{5... | collective-permute-start | bytes 3145736 | tf_op jit(solution)/shard_map/ppermute | solution.py:27
  988.9 66.5 %collective-permute-start.109 = (bf16[128,2048]{1,0:T(8,128)(2,1)S(1)}, bf16[128,2048]{1,0:T(8,128)(2,1)S(1)}, u32[]{:S(2)}, u32[]{:S(2)}) collective-permute-start(bf16[128,2048]{1,0:T(8,128)(2,1)S(1)} %copy-done.120), channel_id=1, source_target_pairs={{0,16},{4,20},{8,24},{12,28},{16,0},{20,4},{24,8},{28,12},{1,17},{... | collective-permute-start | bytes 1572872 | tf_op jit(solution)/shard_map/ppermute | solution.py:27
  989.7 88.7 %collective-permute-start.82 = (bf16[128,2048]{1,0:T(8,128)(2,1)S(1)}, bf16[128,2048]{1,0:T(8,128)(2,1)S(1)}, u32[]{:S(2)}, u32[]{:S(2)}) collective-permute-start(bf16[128,2048]{1,0:T(8,128)(2,1)S(1)} %copy-done.121), channel_id=1, source_target_pairs={{0,8},{4,12},{8,0},{12,4},{16,24},{20,28},{24,16},{28,20},{1,9},{5... | collective-permute-start | bytes 1572872 | tf_op jit(solution)/shard_map/ppermute | solution.py:27
  1006.5 70.1 %collective-permute-start.108 = (bf16[128,2048]{1,0:T(8,128)(2,1)S(1)}, bf16[128,2048]{1,0:T(8,128)(2,1)S(1)}, u32[]{:S(2)}, u32[]{:S(2)}) collective-permute-start(bf16[128,2048]{1,0:T(8,128)(2,1)S(1)} %copy-done.123), channel_id=1, source_target_pairs={{0,8},{4,12},{8,0},{12,4},{16,24},{20,28},{24,16},{28,20},{1,9},{5... | collective-permute-start | bytes 1572872 | tf_op jit(solution)/shard_map/ppermute | solution.py:27
  1010.2 87.8 %collective-permute-start.117 = (bf16[1024,512]{1,0:T(8,128)(2,1)S(1)}, bf16[1024,512]{1,0:T(8,128)(2,1)S(1)}, u32[]{:S(2)}, u32[]{:S(2)}) collective-permute-start(bf16[1024,512]{1,0:T(8,128)(2,1)S(1)} %pad_maximum_fusion.17), channel_id=1, source_target_pairs={{0,0},{1,8},{2,16},{3,24},{4,1},{5,9},{6,17},{7,25},{8,2},{9,10},{... | collective-permute-start | bytes 3145736 | tf_op jit(solution)/shard_map/ppermute | solution.py:613
  (256 other events, 4383.1 us)

commit v2 on v1

--- a/solution.py
+++ b/solution.py
@@ -43,51 +43,14 @@
     return items
 
 
-def add_rounded(left, right):
-    return (left.astype(f32) + right.astype(f32)).astype(bf16)
-
-
 def gather_ctx(block):
     size = lax.axis_size("ctx")
-    if size != 8:
-        whole = block[None]
-        mask = 1
-        while mask < size:
-            whole = jnp.concatenate([whole, swap(whole, "ctx", mask)], 0)
-            mask *= 2
-        return [whole]
-    half = block.shape[0] // 2
-    over_x = swap(block, "ctx", 2)
-    over_y = swap(block, "ctx", 4)
-    other = swap(block, "ctx", 1)
-    low = swap(over_x[:half], "ctx", 4)
-    high = swap(over_y[half:], "ctx", 2)
-    far = jnp.concatenate([low, high], 0)
-    slots = [
-        block,
-        other,
-        over_x,
-        swap(over_x, "ctx", 1),
-        over_y,
-        swap(over_y, "ctx", 1),
-        far,
-        swap(far, "ctx", 1),
-    ]
-    return [slot[None] for slot in slots]
-
-
-def sum_planes(even):
-    s0, s2, s4, s6 = even
-    half = s0.shape[0] // 2
-    from_x = swap(s6[:half], "ctx", 2)
-    from_y = swap(s6[half:], "ctx", 4)
-    low2 = swap(s2[:half], "ctx", 2)
-    high4 = swap(s4[half:], "ctx", 4)
-    low4 = swap(add_rounded(s4[:half], from_x), "ctx", 4)
-    high2 = swap(add_rounded(s2[half:], from_y), "ctx", 2)
-    low = s0[:half].astype(f32) + low2.astype(f32) + low4.astype(f32)
-    high = s0[half:].astype(f32) + high2.astype(f32) + high4.astype(f32)
-    return jnp.concatenate([low, high], 0)
+    whole = block[None]
+    mask = 1
+    while mask < size:
+        whole = jnp.concatenate([whole, swap(whole, "ctx", mask)], 0)
+        mask *= 2
+    return [whole]
 
 
 def sum_halving(slots, axis):
@@ -135,6 +98,12 @@
         ]
         total = jnp.concatenate(parts_out + [total[:, (REPEAT + 1) * HEAD_SIZE :]], 1)
     out_ref[...] = total.astype(out_ref.dtype)
+
+
+def in_order(slots, me):
+    whole = jnp.concatenate(slots, 0)
+    whole = whole[me ^ jnp.arange(whole.shape[0], dtype=jnp.int32)]
+    return whole.reshape(-1, whole.shape[2])
 
 
 def in_order(slots, me):
@@ -251,7 +220,7 @@
     return query, exps / jnp.sum(exps, 1, keepdims=True), best, blk
 
 
-def attend_body(n_slots, natural_ref, start_ref, key_natural_ref, qkv_ref, *refs):
+def attend_body(n_slots, place_ref, natural_ref, start_ref, key_natural_ref, qkv_ref, *refs):
     slot_refs, (out_ref, best_ref) = refs[:n_slots], refs[n_slots:]
     keys, values = keys_of(slot_refs)
     _, probs, best, blk = scores_of(qkv_ref, keys, natural_ref, start_ref, key_natural_ref)
@@ -267,7 +236,7 @@
 
 
 def attend_back_body(
-    n_slots, natural_ref, start_ref, key_natural_ref, cosine_ref, sine_ref, qkv_ref, grad_ref, *refs
+    n_slots, place_ref, natural_ref, start_ref, key_natural_ref, cosine_ref, sine_ref, qkv_ref, grad_ref, *refs
 ):
     slot_refs, (dq_ref, *dkv_refs) = refs[:n_slots], refs[n_slots:]
     keys, values = keys_of(slot_refs)
@@ -298,56 +267,980 @@
         bf16
     )
     both = jnp.concatenate([key_grad, value_grad], 1)
-    rows = both.shape[0] // n_slots
-    for j, ref in enumerate(dkv_refs):
-        ref[...] = both[j * rows : (j + 1) * rows].reshape(ref.shape)
-
-
-def attention_specs(slots, blk, keys):
-    parts = slots[0].shape[0]
-    column = pl.BlockSpec((blk, 1), lambda r, h: (r, 0))
-    slot = pl.BlockSpec((parts, blk, 2 * HEAD_SIZE), lambda r, h: (0, r, h))
+    first = 0
+    for ref in dkv_refs:
+        rows = ref.shape[0] * ref.shape[1]
+        ref[...] = both[first : first + rows].reshape(ref.shape)
+        first += rows
+
+
+def attention_specs(slots, blk, keys, shard_heads):
+    def own_place(r, h, place):
+        return (r, (place[0] ^ (h // shard_heads)) * shard_heads + h % shard_heads)
+
+    column = pl.BlockSpec((blk, 1), lambda r, h, p: (r, 0))
     return (
-        [column, column, pl.BlockSpec((1, 1, keys), lambda r, h: (r, 0, 0))],
-        pl.BlockSpec((blk, UNIT), lambda r, h: (r, h)),
-        pl.BlockSpec((blk, REPEAT * HEAD_SIZE), lambda r, h: (r, h)),
-        slot,
-    )
-
-
-def attend(natural, start, key_natural, qkv, slots):
-    rows = qkv.shape[0]
+        [column, column, pl.BlockSpec((1, 1, keys), lambda r, h, p: (r, 0, 0))],
+        pl.BlockSpec((blk, UNIT), lambda r, h, p: (r, h)),
+        pl.BlockSpec((blk, REPEAT * HEAD_SIZE), lambda r, h, p: (r, h)),
+        pl.BlockSpec((blk, REPEAT * HEAD_SIZE), own_place),
+        pl.BlockSpec((1, 1, 8, 128), lambda r, h, p: own_place(r, h, p) + (0, 0)),
+        [
+            pl.BlockSpec((s.shape[0], blk, 2 * HEAD_SIZE), lambda r, h, p: (0, r, h))
+            for s in slots
+        ],
+    )
+
+
+def attend(place, natural, start, key_natural, qkv, slots):
+    rows, heads = qkv.shape[0], qkv.shape[1] // UNIT
     rounds, _, keys = key_natural.shape
     blk = rows // rounds
-    meta, unit, pair, slot = attention_specs(slots, blk, keys)
+    meta, unit, _, placed, best, slot = attention_specs(
+        slots, blk, keys, heads // lax.axis_size("fsdp")
+    )
     return pl.pallas_call(
         functools.partial(attend_body, len(slots)),
-        grid=(rounds, KEY_VALUE_HEADS),
-        in_specs=meta + [unit] + [slot] * len(slots),
-        out_specs=[pair, pl.BlockSpec((1, 1, 8, 128), lambda r, h: (r, h, 0, 0))],
         out_shape=[
-            jax.ShapeDtypeStruct((rows, QUERY_HEADS * HEAD_SIZE), bf16),
-            jax.ShapeDtypeStruct((rounds, KEY_VALUE_HEADS, 8, 128), f32),
+            jax.ShapeDtypeStruct((rows, heads * REPEAT * HEAD_SIZE), bf16),
+            jax.ShapeDtypeStruct((rounds, heads, 8, 128), f32),
         ],
-        **params(4 * rows * keys * QUERY_HEADS * HEAD_SIZE, 12 * 2**20),
-    )(natural, start, key_natural, qkv, *slots)
-
-
-def attend_back(natural, start, key_natural, cosine, sine, qkv, grad, slots):
-    rows = qkv.shape[0]
+        grid_spec=pltpu.PrefetchScalarGridSpec(
+            num_scalar_prefetch=1,
+            grid=(rounds, heads),
+            in_specs=meta + [unit] + slot,
+            out_specs=[placed, best],
+        ),
+        **params(4 * rows * keys * heads * REPEAT * HEAD_SIZE, 12 * 2**20),
+    )(place, natural, start, key_natural, qkv, *slots)
+
+
+def attend_back(place, natural, start, key_natural, cosine, sine, qkv, grad, slots):
+    rows, heads = qkv.shape[0], qkv.shape[1] // UNIT
     rounds, _, keys = key_natural.shape
     blk = rows // rounds
-    meta, unit, pair, slot = attention_specs(slots, blk, keys)
-    table = pl.BlockSpec((blk, HEAD_SIZE), lambda r, h: (r, 0))
+    meta, unit, pair, placed, _, slot = attention_specs(
+        slots, blk, keys, heads // lax.axis_size("fsdp")
+    )
+    table = pl.BlockSpec((blk, HEAD_SIZE), lambda r, h, p: (r, 0))
     return pl.pallas_call(
         functools.partial(attend_back_body, len(slots)),
-        grid=(rounds, KEY_VALUE_HEADS),
-        in_specs=meta + [table, table, unit, pair] + [slot] * len(slots),
-        out_specs=[pair] + [slot] * len(slots),
-        out_shape=[jax.ShapeDtypeStruct((rows, QUERY_HEADS * HEAD_SIZE), bf16)]
+        out_shape=[jax.ShapeDtypeStruct((rows, heads * REPEAT * HEAD_SIZE), bf16)]
         + [jax.ShapeDtypeStruct(s.shape, bf16) for s in slots],
-        **params(10 * rows * keys * QUERY_HEADS * HEAD_SIZE, 20 * 2**20),
-    )(natural, start, key_natural, cosine, sine, qkv, grad, *slots)
+        grid_spec=pltpu.PrefetchScalarGridSpec(
+            num_scalar_prefetch=1,
+            grid=(rounds, heads),
+            in_specs=meta + [table, table, unit, placed] + slot,
+            out_specs=[pair] + slot,
+        ),
+        **params(10 * rows * keys * heads * REPEAT * HEAD_SIZE, 20 * 2**20),
+    )(place, natural, start, key_natural, cosine, sine, qkv, grad, *slots)
+
+
+ANY = pl.BlockSpec(memory_space=pl.ANY)
+VMEM = pl.BlockSpec(memory_space=pltpu.VMEM)
+MESH = pl.DeviceIdType.MESH
+OVER_ROWS = (((0,), (0,)), ((), ()))
+OVER_COLUMNS = (((1,), (1,)), ((), ()))
+
+
+def flip(place, mask):
+    for bit in (1, 2, 4):
+        if mask & bit:
+            place = place + bit - 2 * bit * lax.rem(lax.div(place, bit), 2)
+    return place
+
+
+def device(ctx, fsdp):
+    return {
+        "ctx": flip(lax.axis_index("ctx"), ctx),
+        "fsdp": flip(lax.axis_index("fsdp"), fsdp),
+    }
+
+
+def greet(ctx_masks, fsdp_masks):
+    barrier = pltpu.get_barrier_semaphore()
+    partners = [(m, 0) for m in ctx_masks] + [(0, m) for m in fsdp_masks]
+    for ctx, fsdp in partners:
+        pl.semaphore_signal(barrier, inc=1, device_id=device(ctx, fsdp), device_id_type=MESH)
+    pl.semaphore_wait(barrier, len(partners))
+
+
+class Transfers:
+    def __init__(self, send, recv):
+        self.send, self.recv, self.count, self.open = send, recv, 0, {}
+
+    def start(self, src, dst, ctx=0, fsdp=0):
+        number = self.count
+        copy = pltpu.make_async_remote_copy(
+            src_ref=src,
+            dst_ref=dst,
+            send_sem=self.send.at[number],
+            recv_sem=self.recv.at[number],
+            device_id=device(ctx, fsdp),
+            device_id_type=MESH,
+        )
+        copy.start()
+        copy_key = id(copy)
+        self.open[copy_key] = copy
+        self.count += 1
+        return copy
+
+    def release(self, copy):
+        self.open.pop(id(copy)).wait_send()
+
+    def finish(self):
+        for copy in self.open.values():
+            copy.wait_send()
+
+
+def remote_call(body, outs, out_specs, in_specs, scratch, transfers, number, flops=0, moved=2**22):
+    return pl.pallas_call(
+        body,
+        out_shape=outs,
+        in_specs=in_specs,
+        out_specs=out_specs,
+        scratch_shapes=list(scratch)
+        + [pltpu.SemaphoreType.DMA((transfers,)), pltpu.SemaphoreType.DMA((transfers,))],
+        compiler_params=pltpu.CompilerParams(
+            vmem_limit_bytes=60 * 2**20, collective_id=number, has_side_effects=True
+        ),
+        cost_estimate=pl.CostEstimate(flops=flops, bytes_accessed=moved, transcendentals=0),
+    )
+
+
+class PlaneGather:
+    def __init__(self, transfers, slots):
+        self.t, self.s = transfers, slots
+        self.half = slots[0].shape[0] // 2
+
+    def begin(self):
+        s, t = self.s, self.t
+        self.x = t.start(s[0], s[2], ctx=2)
+        self.y = t.start(s[0], s[4], ctx=4)
+        self.c = [t.start(s[0], s[1], ctx=1)]
+
+    def middle(self):
+        s, t, h = self.s, self.t, self.half
+        self.x.wait_recv()
+        self.low = t.start(s[2].at[:h], s[6].at[:h], ctx=4)
+        self.c.append(t.start(s[2], s[3], ctx=1))
+        self.y.wait_recv()
+        self.high = t.start(s[4].at[h:], s[6].at[h:], ctx=2)
+        self.c.append(t.start(s[4], s[5], ctx=1))
+
+    def end(self):
+        s, t = self.s, self.t
+        self.low.wait_recv()
+        self.high.wait_recv()
+        self.c.append(t.start(s[6], s[7], ctx=1))
+
+    def ready(self):
+        for copy in self.c:
+            copy.wait_recv()
+
+
+def run_gathers(gathers):
+    for k in range(len(gathers) + 2):
+        if k < len(gathers):
+            for over in gathers[k][0]:
+                over.wait_recv()
+            gathers[k][1].begin()
+        if 0 <= k - 1 < len(gathers):
+            gathers[k - 1][1].middle()
+        if 0 <= k - 2 < len(gathers):
+            gathers[k - 2][1].end()
+    for _, gather in gathers:
+        gather.ready()
+
+
+def weight_gather_body(
+    query_ref, key_ref, value_ref, output_ref, down_ref, unit_out, output_out, down_out, send, recv
+):
+    me, place = lax.axis_index("ctx"), lax.axis_index("fsdp")
+    depth = unit_out.shape[2]
+    own = pl.ds(pl.multiple_of(me * depth, depth), depth)
+    greet((1, 2, 4), (1, 2, 3))
+    t = Transfers(send, recv)
+    gathers = []
+    for d in (1, 2, 3):
+        first, overs = 0, []
+        for ref in (query_ref, key_ref, value_ref):
+            width = ref.shape[1]
+            overs.append(
+                t.start(ref.at[own], unit_out.at[d - 1, 0, :, first : first + width], fsdp=d)
+            )
+            first += width
+        gathers.append((overs, PlaneGather(t, [unit_out.at[d - 1, j] for j in range(8)])))
+    for d in (1, 2, 3):
+        over = t.start(output_ref.at[own], output_out.at[d - 1, 0], fsdp=d)
+        gathers.append(([over], PlaneGather(t, [output_out.at[d - 1, j] for j in range(8)])))
+    for d in (1, 2, 3):
+        row = flip(place, d) * 8 * depth + me * depth
+        over = t.start(
+            down_ref.at[pl.ds(pl.multiple_of(row, depth), depth)], down_out.at[d - 1, 0], fsdp=d
+        )
+        gathers.append(([over], PlaneGather(t, [down_out.at[d - 1, j] for j in range(8)])))
+    run_gathers(gathers)
+    t.finish()
+
+
+def weight_gather(query, key, value, output, down):
+    depth = query.shape[0] // 8
+    widths = (query.shape[1] + key.shape[1] + value.shape[1], output.shape[1], down.shape[1])
+    outs = [jax.ShapeDtypeStruct((3, 8, depth, w), bf16) for w in widths]
+    return remote_call(weight_gather_body, outs, [ANY] * 3, [ANY] * 5, [], 15 + 9 * 8, 0)(
+        query, key, value, output, down
+    )
+
+
+class RowGather:
+    def __init__(self, own, slots, send, recv):
+        self.own, self.slots, self.send, self.recv = own, slots, send, recv
+        place = lax.axis_index("fsdp")
+        self.inner = (place == 1) | (place == 2)
+
+    def copy(self, src, dst, number, fsdp):
+        return pltpu.make_async_remote_copy(
+            src_ref=src,
+            dst_ref=self.slots[dst],
+            send_sem=self.send.at[number],
+            recv_sem=self.recv.at[dst - 1],
+            device_id=device(0, fsdp),
+            device_id_type=MESH,
+        )
+
+    def near(self):
+        return self.copy(self.own, 1, 0, 1)
+
+    def across(self):
+        return self.copy(self.own, 3, 1, 3)
+
+    def near_on(self):
+        return self.copy(self.slots[1], 2, 2, 3)
+
+    def across_on(self):
+        return self.copy(self.slots[3], 2, 3, 1)
+
+    def second_on(self):
+        return self.copy(self.slots[2], 3, 4, 1)
+
+    def begin(self):
+        self.near().start()
+
+        @pl.when(self.inner)
+        def _():
+            self.across().start()
+
+    def first(self):
+        self.near().wait_recv()
+
+        @pl.when(self.inner)
+        def _():
+            self.near_on().start()
+            self.across().wait_recv()
+            self.across_on().start()
+
+    def second(self):
+        self.near_on().wait_recv()
+
+        @pl.when(self.inner)
+        def _():
+            self.second_on().start()
+
+    def third(self):
+        @pl.when(jnp.logical_not(self.inner))
+        def _():
+            self.second_on().wait_recv()
+
+    def finish(self):
+        self.near().wait_send()
+
+        @pl.when(self.inner)
+        def _():
+            self.across().wait_send()
+            self.near_on().wait_send()
+            self.across_on().wait_send()
+            self.second_on().wait_send()
+
+
+def kv_gather_body(kv_ref, dy_ref, kv_out, dy_out, row_send, row_recv, send, recv):
+    greet((1, 2, 4), (1, 3))
+    t = Transfers(send, recv)
+    gather = PlaneGather(t, [kv_ref] + [kv_out.at[j] for j in range(7)])
+    row = RowGather(dy_ref, [None] + [dy_out.at[d] for d in range(3)], row_send, row_recv)
+    gather.begin()
+    row.begin()
+    gather.middle()
+    row.first()
+    gather.end()
+    gather.ready()
+    row.second()
+    row.third()
+    row.finish()
+    t.finish()
+
+
+def kv_gather(kv, dy):
+    return remote_call(
+        kv_gather_body,
+        [jax.ShapeDtypeStruct((7,) + kv.shape, bf16), jax.ShapeDtypeStruct((3,) + dy.shape, bf16)],
+        [ANY] * 2,
+        [ANY] * 2,
+        [pltpu.SemaphoreType.DMA((5,)), pltpu.SemaphoreType.DMA((3,))],
+        8,
+        1,
+    )(kv, dy)
+
+
+TILE = 256
+
+
+def feed_forward_row_body(
+    h_ref, dy_ref, dy_rest, gate_ref, up_ref, down_own, down_rest,
+    hid_out, dg_out, du_out, h_out, y_out, y_rest, back_out,
+    gates, ups, downs, hs, dys, y_acc, back_acc, back_send, back_land, y_send, stage,
+    load_sem, down_sem, dy_sem, h_sem, stage_sem, y_sem, row_send, row_recv, send, recv,
+):
+    rows, model = h_ref.shape
+    tiles = gates.shape[0]
+    me, place = lax.axis_index("ctx"), lax.axis_index("fsdp")
+    width = down_own.shape[1]
+    loads = []
+    for i in range(tiles):
+        cols = pl.ds(i * TILE, TILE)
+        loads.append(pltpu.make_async_copy(gate_ref.at[:, cols], gates.at[i], load_sem.at[0, i]))
+        loads.append(pltpu.make_async_copy(up_ref.at[:, cols], ups.at[i], load_sem.at[1, i]))
+    for j in range(tiles):
+        block = flip(me, j)
+        own_rows = pl.ds(pl.multiple_of(place * tiles * TILE + block * TILE, TILE), TILE)
+        for d in range(4):
+            cols = pl.ds(pl.multiple_of(flip(place, d) * width, width), width)
+            src = down_own.at[own_rows] if d == 0 else down_rest.at[d - 1, j]
+            loads.append(pltpu.make_async_copy(src, downs.at[block, :, cols], down_sem.at[j, d]))
+    for d in range(4):
+        src = dy_ref if d == 0 else dy_rest.at[d - 1]
+        loads.append(pltpu.make_async_copy(src, dys.at[d], dy_sem.at[d]))
+    for load in loads:
+        load.start()
+    greet((), (1, 2, 3))
+    t = Transfers(send, recv)
+    row = RowGather(h_ref, [None] + [hs.at[d] for d in range(3)], row_send, row_recv)
+    row.begin()
+    for load in loads:
+        load.wait()
+
+    def stage_copy(slot, k, part, i):
+        out = (hid_out, dg_out, du_out)[k]
+        cols = pl.ds(pl.multiple_of(i * TILE, TILE), TILE)
+        return pltpu.make_async_copy(
+            stage.at[slot, k], out.at[pl.ds(part * rows, rows), cols], stage_sem.at[slot, k]
+        )
+
+    def chunk(part, h):
+        def step(i, carry):
+            slot = lax.rem(i, 2)
+            gate, up, down = gates[i], ups[i], downs[i]
+            g = jnp.dot(h[...], gate, preferred_element_type=f32)
+            u = jnp.dot(h[...], up, preferred_element_type=f32)
+            grad = lax.dot_general(dys[part], down, OVER_COLUMNS, preferred_element_type=f32)
+            sigmoid = jax.nn.sigmoid(g)
+            silu = g * sigmoid
+            hidden = (silu * u).astype(bf16)
+            grad_gate = (grad * u * sigmoid * (1.0 + g * (1.0 - sigmoid))).astype(bf16)
+            grad_up = (grad * silu).astype(bf16)
+
+            @pl.when(i >= 2)
+            def _():
+                for k in range(3):
+                    stage_copy(slot, k, part, i - 2).wait()
+
+            stage[slot, 0] = hidden
+            stage[slot, 1] = grad_gate
+            stage[slot, 2] = grad_up
+            for k in range(3):
+                stage_copy(slot, k, part, i).start()
+            y = jnp.dot(hidden, down, preferred_element_type=f32)
+            back = lax.dot_general(grad_gate, gate, OVER_COLUMNS, preferred_element_type=f32)
+            back += lax.dot_general(grad_up, up, OVER_COLUMNS, preferred_element_type=f32)
+
+            @pl.when(i == 0)
+            def _():
+                y_acc[...] = y
+                back_acc[...] = back
+
+            @pl.when(i > 0)
+            def _():
+                y_acc[...] += y
+                back_acc[...] += back
+
+            return carry
+
+        lax.fori_loop(0, tiles, step, 0)
+        for i in (tiles - 2, tiles - 1):
+            for k in range(3):
+                stage_copy(i % 2, k, part, i).wait()
+
+    def keep_h(part, h):
+        return pltpu.make_async_copy(h, h_out.at[pl.ds(part * rows, rows)], h_sem.at[part])
+
+    keep_h(0, h_ref).start()
+    chunk(0, h_ref)
+    y_out[...] = y_acc[...]
+    back_out[...] = back_acc[...]
+    row.first()
+    backs, y_copy = [], None
+    for part in (1, 2, 3):
+        h = hs.at[part - 1]
+        if part == 2:
+            row.second()
+        if part == 3:
+            row.third()
+        keep_h(part, h).start()
+        chunk(part, h)
+        back_send[part - 1] = back_acc[...].astype(bf16)
+        backs.append(t.start(back_send.at[part - 1], back_land.at[part - 1], fsdp=part))
+        if y_copy is not None:
+            y_copy.wait()
+        y_send[...] = y_acc[...].astype(bf16)
+        y_copy = pltpu.make_async_copy(y_send, y_rest.at[part - 1], y_sem.at[part - 1])
+        y_copy.start()
+    y_copy.wait()
+    for part in range(4):
+        keep_h(part, h_ref if part == 0 else hs.at[part - 1]).wait()
+    for d in range(3):
+        backs[d].wait_recv()
+        back_out[...] += back_land[d].astype(f32)
+    row.finish()
+    t.finish()
+
+
+def feed_forward_row(h, dy, dy_rest, gate, up, down_own, down_rest):
+    rows, model = h.shape
+    units = gate.shape[1]
+    tiles = units // TILE
+    wide = jax.ShapeDtypeStruct((4 * rows, units), bf16)
+    block = pltpu.VMEM((rows, model), f32)
+    dma = pltpu.SemaphoreType.DMA
+    return remote_call(
+        feed_forward_row_body,
+        [wide, wide, wide, jax.ShapeDtypeStruct((4 * rows, model), bf16)]
+        + [jax.ShapeDtypeStruct((rows, model), f32), jax.ShapeDtypeStruct((3, rows, model), bf16)]
+        + [jax.ShapeDtypeStruct((rows, model), f32)],
+        [ANY] * 4 + [VMEM, ANY, VMEM],
+        [VMEM] + [ANY] * 6,
+        [
+            pltpu.VMEM((tiles, model, TILE), bf16),
+            pltpu.VMEM((tiles, model, TILE), bf16),
+            pltpu.VMEM((tiles, TILE, model), bf16),
+            pltpu.VMEM((3, rows, model), bf16),
+            pltpu.VMEM((4, rows, model), bf16),
+            block,
+            block,
+            pltpu.VMEM((3, rows, model), bf16),
+            pltpu.VMEM((3, rows, model), bf16),
+            pltpu.VMEM((rows, model), bf16),
+            pltpu.VMEM((2, 3, rows, TILE), bf16),
+            dma((2, tiles)),
+            dma((tiles, 4)),
+            dma((4,)),
+            dma((4,)),
+            dma((2, 3)),
+            dma((3,)),
+            dma((5,)),
+            dma((3,)),
+        ],
+        3,
+        2,
+        flops=48 * rows * model * units,
+    )(h, dy, dy_rest, gate, up, down_own, down_rest)
+
+
+class PlaneSum:
+    def __init__(self, transfers, cores, far, near, sums, total):
+        self.t, self.cores, self.far, self.near = transfers, cores, far, near
+        self.sums, self.total = sums, total
+        self.half = cores.shape[1] // 2
+        self.over = {}
+
+    def send_odd(self, j, src):
+        self.over[j - 1] = self.t.start(src, self.cores.at[(j - 1) // 2], ctx=1)
+        return self.over[j - 1]
+
+    def even(self, j, value):
+        t, h = self.t, self.half
+        self.over[j].wait_recv()
+        value = value + self.cores[j // 2].astype(f32)
+        if j == 0:
+            self.total[...] = value
+            return
+        out = self.sums.at[(6, 2, 4).index(j)]
+        out[...] = value.astype(bf16)
+        if j == 6:
+            self.x6 = t.start(out.at[:h], self.far.at[:h], ctx=2)
+            self.y6 = t.start(out.at[h:], self.far.at[h:], ctx=4)
+        elif j == 2:
+            self.x2 = t.start(out.at[:h], self.near.at[0, :h], ctx=2)
+        else:
+            self.y4 = t.start(out.at[h:], self.near.at[1, h:], ctx=4)
+
+    def pass_on(self):
+        t, h = self.t, self.half
+        two, four = self.sums.at[1], self.sums.at[2]
+        self.y6.wait_recv()
+        two[h:] = (two[h:].astype(f32) + self.far[h:].astype(f32)).astype(bf16)
+        self.x2b = t.start(two.at[h:], self.near.at[0, h:], ctx=2)
+        self.x6.wait_recv()
+        four[:h] = (four[:h].astype(f32) + self.far[:h].astype(f32)).astype(bf16)
+        self.y4b = t.start(four.at[:h], self.near.at[1, :h], ctx=4)
+
+    def close(self):
+        for copy in (self.x2, self.x2b, self.y4, self.y4b):
+            copy.wait_recv()
+        return self.total[...] + self.near[0].astype(f32) + self.near[1].astype(f32)
+
+
+def plane_sum_scratch(count, rows, columns):
+    return [
+        pltpu.VMEM((count, 4, rows, columns), bf16),
+        pltpu.VMEM((count, rows, columns), bf16),
+        pltpu.VMEM((count, 2, rows, columns), bf16),
+        pltpu.VMEM((count, 3, rows, columns), bf16),
+        pltpu.VMEM((count, rows, columns), f32),
+    ]
+
+
+def grads_body(
+    h_ref, dg_ref, du_ref, hid_ref, dy_ref, dy_rest, y_rest,
+    gate_out, up_out, down_out, y_land,
+    left, rights, odd, cores, far, near, sums, totals, left_sem, right_sem, dy_sem, out_sem,
+    send, recv,
+):
+    me = lax.axis_index("ctx")
+    rows = dy_ref.shape[0]
+    depth = cores.shape[2]
+    dys = [dy_ref] + [dy_rest.at[d] for d in range(3)]
+    right_copies = [
+        [pltpu.make_async_copy(dg_ref, rights.at[0], right_sem.at[0])],
+        [pltpu.make_async_copy(du_ref, rights.at[1], right_sem.at[1])],
+        [
+            pltpu.make_async_copy(p, rights.at[0, i * rows : (i + 1) * rows], dy_sem.at[i])
+            for i, p in enumerate(dys)
+        ],
+    ]
+    left_copies = [
+        pltpu.make_async_copy(h_ref, left, left_sem.at[0]),
+        pltpu.make_async_copy(hid_ref, left, left_sem.at[1]),
+    ]
+    left_copies[0].start()
+    right_copies[0][0].start()
+    right_copies[1][0].start()
+    greet((1, 2, 4), (1, 2, 3))
+    t = Transfers(send, recv)
+    y_copies = [t.start(y_rest.at[d - 1], y_land.at[d - 1], fsdp=d) for d in (1, 2, 3)]
+    left_copies[0].wait()
+    jobs, odd_copies, outs = [], {}, []
+
+    def close(k):
+        totals[k] = jobs[k].close()
+        out = pltpu.make_async_copy(totals.at[k], (gate_out, up_out)[k], out_sem.at[k])
+        out.start()
+        outs.append(out)
+
+    for k in range(3):
+        job = PlaneSum(t, cores.at[k], far.at[k], near.at[k], sums.at[k], totals.at[k])
+        jobs.append(job)
+        if k == 2:
+            for copy in [left_copies[1]] + right_copies[2]:
+                copy.start()
+            left_copies[1].wait()
+        for copy in right_copies[k]:
+            copy.wait()
+
+        def partial(j):
+            block = pl.ds(pl.multiple_of(flip(me, j) * depth, depth), depth)
+            return lax.dot_general(
+                left[:, block], rights[k % 2], OVER_ROWS, preferred_element_type=f32
+            )
+
+        for j in (7, 5, 3, 1):
+            if j in odd_copies:
+                t.release(odd_copies[j])
+            odd[j // 2] = partial(j).astype(bf16)
+            odd_copies[j] = job.send_odd(j, odd.at[j // 2])
+        if k:
+            jobs[k - 1].pass_on()
+        for j in (6, 2, 4, 0):
+            job.even(j, partial(j))
+        if k:
+            close(k - 1)
+    jobs[2].pass_on()
+    for copy in y_copies:
+        copy.wait_recv()
+    down_out[...] = jobs[2].close().astype(bf16)
+    for copy in outs:
+        copy.wait()
+    t.finish()
+
+
+def grads_row(h, dg, du, hid, dy, dy_rest, y_rest):
+    rows, model = dy.shape
+    depth = model // 8
+    dma = pltpu.SemaphoreType.DMA
+    summed = jax.ShapeDtypeStruct((depth, dg.shape[1]), f32)
+    return remote_call(
+        grads_body,
+        [summed, summed, jax.ShapeDtypeStruct((depth, model), bf16), jax.ShapeDtypeStruct(y_rest.shape, bf16)],
+        [ANY, ANY, VMEM, ANY],
+        [ANY] * 7,
+        [
+            pltpu.VMEM(h.shape, bf16),
+            pltpu.VMEM((2,) + h.shape, bf16),
+            pltpu.VMEM((4, depth, model), bf16),
+        ]
+        + plane_sum_scratch(3, depth, model)
+        + [dma((2,)), dma((2,)), dma((4,)), dma((2,))],
+        3 + 3 * 10,
+        3,
+        flops=6 * h.shape[0] * model * model,
+    )(h, dg, du, hid, dy, dy_rest, y_rest)
+
+
+def kv_sum_body(
+    first_ref, rest_ref, cosine_ref, sine_ref, out_ref,
+    evens, cores, far, near, sums, totals, even_sem, send, recv,
+):
+    slots = [first_ref.at[0]] + [rest_ref.at[j] for j in range(7)]
+    copies = {
+        j: pltpu.make_async_copy(slots[j], evens.at[j // 2], even_sem.at[j // 2])
+        for j in (6, 2, 4, 0)
+    }
+    for copy in copies.values():
+        copy.start()
+    greet((1, 2, 4), ())
+    t = Transfers(send, recv)
+    job = PlaneSum(t, cores.at[0], far.at[0], near.at[0], sums.at[0], totals.at[0])
+    for j in (7, 3, 5, 1):
+        job.send_odd(j, slots[j])
+    for j in (6, 2, 4, 0):
+        copies[j].wait()
+        job.even(j, evens[j // 2].astype(f32))
+    job.pass_on()
+    total = job.close()
+    cosine, sine = cosine_ref[...], -sine_ref[...]
+    for h in range(total.shape[1] // (2 * HEAD_SIZE)):
+        first = 2 * h * HEAD_SIZE
+        middle = first + HEAD_SIZE
+        out_ref[:, first:middle] = rotate(total[:, first:middle], cosine, sine).astype(bf16)
+        out_ref[:, middle : middle + HEAD_SIZE] = total[:, middle : middle + HEAD_SIZE].astype(bf16)
+    t.finish()
+
+
+def kv_sum(first, rest, cosine, sine):
+    _, rows, width = first.shape
+    return remote_call(
+        kv_sum_body,
+        jax.ShapeDtypeStruct((rows, width), bf16),
+        VMEM,
+        [ANY, ANY, VMEM, VMEM],
+        [pltpu.VMEM((4, rows, width), bf16)]
+        + plane_sum_scratch(1, rows, width)
+        + [pltpu.SemaphoreType.DMA((4,))],
+        10,
+        4,
+    )(first, rest, cosine, sine)
+
+
+def unit_grads_body(
+    h_ref, dq_ref, dkv_ref, attended_ref, db_ref,
+    query_out, key_out, value_out, output_out,
+    odd, cores, far, near, sums, totals, row_send, row_land,
+    send, recv,
+):
+    me, place = lax.axis_index("ctx"), lax.axis_index("fsdp")
+    depth = cores.shape[2]
+    width = row_land.shape[3]
+    greet((1, 2, 4), (1, 2, 3))
+    t = Transfers(send, recv)
+    pairs = ((attended_ref, db_ref), (h_ref, dq_ref), (h_ref, dkv_ref))
+    jobs, odd_copies, over = [], {}, [None] * 3
+
+    def columns(k, d):
+        if k == 0:
+            return pl.ds(pl.multiple_of(flip(place, d) * width, width), width)
+        return pl.ds(d * width, width)
+
+    def close(k):
+        totals[k] = jobs[k].close()
+        over[k] = []
+        for d in (1, 2, 3):
+            row_send[k, d - 1] = totals[k, :, columns(k, d)].astype(bf16)
+            over[k].append(t.start(row_send.at[k, d - 1], row_land.at[k, d - 1], fsdp=d))
+
+    for k in range(3):
+        left, right = pairs[k]
+        job = PlaneSum(t, cores.at[k], far.at[k], near.at[k], sums.at[k], totals.at[k])
+        jobs.append(job)
+
+        def partial(j):
+            block = pl.ds(pl.multiple_of(flip(me, j) * depth, depth), depth)
+            return lax.dot_general(
+                left[:, block], right[...], OVER_ROWS, preferred_element_type=f32
+            )
+
+        for j in (7, 5, 3, 1):
+            if j in odd_copies:
+                t.release(odd_copies[j])
+            odd[j // 2] = partial(j).astype(bf16)
+            odd_copies[j] = job.send_odd(j, odd.at[j // 2])
+        if k:
+            jobs[k - 1].pass_on()
+        for j in (6, 2, 4, 0):
+            job.even(j, partial(j))
+        if k:
+            close(k - 1)
+    jobs[2].pass_on()
+    close(2)
+    for k in range(3):
+        total = totals[k, :, columns(k, 0)]
+        for d in range(3):
+            over[k][d].wait_recv()
+            total = total + row_land[k, d].astype(f32)
+        if k == 0:
+            output_out[...] = total
+        elif k == 1:
+            query_out[...] = total
+        else:
+            for h in range(total.shape[1] // (2 * HEAD_SIZE)):
+                first = 2 * h * HEAD_SIZE
+                here = slice(h * HEAD_SIZE, (h + 1) * HEAD_SIZE)
+                key_out[:, here] = total[:, first : first + HEAD_SIZE]
+                value_out[:, here] = total[:, first + HEAD_SIZE : first + 2 * HEAD_SIZE]
+    t.finish()
+
+
+def unit_grads(h, dq, dkv, attended, db):
+    rows, model = h.shape
+    depth, width = model // 8, model // 4
+    wide = jax.ShapeDtypeStruct((depth, width), f32)
+    half = jax.ShapeDtypeStruct((depth, width // 2), f32)
+    return remote_call(
+        unit_grads_body,
+        [wide, half, half, wide],
+        [VMEM] * 4,
+        [VMEM] * 5,
+        [pltpu.VMEM((4, depth, model), bf16)]
+        + plane_sum_scratch(3, depth, model)
+        + [pltpu.VMEM((3, 3, depth, width), bf16)] * 2,
+        3 * (10 + 3),
+        5,
+        flops=6 * rows * model * model,
+    )(h, dq, dkv, attended, db)
+
+
+def unit_specs(depth, slots):
+    def of_rest(width, first):
+        return pl.BlockSpec(
+            (1, slots, depth, width), lambda d, h, p: (jnp.maximum(d - 1, 0), 0, 0, first + h)
+        )
+
+    def of_own(width):
+        return pl.BlockSpec(
+            (slots * depth, width), lambda d, h, p: (0, jnp.where(d == 0, h, 1))
+        )
+
+    widths = ((2 * HEAD_SIZE, 0), (HEAD_SIZE, 4), (HEAD_SIZE, 6))
+    return [of_own(w) for w, _ in widths] + [of_rest(w, first) for w, first in widths]
+
+
+def unit_forward_body(
+    place_ref, h_ref, cosine_ref, sine_ref, q_own, k_own, v_own, q_rest, k_rest, v_rest,
+    unit_out, kv_out, total,
+):
+    d = pl.program_id(0)
+
+    @pl.when(d == 0)
+    def _():
+        weight = jnp.concatenate([q_own[...], k_own[...], v_own[...]], 1)
+        total[...] = jnp.dot(h_ref[...], weight, preferred_element_type=f32)
+
+    @pl.when(d > 0)
+    def _():
+        slots, depth = q_rest.shape[1], q_rest.shape[2]
+        value = None
+        for j in range(slots):
+            owner = place_ref[0] ^ j
+            part = h_ref[:, pl.ds(pl.multiple_of(owner * depth, depth), depth)]
+            weight = jnp.concatenate([q_rest[0, j], k_rest[0, j], v_rest[0, j]], 1)
+            term = jnp.dot(part, weight, preferred_element_type=f32)
+            value = term if value is None else value + term
+        total[...] = value
+
+    cosine, sine = cosine_ref[...], sine_ref[...]
+    turned = [
+        rotate(total[:, i * HEAD_SIZE : (i + 1) * HEAD_SIZE], cosine, sine).astype(bf16)
+        for i in range(REPEAT + 1)
+    ]
+    value = total[:, (REPEAT + 1) * HEAD_SIZE :].astype(bf16)
+    unit_out[...] = jnp.concatenate(turned + [value], 1)
+    kv_out[...] = jnp.concatenate([turned[REPEAT], value], 1)
+
+
+def unit_forward(places, h, cosine, sine, query, key, value, rest):
+    rows = h.shape[0]
+    heads = query.shape[1] // (REPEAT * HEAD_SIZE)
+    _, slots, depth, _ = rest.shape
+    whole = lambda a: pl.BlockSpec(a.shape, lambda d, h, p: (0, 0))
+    return pl.pallas_call(
+        unit_forward_body,
+        out_shape=[
+            jax.ShapeDtypeStruct((rows, 4 * heads * UNIT), bf16),
+            jax.ShapeDtypeStruct((rows, 4 * heads * 2 * HEAD_SIZE), bf16),
+        ],
+        grid_spec=pltpu.PrefetchScalarGridSpec(
+            num_scalar_prefetch=1,
+            grid=(4, heads),
+            in_specs=[whole(h), whole(cosine), whole(sine)] + unit_specs(depth, slots),
+            out_specs=[
+                pl.BlockSpec((rows, UNIT), lambda d, h, p: (0, d * heads + h)),
+                pl.BlockSpec((rows, 2 * HEAD_SIZE), lambda d, h, p: (0, d * heads + h)),
+            ],
+            scratch_shapes=[pltpu.VMEM((rows, UNIT), f32)],
+        ),
+        **params(8 * rows * h.shape[1] * heads * UNIT, 8 * h.shape[1] * heads * UNIT),
+    )(places, h, cosine, sine, query, key, value, rest, rest, rest)
+
+
+def unit_back_body(
+    place_ref, dq_ref, dkv_ref, q_own, k_own, v_own, q_rest, k_rest, v_rest, out_ref
+):
+    d, h = pl.program_id(0), pl.program_id(1)
+    grad = jnp.concatenate([dq_ref[...], dkv_ref[...]], 1)
+
+    @pl.when((d == 0) & (h == 0))
+    def _():
+        out_ref[...] = jnp.zeros_like(out_ref)
+
+    @pl.when(d == 0)
+    def _():
+        weight = jnp.concatenate([q_own[...], k_own[...], v_own[...]], 1)
+        out_ref[...] += lax.dot_general(grad, weight, OVER_COLUMNS, preferred_element_type=f32)
+
+    @pl.when(d > 0)
+    def _():
+        slots, depth = q_rest.shape[1], q_rest.shape[2]
+        for j in range(slots):
+            owner = place_ref[0] ^ j
+            cols = pl.ds(pl.multiple_of(owner * depth, depth), depth)
+            weight = jnp.concatenate([q_rest[0, j], k_rest[0, j], v_rest[0, j]], 1)
+            out_ref[:, cols] += lax.dot_general(
+                grad, weight, OVER_COLUMNS, preferred_element_type=f32
+            )
+
+
+def unit_back(places, dq, dkv, query, key, value, rest):
+    rows = dq.shape[0]
+    heads = query.shape[1] // (REPEAT * HEAD_SIZE)
+    _, slots, depth, _ = rest.shape
+    model = slots * depth
+    pair = pl.BlockSpec((rows, 2 * HEAD_SIZE), lambda d, h, p: (0, d * heads + h))
+    return pl.pallas_call(
+        unit_back_body,
+        out_shape=jax.ShapeDtypeStruct((rows, model), f32),
+        grid_spec=pltpu.PrefetchScalarGridSpec(
+            num_scalar_prefetch=1,
+            grid=(4, heads),
+            in_specs=[pair, pair] + unit_specs(depth, slots),
+            out_specs=pl.BlockSpec((rows, model), lambda d, h, p: (0, 0)),
+        ),
+        **params(8 * rows * model * heads * UNIT, 8 * model * heads * UNIT),
+    )(places, dq, dkv, query, key, value, rest, rest, rest)
+
+
+def output_specs(own, rest):
+    _, slots, depth, width = rest.shape
+    return [
+        pl.BlockSpec(own.shape, lambda d, p: (0, 0)),
+        pl.BlockSpec((1, slots, depth, width), lambda d, p: (jnp.maximum(d - 1, 0), 0, 0, 0)),
+    ]
+
+
+def output_forward_body(place_ref, attended_ref, x_ref, own_ref, rest_ref, out_ref):
+    d = pl.program_id(0)
+    x = x_ref[...].astype(f32)
+
+    @pl.when(d == 0)
+    def _():
+        out_ref[...] = x + jnp.dot(attended_ref[...], own_ref[...], preferred_element_type=f32)
+
+    @pl.when(d > 0)
+    def _():
+        slots, depth = rest_ref.shape[1], rest_ref.shape[2]
+        value = x
+        for j in range(slots):
+            owner = place_ref[0] ^ j
+            part = attended_ref[:, pl.ds(pl.multiple_of(owner * depth, depth), depth)]
+            value = value + jnp.dot(part, rest_ref[0, j], preferred_element_type=f32)
+        out_ref[...] = value
+
+
+def output_forward(places, attended, x, own, rest):
+    rows, model = x.shape
+    width = own.shape[1]
+    tile = pl.BlockSpec((rows, width), lambda d, p: (0, p[1] ^ d))
+    return pl.pallas_call(
+        output_forward_body,
+        out_shape=jax.ShapeDtypeStruct((rows, model), f32),
+        grid_spec=pltpu.PrefetchScalarGridSpec(
+            num_scalar_prefetch=1,
+            grid=(4,),
+            in_specs=[pl.BlockSpec(attended.shape, lambda d, p: (0, 0)), tile]
+            + output_specs(own, rest),
+            out_specs=tile,
+        ),
+        **params(2 * rows * model * model, 2 * model * model),
+    )(places, attended, x, own, rest)
+
+
+def output_back_body(place_ref, db_ref, own_ref, rest_ref, out_ref, total):
+    d = pl.program_id(0)
+    db = db_ref[...]
+
+    @pl.when(d == 0)
+    def _():
+        total[...] = lax.dot_general(db, own_ref[...], OVER_COLUMNS, preferred_element_type=f32)
+
+    @pl.when(d > 0)
+    def _():
+        slots, depth = rest_ref.shape[1], rest_ref.shape[2]
+        for j in range(slots):
+            owner = place_ref[0] ^ j
+            cols = pl.ds(pl.multiple_of(owner * depth, depth), depth)
+            total[:, cols] += lax.dot_general(
+                db, rest_ref[0, j], OVER_COLUMNS, preferred_element_type=f32
+            )
+
+    @pl.when(d == pl.num_programs(0) - 1)
+    def _():
+        out_ref[...] = total[...].astype(bf16)
+
+
+def output_back(places, db, own, rest):
+    rows, model = db.shape
+    height, width = own.shape
+    return pl.pallas_call(
+        output_back_body,
+        out_shape=jax.ShapeDtypeStruct((rows, height), bf16),
+        grid_spec=pltpu.PrefetchScalarGridSpec(
+            num_scalar_prefetch=1,
+            grid=(4,),
+            in_specs=[pl.BlockSpec((rows, width), lambda d, p: (0, p[1] ^ d))]
+            + output_specs(own, rest),
+            out_specs=pl.BlockSpec((rows, height), lambda d, p: (0, 0)),
+            scratch_shapes=[pltpu.VMEM((rows, height), f32)],
+        ),
+        **params(2 * rows * model * height, 2 * model * height),
+    )(places, db, own, rest)
 
 
 def token_layout(length_row, block_slots, block_size):
@@ -400,11 +1293,6 @@
 
 def weight_grad_sum(left, right, me, count):
     depth = left.shape[1] // count
-    if count == 8:
-        sent = over_rows(column_blocks(left, 8, [me ^ j for j in (1, 3, 5, 7)]), right)
-        kept = over_rows(column_blocks(left, 8, [me ^ j for j in (0, 2, 4, 6)]), right)
-        both = add_rounded(kept.astype(bf16), swap(sent.astype(bf16), "ctx", 1))
-        return sum_planes([both[i * depth : (i + 1) * depth] for i in range(4)])
     full = over_rows(column_blocks(left, count, [me ^ j for j in range(count)]), right)
     return sum_halving(full.astype(bf16).reshape(count, depth, right.shape[1]), "ctx")
 
@@ -415,17 +1303,6 @@
     depth = hidden.shape[1] // bands
     width = grad.shape[1] // fsdp_count
     left = column_blocks(hidden, bands, [band ^ j for j in range(bands)])
-    if count == 8:
-        sent = over_rows(left, column_blocks(grad, 4, [column ^ 1, column ^ 3])).astype(bf16)
-        kept = over_rows(left, column_blocks(grad, 4, [column, column ^ 2])).astype(bf16)
-        both = add_rounded(kept, swap(sent, "ctx", 1))
-        return sum_planes(
-            [
-                both[r * depth : (r + 1) * depth, s * width : (s + 1) * width]
-                for r in range(2)
-                for s in range(2)
-            ]
-        )
     right = column_blocks(grad, fsdp_count, [column ^ j for j in range(fsdp_count)])
     full = over_rows(left, right).astype(bf16).reshape(bands, depth, fsdp_count, width)
     return sum_halving(full.transpose(0, 2, 1, 3).reshape(count, depth, width), "ctx")
@@ -447,6 +1324,24 @@
     mine = sum_halving(table, "ctx")
     mine = jnp.stack(by_place([mine[i] for i in range(fsdp_count)], place))
     return sum_halving(mine, "fsdp")
+
+
+def attention_layout(seq_lengths, block_perm, rows):
+    count, me = lax.axis_size("ctx"), lax.axis_index("ctx")
+    rounds = block_perm.shape[0] // count
+    blk = rows // rounds
+    plain_order, begins = token_layout(seq_lengths[0], block_perm, blk)
+    natural = lax.dynamic_slice_in_dim(plain_order, me * rows, rows)
+    begin = lax.dynamic_slice_in_dim(begins, me * rows, rows)
+    half_dim = HEAD_SIZE // 2
+    exponent = jnp.arange(half_dim, dtype=f32) * (2.0 / HEAD_SIZE)
+    inverse = rope_base ** (-exponent)
+    angles = (natural - begin).astype(f32)[:, None] * inverse[None, :]
+    cosine = jnp.concatenate([jnp.cos(angles)] * 2, 1)
+    sine = jnp.concatenate([-jnp.sin(angles), jnp.sin(angles)], 1)
+    order = plain_order.reshape(count, rounds, blk)
+    order = jnp.stack(by_place([order[i] for i in range(count)], me), 1)
+    return natural[:, None], begin[:, None], order.reshape(rounds, 1, count * blk), cosine, sine
 
 
 def on_device(
@@ -470,9 +1365,7 @@
     me, place = lax.axis_index("ctx"), lax.axis_index("fsdp")
     me_ref = me.astype(jnp.int32).reshape(1)
     depth = model // count
-    blocks = block_perm.shape[0]
-    rounds = blocks // count
-    blk = rows // rounds
+    zero = jnp.zeros((1,), jnp.int32)
     shard_heads = KEY_VALUE_HEADS // fsdp_count
 
     def own_rows(weight):
@@ -508,20 +1401,10 @@
     ]
     down_slots = gather_ctx(jnp.concatenate(by_place(down_rows, place), 1))
 
-    plain_order, begins = token_layout(seq_lengths[0], block_perm, blk)
-    first_row = me * rows
-    natural = lax.dynamic_slice_in_dim(plain_order, first_row, rows)
-    begin = lax.dynamic_slice_in_dim(begins, first_row, rows)
+    natural_column, begin_column, key_natural, cosine, sine = attention_layout(
+        seq_lengths, block_perm, rows
+    )
     half_dim = HEAD_SIZE // 2
-    exponent = jnp.arange(half_dim, dtype=f32) * (2.0 / HEAD_SIZE)
-    inverse = rope_base ** (-exponent)
-    angles = (natural - begin).astype(f32)[:, None] * inverse[None, :]
-    cosine = jnp.concatenate([jnp.cos(angles)] * 2, 1)
-    sine = jnp.concatenate([-jnp.sin(angles), jnp.sin(angles)], 1)
-    slot_order = plain_order.reshape(count, rounds, blk)
-    slot_order = jnp.stack(by_place([slot_order[i] for i in range(count)], me), 1)
-    key_natural = slot_order.reshape(rounds, 1, count * blk)
-    natural_column, begin_column = natural[:, None], begin[:, None]
 
     tokens = hidden_in.reshape(rows, model).astype(f32)
     scale_one = rms_scale(tokens)
@@ -532,7 +1415,7 @@
         rows, KEY_VALUE_HEADS * 2 * HEAD_SIZE
     )
     kv_slots = gather_ctx(kv_local)
-    attended, best = attend(natural_column, begin_column, key_natural, qkv, kv_slots)
+    attended, best = attend(zero, natural_column, begin_column, key_natural, qkv, kv_slots)
     head_max = jnp.max(best[:, :, :REPEAT, 0], 0).reshape(QUERY_HEADS)
     for mask in bits_down(count):
         head_max = jnp.maximum(head_max, swap(head_max, "ctx", mask))
@@ -573,16 +1456,9 @@
     grad_branch = grad_residual.astype(bf16)
     head_grad = slot_matmul_t(grad_branch, output_slots, me_ref, 512, bf16)
     query_grad, *dkv_slots = attend_back(
-        natural_column, begin_column, key_natural, cosine, sine, qkv, head_grad, kv_slots
-    )
-    if count == 8:
-        even = [
-            add_rounded(dkv_slots[j][0], swap(dkv_slots[j + 1][0], "ctx", 1))
-            for j in (0, 2, 4, 6)
-        ]
-        dkv = sum_planes(even)
-    else:
-        dkv = sum_halving(dkv_slots[0], "ctx")
+        zero, natural_column, begin_column, key_natural, cosine, sine, qkv, head_grad, kv_slots
+    )
+    dkv = sum_halving(dkv_slots[0], "ctx")
     dkv = dkv.reshape(rows, KEY_VALUE_HEADS, 2, HEAD_SIZE)
     grad_key = dkv[:, :, 0]
     first, second = grad_key[..., :half_dim], grad_key[..., half_dim:]
@@ -652,12 +1528,124 @@
     )
 
 
+def full_gains(first_gain, second_gain):
+    count, place = lax.axis_size("fsdp"), lax.axis_index("fsdp")
+    gains = jnp.stack([first_gain, second_gain])
+    parts = [gains] + [swap(gains, "fsdp", d) for d in range(1, count)]
+    gains = jnp.concatenate(by_place(parts, place), 1).astype(f32)
+    return gains[0], gains[1]
+
+
+def on_row_of_chips(
+    hidden_in,
+    out_grad,
+    seq_lengths,
+    block_perm,
+    first_gain,
+    query_weight,
+    key_matrix,
+    value_matrix,
+    output_weight,
+    second_gain,
+    gate_weight,
+    up_weight,
+    down_weight,
+    clip_limit,
+):
+    rows, model = hidden_in.shape[1], hidden_in.shape[2]
+    me, place = lax.axis_index("ctx"), lax.axis_index("fsdp")
+    places = jnp.stack([me, place]).astype(jnp.int32)
+    place_one = places[1:]
+    natural, begin, key_natural, cosine, sine = attention_layout(seq_lengths, block_perm, rows)
+    first_full, second_full = full_gains(first_gain, second_gain)
+    tokens_low = hidden_in.reshape(rows, model)
+    grad_out = out_grad.reshape(rows, model)
+
+    unit_rest, output_rest, down_rest = weight_gather(
+        query_weight, key_matrix, value_matrix, output_weight, down_weight
+    )
+    tokens = tokens_low.astype(f32)
+    scale_one = rms_scale(tokens)
+    unit_one = tokens * scale_one
+    normalized = (unit_one * first_full).astype(bf16)
+    qkv, kv_local = unit_forward(
+        places, normalized, cosine, sine, query_weight, key_matrix, value_matrix, unit_rest
+    )
+    kv_rest, dy_rest = kv_gather(kv_local, grad_out)
+    kv_slots = [kv_local[None], kv_rest]
+    attended, best = attend(place_one, natural, begin, key_natural, qkv, kv_slots)
+    head_max = jnp.max(best[:, :, :REPEAT, 0], 0).reshape(QUERY_HEADS)
+    for mask in (4, 2, 1):
+        head_max = jnp.maximum(head_max, swap(head_max, "ctx", mask))
+    for mask in (2, 1):
+        head_max = jnp.maximum(head_max, swap(head_max, "fsdp", mask))
+    residual = output_forward(places, attended, tokens_low, output_weight, output_rest)
+    scale_two = rms_scale(residual)
+    unit_two = residual * scale_two
+    normed_two = (unit_two * second_full).astype(bf16)
+
+    hid, dg, du, h_all, y_own, y_rest, grad_normed_two = feed_forward_row(
+        normed_two, grad_out, dy_rest, gate_weight, up_weight, down_weight, down_rest
+    )
+    second_term = jnp.sum(grad_normed_two * unit_two, 0)
+    grad_residual = grad_out.astype(f32) + norm_back(
+        grad_normed_two * second_full, unit_two, scale_two
+    )
+    grad_branch = grad_residual.astype(bf16)
+    gate_grad, up_grad, down_sum, y_land = grads_row(h_all, dg, du, hid, grad_out, dy_rest, y_rest)
+    result = (residual + y_own + jnp.sum(y_land.astype(f32), 0)).astype(bf16)
+    width = model // 4
+    moved = []
+    for k in range(4):
+        pairs = [
+            (c * 4 + f, (2 * f + c // 4) * 4 + (c % 4 ^ k)) for c in range(8) for f in range(4)
+        ]
+        piece = lax.dynamic_slice_in_dim(down_sum, ((me % 4) ^ k) * width, width, 1)
+        moved.append(lax.ppermute(piece, ("ctx", "fsdp"), pairs))
+    down_grad = jnp.concatenate(by_place(moved, place), 0).astype(f32)
+
+    head_grad = output_back(places, grad_branch, output_weight, output_rest)
+    query_grad, dkv_first, dkv_rest = attend_back(
+        place_one, natural, begin, key_natural, cosine, sine, qkv, head_grad, kv_slots
+    )
+    dkv = kv_sum(dkv_first, dkv_rest, cosine, sine)
+    grad_normed_one = unit_back(
+        places, query_grad, dkv, query_weight, key_matrix, value_matrix, unit_rest
+    )
+    first_term = jnp.sum(grad_normed_one * unit_one, 0)
+    grad_input = grad_residual + norm_back(grad_normed_one * first_full, unit_one, scale_one)
+    query_out, key_out, value_out, output_out = unit_grads(
+        normalized, query_grad, dkv, attended, grad_branch
+    )
+    first_out = gain_sum(first_term, me, place, 8, 4)
+    second_out = gain_sum(second_term, me, place, 8, 4)
+    multiplier = jnp.sqrt(clip_limit / jnp.maximum(head_max, clip_limit))
+    key_ratio = jnp.min(multiplier.reshape(KEY_VALUE_HEADS, REPEAT), 1)
+    return (
+        result.reshape(1, rows, model),
+        grad_input.astype(bf16).reshape(1, rows, model),
+        first_out,
+        query_out,
+        key_out,
+        value_out,
+        output_out,
+        second_out,
+        gate_grad,
+        up_grad,
+        down_grad,
+        head_max,
+        clipped(query_weight, multiplier),
+        clipped(key_matrix, key_ratio),
+    )
+
+
 def solution(mesh):
     shard, whole = P(None, "fsdp"), P()
     token, block = P("fsdp", "ctx", None), P("ctx", "fsdp")
     gain = P(("ctx", "fsdp"))
+    chips = mesh.shape["ctx"] == 8 and mesh.shape["fsdp"] == 4
     return jax.shard_map(
-        on_device,
+        on_row_of_chips if chips else on_device,
         mesh=mesh,
         in_specs=(token, token, P("fsdp", None), whole, P("fsdp"))
         + (shard,) * 4

time: 1150 us -> 903 us (0.79)
  Pallas kernels: 127 us -> 761 us
  waiting for transfers between devices: 577 us -> 21.5 us
  matrix products: 146 us -> 0 us
  starting transfers between devices: 113 us -> 40.6 us
  local copies, waits for them, and re-layouts: 98.2 us -> 27.8 us
  other arithmetic: 82.8 us -> 41.2 us
    pallas_call x14 -> x12, Pallas kernels: 127 us -> 761 us  [the longest x1 154 us: feed_forward_row(): remote_call(feed_forward_row_body, [wide, wide, wide, jax.ShapeDtypeStruc...]
    ppermute x122 -> x18, waiting for transfers between devices: 577 us -> 21.5 us  [swap(): return lax.ppermute(value, axis, [(i, i ^ mask) for i in range(size)])]
    dot_general x26 -> x0, matrix products: 146 us -> none  [the longest x10 60.6 us: over_rows(): lax.dot_general(left, right, (((0,), (0,)), ((), ())), preferred_element_...]
    ppermute x122 -> x18, starting transfers between devices: 112 us -> 32.2 us  [swap(): return lax.ppermute(value, axis, [(i, i ^ mask) for i in range(size)])]
    slice x22 -> x1, local copies, waits for them, and re-layouts: 26.6 us -> 0.01 us  [full_gains(): return (gains[0], gains[1])]
    concatenate x15 -> x2, other arithmetic: 20.2 us -> 0.2 us  [the longest x1 0.1 us: attention_layout(): cosine = jnp.concatenate([jnp.cos(angles)] * 2, 1)]
    convert_element_type x23 -> x6, other arithmetic: 23.3 us -> 4.59 us  [the longest x1 1.61 us: on_row_of_chips(): down_grad = jnp.concatenate(by_place(moved, place), 0).astype(f32)]
    unnamed x340 -> x98, local copies, waits for them, and re-layouts: 31.5 us -> 18.7 us
  transfers between devices with their start and end apart: 123 -> 22, of which waited for: 48 -> 12; matrix products, arithmetic and copies ran while one was open for 25% -> 4% of each run, Pallas kernels for 11% -> 15%
where the time goes in v2:
time: 903 us; the launch traced here: 894 us
  Pallas kernels  761 us (84%)
  other arithmetic  41.2 us (5%)
  starting transfers between devices  40.6 us (4%)
  local copies, waits for them, and re-layouts  27.8 us (3%)
  waiting for transfers between devices  21.5 us (2%)
    pallas_call x1, Pallas kernels, feed_forward_row(): remote_call(feed_forward_row_body, [wide, wide, wide, jax.ShapeDtypeStruc...  154 us
    pallas_call x1, Pallas kernels, unit_grads(): remote_call(unit_grads_body, [wide, half, half, wide], [VMEM] * 4, [VMEM]...  152 us
    pallas_call x1, Pallas kernels, weight_gather(): remote_call(weight_gather_body, outs, [ANY] * 3, [ANY] * 5, [], 15 + 9 *...  135 us
    pallas_call x1, Pallas kernels, grads_row(): remote_call(grads_body, [summed, summed, jax.ShapeDtypeStruct((depth, mod...  117 us
    pallas_call x1, Pallas kernels, kv_gather(): remote_call(kv_gather_body, [jax.ShapeDtypeStruct((7,) + kv.shape, bf16),...  78.6 us
    pallas_call x1, Pallas kernels, kv_sum(): remote_call(kv_sum_body, jax.ShapeDtypeStruct((rows, width), bf16), VMEM,...  42.4 us
    ppermute x18, starting transfers between devices, swap(): return lax.ppermute(value, axis, [(i, i ^ mask) for i in range(size)])  32.2 us
    pallas_call x1, Pallas kernels, attend_back(): pl.pallas_call(functools.partial(attend_back_body, len(slots)), out_shape...  24.2 us
  transfers between devices with their start and end apart: 22, of which 12 were waited for; matrix products, arithmetic and copies ran while one was open for 4% of the time, Pallas kernels for 15%

profile of v2, /device:TPU:0, one launch (start us, length us, event | category | flops | bytes accessed | tf_op | source)
XLA Modules:
  0.0 894.1 jit_solution(7983095738964705261)
XLA Ops:
  2.6 5.0 collective-permute-start
  18.4 135.2 %shard_map.245 = (bf16[3,8,256,1024]{3,2,1,0:T(8,128)(2,1)}, bf16[3,8,256,512]{3,2,1,0:T(8,128)(2,1)}, bf16[3,8,256,512]{3,2,1,0:T(8,128)(2,1)}) custom-call(bf16[2048,512]{1,0:T(8,128)(2,1)} %q_own.3, bf16[2048,256]{1,0:T(8,128)(2,1)} %k_own.3, bf16[2048,256]{1,0:T(8,128)(2,1)} %v_own.3, bf16[2048,512]{1,0:T(8,128)(2,1)} %own_ref.3, bf16[8192,512]{1,0:T(8,128)(2,1)} %down_own.1), custom_call_target="tpu_custom_call" | custom-call | bytes 4194304 | tf_op jit(solution)/shard_map/pallas_call | solution.py:492
  156.4 13.1 %shard_map.246 = (bf16[256,4096]{1,0:T(8,128)(2,1)}, bf16[256,2048]{1,0:T(8,128)(2,1)S(1)}) custom-call(s32[2]{0:T(128)S(1)} %pad_add_fusion.place_ref, bf16[256,2048]{1,0:T(8,128)(2,1)S(1)} %fusion.4.h_ref, f32[256,128]{1,0:T(8,128)S(1)} %pad_maximum_fusion.cosine_ref, f32[256,128]{1,0:T(8,128)S(1)} %pad_maximum_fusion.1.sine_ref, bf16[2048,512]{1,0:T(8,128)(2,1)} %q_own.3, ...), custom_call_target="tpu_custom_call" | custom-call | flops 4294967296 | bytes 16777216 | tf_op jit(solution)/shard_map/pallas_call | solution.py:1094
  170.5 78.6 %shard_map.247 = (bf16[7,256,2048]{2,1,0:T(8,128)(2,1)}, bf16[3,256,2048]{2,1,0:T(8,128)(2,1)}) custom-call(bf16[256,2048]{1,0:T(8,128)(2,1)} %copy-done.8, bf16[256,2048]{1,0:T(8,128)(2,1)} %bitcast.81), custom_call_target="tpu_custom_call" | custom-call | bytes 4194304 | tf_op jit(solution)/shard_map/pallas_call | solution.py:585
  250.7 16.4 %shard_map.248 = (bf16[256,2048]{1,0:T(8,128)(2,1)S(1)}, f32[2,8,8,128]{3,2,1,0:T(8,128)S(1)}) custom-call(s32[1]{0:T(128)} %bitcast.1.place_ref, s32[256,1]{1,0:T(8,128)S(1)} %copy.53.natural_ref, s32[256,1]{1,0:T(8,128)S(1)} %copy-done.20, s32[2,1,1024]{2,1,0:T(1,128)S(1)} %bitcast.79, bf16[256,4096]{1,0:T(8,128)(2,1)S(1)} %copy-done.13, ...), custom_call_target="tpu_custom_call" | custom-call | flops 2147483648 | bytes 12582912 | tf_op jit(solution)/shard_map/pallas_call | solution.py:302
  267.7 7.0 shard_map.249
  276.1 154.2 %shard_map.250 = (bf16[1024,2048]{1,0:T(8,128)(2,1)}, bf16[1024,2048]{1,0:T(8,128)(2,1)}, bf16[1024,2048]{1,0:T(8,128)(2,1)}, bf16[1024,2048]{1,0:T(8,128)(2,1)}...) custom-call(bf16[256,2048]{1,0:T(8,128)(2,1)} %multiply_convert_fusion.2.h_ref, ...), custom_call_target="tpu_custom_call" | custom-call | flops 51539607552 | bytes 4194304 | tf_op jit(solution)/shard_map/pallas_call | solution.py:725
  430.4 2.9 multiply_reduce_fusion
  434.9 6.8 shard_map.252.grad_ref
  442.7 24.2 %shard_map.253 = (bf16[256,2048]{1,0:T(8,128)(2,1)S(1)}, bf16[1,256,2048]{2,1,0:T(8,128)(2,1)S(1)}, bf16[7,256,2048]{2,1,0:T(8,128)(2,1)}) custom-call(s32[1]{0:T(128)} %bitcast.1.place_ref, s32[256,1]{1,0:T(8,128)S(1)} %copy.53.natural_ref, s32[256,1]{1,0:T(8,128)S(1)} %copy-done.21, s32[2,1,1024]{2,1,0:T(1,128)S(1)} %bitcast.80, ...), custom_call_target="tpu_custom_call" | custom-call | flops 5368709120 | bytes 20971520 | tf_op jit(solution)/shard_map/pallas_call | solution.py:326
  468.9 42.4 %shard_map.254.dkv_ref = bf16[256,2048]{1,0:T(8,128)(2,1)} custom-call(bf16[1,256,2048]{2,1,0:T(8,128)(2,1)} %copy-done.19, bf16[7,256,2048]{2,1,0:T(8,128)(2,1)} %get-tuple-element.61.rest_ref, f32[256,128]{1,0:T(8,128)} %copy-done.15, f32[256,128]{1,0:T(8,128)} %copy-done.14), custom_call_target="tpu_custom_call" | custom-call | bytes 4194304 | tf_op jit(solution)/shard_map/pallas_call | solution.py:941
  516.1 14.0 %shard_map.255 = f32[256,2048]{1,0:T(8,128)} custom-call(s32[2]{0:T(128)S(1)} %pad_add_fusion.place_ref, bf16[256,2048]{1,0:T(8,128)(2,1)S(1)} %copy-done.18, bf16[256,2048]{1,0:T(8,128)(2,1)S(1)} %copy-done.7, bf16[2048,512]{1,0:T(8,128)(2,1)} %q_own.3, bf16[2048,256]{1,0:T(8,128)(2,1)S(1)} %copy-done.3, bf16[2048,256]{1,0:T(8,128)(2,1)S(1)} %copy-done.6, ...), custom_call_target="tpu_custom_call" | custom-call | flops 4294967296 | bytes 16777216 | tf_op jit(solution)/shard_map/pallas_call | solution.py:1147
  530.1 152.3 %shard_map.256 = (f32[256,512]{1,0:T(8,128)}, f32[256,256]{1,0:T(8,128)}, f32[256,256]{1,0:T(8,128)}, f32[256,512]{1,0:T(8,128)}) custom-call(bf16[256,2048]{1,0:T(8,128)(2,1)} %copy-done.11, bf16[256,2048]{1,0:T(8,128)(2,1)} %copy-done.17, bf16[256,2048]{1,0:T(8,128)(2,1)} %shard_map.254.dkv_ref, bf16[256,2048]{1,0:T(8,128)(2,1)} %copy-done.16, ...), custom_call_target="tpu_custom_call" | custom-call | flops 6442450944 | bytes 4194304 | tf_op jit(solution)/shard_map/pallas_call | solution.py:1027
  682.5 2.3 fusion.10
  684.7 117.0 %shard_map.251 = (f32[256,2048]{1,0:T(8,128)}, f32[256,2048]{1,0:T(8,128)}, bf16[256,2048]{1,0:T(8,128)(2,1)}, bf16[3,256,2048]{2,1,0:T(8,128)(2,1)}) custom-call(bf16[1024,2048]{1,0:T(8,128)(2,1)} %get-tuple-element.52.h_ref, bf16[1024,2048]{1,0:T(8,128)(2,1)} %get-tuple-element.53.dg_ref, bf16[1024,2048]{1,0:T(8,128)(2,1)} %get-tuple-element.54.du_ref, ...), custom_call_target="tpu_custom_call" | custom-call | flops 25769803776 | bytes 4194304 | tf_op jit(solution)/shard_map/pallas_call | solution.py:891
  801.8 4.0 convert_reduce_fusion
  811.3 2.1 constant_dynamic-slice_fusion.1
  813.4 3.3 collective-permute-start.13
  816.8 2.3 collective-permute-start.14
  821.3 6.3 fusion.13
  827.6 2.1 collective-permute-start.18
  833.2 4.4 collective-permute-done.20
  837.5 4.5 collective-permute-start.21
  843.6 2.0 collective-permute-start.15
  846.9 3.4 multiply_convert_fusion
  853.2 5.5 collective-permute-start.4
  860.2 2.0 collective-permute-start.9
  867.8 2.9 collective-permute-done.6
  872.2 2.9 collective-permute-done.11
  875.1 3.5 collective-permute-start.7
  880.1 2.0 collective-permute-start.12
  885.3 1.6 maximum_convert_fusion
  (221 shorter events, 66.2 us)
Async XLA Ops:
  2.6 151.9 %collective-permute-start = (bf16[2,512]{1,0:T(2,128)(2,1)}, bf16[2,512]{1,0:T(2,128)(2,1)}, u32[]{:S(2)}, u32[]{:S(2)}) collective-permute-start(bf16[2,512]{1,0:T(2,128)(2,1)} %pad_maximum_fusion.4), channel_id=1, source_target_pairs={{0,3},{1,2},{2,1},{3,0},{4,7},{5,6},{6,5},{7,4},{8,11},{9,10},{10,... | collective-permute-start | bytes 6152 | tf_op jit(solution)/shard_map/ppermute | solution.py:27
  7.6 146.9 %collective-permute-start.1 = (bf16[2,512]{1,0:T(2,128)(2,1)}, bf16[2,512]{1,0:T(2,128)(2,1)}, u32[]{:S(2)}, u32[]{:S(2)}) collective-permute-start(bf16[2,512]{1,0:T(2,128)(2,1)} %pad_maximum_fusion.4), channel_id=1, source_target_pairs={{0,2},{1,3},{2,0},{3,1},{4,6},{5,7},{6,4},{7,5},{8,10},{9,11},{10,... | collective-permute-start | bytes 6152 | tf_op jit(solution)/shard_map/ppermute | solution.py:27
  7.7 146.9 %collective-permute-start.2 = (bf16[2,512]{1,0:T(2,128)(2,1)}, bf16[2,512]{1,0:T(2,128)(2,1)}, u32[]{:S(2)}, u32[]{:S(2)}) collective-permute-start(bf16[2,512]{1,0:T(2,128)(2,1)} %pad_maximum_fusion.4), channel_id=1, source_target_pairs={{0,1},{1,0},{2,3},{3,2},{4,5},{5,4},{6,7},{7,6},{8,9},{9,8},{10,11... | collective-permute-start | bytes 6152 | tf_op jit(solution)/shard_map/ppermute | solution.py:27
  12.1 429.6 %copy-start.15 = (f32[256,128]{1,0:T(8,128)}, f32[256,128]{1,0:T(8,128)S(1)}, u32[]{:S(2)}) copy-start(f32[256,128]{1,0:T(8,128)S(1)} %pad_maximum_fusion.cosine_ref) | copy-start | bytes 393220
  15.6 426.1 %copy-start.14 = (f32[256,128]{1,0:T(8,128)}, f32[256,128]{1,0:T(8,128)S(1)}, u32[]{:S(2)}) copy-start(f32[256,128]{1,0:T(8,128)S(1)} %pad_maximum_fusion.1.sine_ref) | copy-start | bytes 393220
  18.4 136.9 %copy-start = (bf16[1,256,2048]{2,1,0:T(8,128)(2,1)S(1)}, bf16[1,256,2048]{2,1,0:T(8,128)(2,1)}, u32[]{:S(2)}) copy-start(bf16[1,256,2048]{2,1,0:T(8,128)(2,1)} %param.14) | copy-start | bytes 3145732
  155.3 278.0 %copy-start.31 = (f32[1,2048]{1,0:T(1,128)}, f32[1,2048]{1,0:T(1,128)S(1)}, u32[]{:S(2)}) copy-start(f32[1,2048]{1,0:T(1,128)S(1)} %get-tuple-element.119) | copy-start | bytes 24580
  155.3 527.1 %copy-start.33 = (f32[1,2048]{1,0:T(1,128)}, f32[1,2048]{1,0:T(1,128)S(1)}, u32[]{:S(2)}) copy-start(f32[1,2048]{1,0:T(1,128)S(1)} %get-tuple-element.120) | copy-start | bytes 24580
  170.5 78.6 %copy-start.20 = (s32[256,1]{1,0:T(8,128)S(1)}, s32[256,1]{1,0:T(8,128)}, u32[]{:S(2)}) copy-start(s32[256,1]{1,0:T(8,128)} %copy.54.start_ref) | copy-start | bytes 3076
  170.5 78.6 %copy-start.9 = (bf16[256,2048]{1,0:T(8,128)(2,1)S(1)}, bf16[256,2048]{1,0:T(8,128)(2,1)}, u32[]{:S(2)}) copy-start(bf16[256,2048]{1,0:T(8,128)(2,1)} %copy-done.8) | copy-start | bytes 3145732
  530.1 152.3 %copy-start.37 = (f32[256]{0:T(256)S(1)}, f32[256]{0:T(256)}, u32[]{:S(2)}) copy-start(f32[256]{0:T(256)} %add_rsqrt_fusion.1) | copy-start | bytes 3076
  805.8 15.4 %copy-start.39 = (f32[256]{0:T(256)S(1)}, f32[256]{0:T(256)}, u32[]{:S(2)}) copy-start(f32[256]{0:T(256)} %copy-done.38) | copy-start | bytes 3076
  806.8 45.0 %collective-permute-start.3 = (f32[4,4,64]{2,1,0:T(4,128)}, f32[4,4,64]{2,1,0:T(4,128)}, u32[]{:S(2)}, u32[]{:S(2)}) collective-permute-start(f32[4,4,64]{2,1,0:T(4,128)} %pad_maximum_fusion.2), channel_id=1, source_target_pairs={{0,16},{4,20},{8,24},{12,28},{16,0},{20,4},{24,8},{28,12},{1,17},{... | collective-permute-start | bytes 12296 | tf_op jit(solution)/shard_map/ppermute | solution.py:27
  813.4 70.7 %collective-permute-start.13 = (bf16[256,512]{1,0:T(8,128)(2,1)}, bf16[256,512]{1,0:T(8,128)(2,1)}, u32[]{:S(2)}, u32[]{:S(2)}) collective-permute-start(bf16[256,512]{1,0:T(8,128)(2,1)} %get-tuple-element.118), channel_id=1, source_target_pairs={{0,3},{1,11},{2,19},{3,27},{4,2},{5,10},{6,18},{7,26},{8,1},{9,9},... | collective-permute-start | bytes 786440 | tf_op jit(solution)/shard_map/ppermute | solution.py:1604
  816.8 67.4 %collective-permute-start.14 = (bf16[256,512]{1,0:T(8,128)(2,1)}, bf16[256,512]{1,0:T(8,128)(2,1)}, u32[]{:S(2)}, u32[]{:S(2)}) collective-permute-start(bf16[256,512]{1,0:T(8,128)(2,1)} %get-tuple-element.117), channel_id=1, source_target_pairs={{0,2},{1,10},{2,18},{3,26},{4,3},{5,11},{6,19},{7,27},{8,0},{9,8},... | collective-permute-start | bytes 786440 | tf_op jit(solution)/shard_map/ppermute | solution.py:1604
  820.1 7.6 collective-permute-start.17
  821.3 25.6 %copy-start.44 = (s32[512]{0:T(512)S(1)}, s32[512]{0:T(512)}, u32[]{:S(2)}) copy-start(s32[512]{0:T(512)} %add_select_fusion.2) | copy-start | bytes 6148
  827.6 3.6 collective-permute-start.18
  829.7 23.5 %collective-permute-start.8 = (f32[4,4,64]{2,1,0:T(4,128)S(1)}, f32[4,4,64]{2,1,0:T(4,128)S(1)}, u32[]{:S(2)}, u32[]{:S(2)}) collective-permute-start(f32[4,4,64]{2,1,0:T(4,128)S(1)} %pad_maximum_fusion.3), channel_id=1, source_target_pairs={{0,16},{4,20},{8,24},{12,28},{16,0},{20,4},{24,8},{28,12},{1,17},{... | collective-permute-start | bytes 12296 | tf_op jit(solution)/shard_map/ppermute | solution.py:27
  831.2 1.9 collective-permute-start.19
  833.1 4.4 collective-permute-start.20
  837.5 6.1 collective-permute-start.21
  843.6 40.6 %collective-permute-start.15 = (bf16[256,512]{1,0:T(8,128)(2,1)}, bf16[256,512]{1,0:T(8,128)(2,1)S(1)}, u32[]{:S(2)}, u32[]{:S(2)}) collective-permute-start(bf16[256,512]{1,0:T(8,128)(2,1)} %get-tuple-element.115), channel_id=1, source_target_pairs={{0,1},{1,9},{2,17},{3,25},{4,0},{5,8},{6,16},{7,24},{8,3},{9,11},{... | collective-permute-start | bytes 786440 | tf_op jit(solution)/shard_map/ppermute | solution.py:1604
  851.8 32.4 %collective-permute-start.16 = (bf16[256,512]{1,0:T(8,128)(2,1)S(1)}, bf16[256,512]{1,0:T(8,128)(2,1)S(1)}, u32[]{:S(2)}, u32[]{:S(2)}) collective-permute-start(bf16[256,512]{1,0:T(8,128)(2,1)S(1)} %get-tuple-element.116), channel_id=1, source_target_pairs={{0,0},{1,8},{2,16},{3,24},{4,1},{5,9},{6,17},{7,25},{8,2},{9,10},{... | collective-permute-start | bytes 786440 | tf_op jit(solution)/shard_map/ppermute | solution.py:1604
  853.2 7.1 collective-permute-start.4
  860.2 3.6 collective-permute-start.9
  863.8 1.2 collective-permute-start.5
  865.0 1.2 collective-permute-start.10
  866.2 4.5 collective-permute-start.6
  870.6 4.5 collective-permute-start.11
  875.1 5.0 collective-permute-start.7
  880.1 3.5 collective-permute-start.12
  (36 other events, 145.6 us)

commit v3 on v2

--- a/solution.py
+++ b/solution.py
@@ -192,7 +192,7 @@
 def keys_of(slot_refs):
     def column(i):
         parts = [
-            r[:, :, i * HEAD_SIZE : (i + 1) * HEAD_SIZE].reshape(-1, HEAD_SIZE)
+            r[..., i * HEAD_SIZE : (i + 1) * HEAD_SIZE].reshape(-1, HEAD_SIZE)
             for r in slot_refs
         ]
         return parts[0] if len(parts) == 1 else jnp.concatenate(parts, 0)
@@ -217,7 +217,7 @@
     scores = jnp.where(allowed, scores, hidden_fill_value)
     best = jnp.max(scores, 1, keepdims=True)
     exps = jnp.exp(scores - best)
-    return query, exps / jnp.sum(exps, 1, keepdims=True), best, blk
+    return query, exps * (1.0 / jnp.sum(exps, 1, keepdims=True)), best, blk
 
 
 def attend_body(n_slots, place_ref, natural_ref, start_ref, key_natural_ref, qkv_ref, *refs):
@@ -269,7 +269,7 @@
     both = jnp.concatenate([key_grad, value_grad], 1)
     first = 0
     for ref in dkv_refs:
-        rows = ref.shape[0] * ref.shape[1]
+        rows = math.prod(ref.shape[:-1])
         ref[...] = both[first : first + rows].reshape(ref.shape)
         first += rows
 
@@ -287,6 +287,11 @@
         pl.BlockSpec((1, 1, 8, 128), lambda r, h, p: own_place(r, h, p) + (0, 0)),
         [
             pl.BlockSpec((s.shape[0], blk, 2 * HEAD_SIZE), lambda r, h, p: (0, r, h))
+            if s.ndim == 3
+            else pl.BlockSpec(
+                (1, s.shape[1], blk, 2 * HEAD_SIZE),
+                lambda r, h, p: (h // shard_heads, 0, r, h % shard_heads),
+            )
             for s in slots
         ],
     )
@@ -440,60 +445,6 @@
             copy.wait_recv()
 
 
-def run_gathers(gathers):
-    for k in range(len(gathers) + 2):
-        if k < len(gathers):
-            for over in gathers[k][0]:
-                over.wait_recv()
-            gathers[k][1].begin()
-        if 0 <= k - 1 < len(gathers):
-            gathers[k - 1][1].middle()
-        if 0 <= k - 2 < len(gathers):
-            gathers[k - 2][1].end()
-    for _, gather in gathers:
-        gather.ready()
-
-
-def weight_gather_body(
-    query_ref, key_ref, value_ref, output_ref, down_ref, unit_out, output_out, down_out, send, recv
-):
-    me, place = lax.axis_index("ctx"), lax.axis_index("fsdp")
-    depth = unit_out.shape[2]
-    own = pl.ds(pl.multiple_of(me * depth, depth), depth)
-    greet((1, 2, 4), (1, 2, 3))
-    t = Transfers(send, recv)
-    gathers = []
-    for d in (1, 2, 3):
-        first, overs = 0, []
-        for ref in (query_ref, key_ref, value_ref):
-            width = ref.shape[1]
-            overs.append(
-                t.start(ref.at[own], unit_out.at[d - 1, 0, :, first : first + width], fsdp=d)
-            )
-            first += width
-        gathers.append((overs, PlaneGather(t, [unit_out.at[d - 1, j] for j in range(8)])))
-    for d in (1, 2, 3):
-        over = t.start(output_ref.at[own], output_out.at[d - 1, 0], fsdp=d)
-        gathers.append(([over], PlaneGather(t, [output_out.at[d - 1, j] for j in range(8)])))
-    for d in (1, 2, 3):
-        row = flip(place, d) * 8 * depth + me * depth
-        over = t.start(
-            down_ref.at[pl.ds(pl.multiple_of(row, depth), depth)], down_out.at[d - 1, 0], fsdp=d
-        )
-        gathers.append(([over], PlaneGather(t, [down_out.at[d - 1, j] for j in range(8)])))
-    run_gathers(gathers)
-    t.finish()
-
-
-def weight_gather(query, key, value, output, down):
-    depth = query.shape[0] // 8
-    widths = (query.shape[1] + key.shape[1] + value.shape[1], output.shape[1], down.shape[1])
-    outs = [jax.ShapeDtypeStruct((3, 8, depth, w), bf16) for w in widths]
-    return remote_call(weight_gather_body, outs, [ANY] * 3, [ANY] * 5, [], 15 + 9 * 8, 0)(
-        query, key, value, output, down
-    )
-
-
 class RowGather:
     def __init__(self, own, slots, send, recv):
         self.own, self.slots, self.send, self.recv = own, slots, send, recv
@@ -564,33 +515,320 @@
             self.second_on().wait_send()
 
 
-def kv_gather_body(kv_ref, dy_ref, kv_out, dy_out, row_send, row_recv, send, recv):
-    greet((1, 2, 4), (1, 3))
+def probabilities(query, keys, allowed):
+    scores = lax.dot_general(query, keys, OVER_COLUMNS, preferred_element_type=f32) * SCALE
+    scores = jnp.where(allowed, scores, hidden_fill_value)
+    best = jnp.max(scores, 1, keepdims=True)
+    exps = jnp.exp(scores - best)
+    return exps * (1.0 / jnp.sum(exps, 1, keepdims=True)), best
+
+
+def stacked_heads(value):
+    return jnp.concatenate(
+        [value[:, i * HEAD_SIZE : (i + 1) * HEAD_SIZE] for i in range(REPEAT)], 0
+    )
+
+
+def attention_row_body(
+    x_ref, gain_ref, cosine_ref, sine_ref, natural_ref, begin_ref, key_natural_ref,
+    q_ref, k_ref, v_ref, o_ref, down_ref, dy_ref,
+    h_out, qkv_out, attended_out, best_out, residual_out, h2_out, gain_out,
+    kv_out, unit_out, output_out, down_out, dy_out,
+    q_own, k_own, v_own, o_own, units, outputs, kvs, h_rel,
+    own_sem, keep_sem, gain_send, gain_recv, row_send, row_recv, send, recv,
+):
+    me, place = lax.axis_index("ctx"), lax.axis_index("fsdp")
+    rows, model = x_ref.shape
+    depth = units.shape[2]
+    rounds = key_natural_ref.shape[0]
+    blk = rows // rounds
+    heads = q_ref.shape[1] // (REPEAT * HEAD_SIZE)
+    width = o_ref.shape[1]
+    own = pl.ds(pl.multiple_of(me * depth, depth), depth)
+    loads = [
+        pltpu.make_async_copy(src, dst, own_sem.at[i])
+        for i, (src, dst) in enumerate(
+            ((q_ref, q_own), (k_ref, k_own), (v_ref, v_own), (o_ref, o_own))
+        )
+    ]
+    for load in loads:
+        load.start()
+    gain_out[0] = gain_ref[...]
+    greet((1, 2, 4), (1, 2, 3))
+    gains = Transfers(gain_send, gain_recv)
+    gain_copies = [gains.start(gain_ref, gain_out.at[d], fsdp=d) for d in (1, 2, 3)]
     t = Transfers(send, recv)
-    gather = PlaneGather(t, [kv_ref] + [kv_out.at[j] for j in range(7)])
-    row = RowGather(dy_ref, [None] + [dy_out.at[d] for d in range(3)], row_send, row_recv)
-    gather.begin()
-    row.begin()
-    gather.middle()
-    row.first()
-    gather.end()
-    gather.ready()
-    row.second()
-    row.third()
-    row.finish()
+    unit_rows, first = [], 0
+    for i, ref in enumerate((q_ref, k_ref, v_ref)):
+        cols = slice(first, first + ref.shape[1])
+        first += ref.shape[1]
+        unit_rows.append(
+            RowGather(
+                ref.at[own],
+                [None] + [units.at[d, 0, :, cols] for d in range(3)],
+                row_send.at[i],
+                row_recv.at[i],
+            )
+        )
+    output_row = RowGather(
+        o_ref.at[own], [None] + [outputs.at[d, 0] for d in range(3)], row_send.at[3], row_recv.at[3]
+    )
+    dy_row = RowGather(
+        dy_ref, [None] + [dy_out.at[d] for d in range(3)], row_send.at[4], row_recv.at[4]
+    )
+    unit_plane = [None] + [
+        PlaneGather(t, [units.at[d, j] for j in range(8)]) for d in range(3)
+    ]
+    output_plane = [None] + [
+        PlaneGather(t, [outputs.at[d, j] for j in range(8)]) for d in range(3)
+    ]
+    down_plane = [None] + [
+        PlaneGather(t, [down_out.at[d, j] for j in range(8)]) for d in range(3)
+    ]
+    kv_plane = [PlaneGather(t, [kvs.at[d, j] for j in range(8)]) for d in range(4)]
+    for row in unit_rows:
+        row.begin()
+
+    x = x_ref[...].astype(f32)
+    unit = x * lax.rsqrt(jnp.mean(x * x, 1, keepdims=True) + epsilon)
+    for copy in gain_copies:
+        copy.wait_recv()
+    for d in range(4):
+        gain_cols = pl.ds(pl.multiple_of(flip(place, d) * width, width), width)
+        residual_out[:, gain_cols] = jnp.broadcast_to(gain_out[d, 0:1], (rows, width))
+    h_out[...] = (unit * residual_out[...]).astype(bf16)
+    for j in range(8):
+        block = pl.ds(pl.multiple_of(flip(me, j) * depth, depth), depth)
+        h_rel[:, j * depth : (j + 1) * depth] = h_out[:, block]
+    cosine, sine = cosine_ref[...], sine_ref[...]
+
+    def project(d):
+        if d == 0:
+            h = h_out[...]
+            parts = [
+                jnp.dot(h, w[...], preferred_element_type=f32) for w in (q_own, k_own, v_own)
+            ]
+            total = jnp.concatenate(parts, 1)
+        else:
+            weight = units[d - 1].reshape(model, units.shape[3])
+            total = jnp.dot(h_rel[...], weight, preferred_element_type=f32)
+
+        def head(i):
+            return total[:, i * HEAD_SIZE : (i + 1) * HEAD_SIZE]
+
+        for h in range(heads):
+            query = [
+                rotate(head(REPEAT * h + i), cosine, sine).astype(bf16) for i in range(REPEAT)
+            ]
+            key = rotate(head(REPEAT * heads + h), cosine, sine).astype(bf16)
+            value = head((REPEAT + 1) * heads + h).astype(bf16)
+            first = (d * heads + h) * UNIT
+            qkv_out[:, first : first + UNIT] = jnp.concatenate(query + [key, value], 1)
+            first = h * 2 * HEAD_SIZE
+            kvs[d, 0, :, first : first + 2 * HEAD_SIZE] = jnp.concatenate([key, value], 1)
+
+    def attend_heads(d):
+        def step(i, carry):
+            r, h = lax.div(i, heads), lax.rem(i, heads)
+            here = pl.ds(pl.multiple_of(r * blk, blk), blk)
+            first = pl.multiple_of(d * heads * UNIT + h * UNIT, UNIT)
+            query = stacked_heads(qkv_out[here, pl.ds(first, REPEAT * HEAD_SIZE)])
+            cols = pl.ds(pl.multiple_of(h * 2 * HEAD_SIZE, 2 * HEAD_SIZE), 2 * HEAD_SIZE)
+            both = kvs[d, :, here, cols].reshape(8 * blk, 2 * HEAD_SIZE)
+            natural = key_natural_ref[r]
+            allowed = (natural >= begin_ref[here]) & (natural <= natural_ref[here])
+            allowed = jnp.concatenate([allowed] * REPEAT, 0)
+            probs, best = probabilities(query, both[:, :HEAD_SIZE], allowed)
+            out = jnp.dot(probs.astype(bf16), both[:, HEAD_SIZE:], preferred_element_type=f32)
+            spot = flip(place, d) * heads + h
+            cols = pl.ds(pl.multiple_of(spot * REPEAT * HEAD_SIZE, REPEAT * HEAD_SIZE), REPEAT * HEAD_SIZE)
+            attended_out[here, cols] = jnp.concatenate(
+                [out[i * blk : (i + 1) * blk] for i in range(REPEAT)], 1
+            ).astype(bf16)
+            tops = [
+                jnp.broadcast_to(jnp.max(best[i * blk : (i + 1) * blk], 0, keepdims=True), (1, 128))
+                for i in range(REPEAT)
+            ]
+            best_out[r, spot] = jnp.concatenate(tops + [jnp.zeros((8 - REPEAT, 128), f32)], 0)
+            return carry
+
+        lax.fori_loop(0, rounds * heads, step, 0)
+
+    keeps = []
+
+    def keep(src, dst):
+        copy = pltpu.make_async_copy(src, dst, keep_sem.at[len(keeps)])
+        copy.start()
+        keeps.append(copy)
+
+    for load in loads[:3]:
+        load.wait()
+    project(0)
+    kv_plane[0].begin()
+    for row in unit_rows:
+        row.first()
+    unit_plane[1].begin()
+    output_row.begin()
+    kv_plane[0].middle()
+    for row in unit_rows:
+        row.second()
+    unit_plane[2].begin()
+    unit_plane[1].middle()
+    kv_plane[0].end()
+    output_row.first()
+    for row in unit_rows:
+        row.third()
+    unit_plane[3].begin()
+    downs = []
+    for d in (1, 2, 3):
+        row = flip(place, d) * 8 * depth + me * depth
+        downs.append(
+            t.start(
+                down_ref.at[pl.ds(pl.multiple_of(row, depth), depth)], down_out.at[d - 1, 0], fsdp=d
+            )
+        )
+    dy_row.begin()
+    unit_plane[2].middle()
+    unit_plane[1].end()
+    output_row.second()
+    unit_plane[1].ready()
+    project(1)
+    kv_plane[1].begin()
+    unit_plane[3].middle()
+    unit_plane[2].end()
+    output_row.third()
+    unit_plane[2].ready()
+    project(2)
+    kv_plane[2].begin()
+    kv_plane[1].middle()
+    unit_plane[3].end()
+    kv_plane[0].ready()
+    attend_heads(0)
+    unit_plane[3].ready()
+    project(3)
+    kv_plane[3].begin()
+    kv_plane[2].middle()
+    kv_plane[1].end()
+    output_plane[1].begin()
+    dy_row.first()
+    kv_plane[3].middle()
+    kv_plane[2].end()
+    output_plane[2].begin()
+    kv_plane[1].ready()
+    attend_heads(1)
+    output_plane[1].middle()
+    kv_plane[3].end()
+    output_plane[3].begin()
+    kv_plane[2].ready()
+    attend_heads(2)
+    output_plane[2].middle()
+    output_plane[1].end()
+    downs[0].wait_recv()
+    down_plane[1].begin()
+    dy_row.second()
+    kv_plane[3].ready()
+    attend_heads(3)
+    output_plane[3].middle()
+    output_plane[2].end()
+    downs[1].wait_recv()
+    down_plane[2].begin()
+    output_plane[3].end()
+    for j in range(8):
+        block = pl.ds(pl.multiple_of(flip(me, j) * depth, depth), depth)
+        h_rel[:, j * depth : (j + 1) * depth] = attended_out[:, block]
+    downs[2].wait_recv()
+    down_plane[3].begin()
+    for d in range(3):
+        keep(units.at[d], unit_out.at[d])
+    for d in range(4):
+        keep(kvs.at[d], kv_out.at[d])
+    loads[3].wait()
+    square = None
+    for d in range(4):
+        cols = pl.ds(pl.multiple_of(flip(place, d) * width, width), width)
+        if d == 0:
+            term = jnp.dot(attended_out[...], o_own[...], preferred_element_type=f32)
+        else:
+            output_plane[d].ready()
+            weight = outputs[d - 1].reshape(model, width)
+            term = jnp.dot(h_rel[...], weight, preferred_element_type=f32)
+        value = x_ref[:, cols].astype(f32) + term
+        residual_out[:, cols] = value
+        part = jnp.sum(value * value, 1, keepdims=True)
+        square = part if square is None else square + part
+        if d == 1:
+            down_plane[1].middle()
+    scale = lax.rsqrt(square * (1.0 / model) + epsilon)
+    for d in range(4):
+        cols = pl.ds(pl.multiple_of(flip(place, d) * width, width), width)
+        h2_out[:, cols] = (residual_out[:, cols] * scale * gain_out[d, 1:2]).astype(bf16)
+    for d in range(3):
+        keep(outputs.at[d], output_out.at[d])
+    down_plane[2].middle()
+    down_plane[1].end()
+    down_plane[3].middle()
+    down_plane[2].end()
+    down_plane[3].end()
+    dy_row.third()
+    for d in (1, 2, 3):
+        down_plane[d].ready()
+    for copy in keeps:
+        copy.wait()
+    for row in unit_rows + [output_row, dy_row]:
+        row.finish()
+    gains.finish()
     t.finish()
 
 
-def kv_gather(kv, dy):
+def attention_row(x, gains, cosine, sine, natural, begin, key_natural, query, key, value, output, down, dy):
+    rows, model = x.shape
+    depth = model // 8
+    width = query.shape[1] + key.shape[1] + value.shape[1]
+    kv_width = key.shape[1] + value.shape[1]
+    rounds = key_natural.shape[0]
+    dma = pltpu.SemaphoreType.DMA
+
+    def out(shape, dtype=bf16):
+        return jax.ShapeDtypeStruct(shape, dtype)
+
     return remote_call(
-        kv_gather_body,
-        [jax.ShapeDtypeStruct((7,) + kv.shape, bf16), jax.ShapeDtypeStruct((3,) + dy.shape, bf16)],
-        [ANY] * 2,
-        [ANY] * 2,
-        [pltpu.SemaphoreType.DMA((5,)), pltpu.SemaphoreType.DMA((3,))],
-        8,
-        1,
-    )(kv, dy)
+        attention_row_body,
+        [
+            out((rows, model)),
+            out((rows, 4 * width)),
+            out((rows, model)),
+            out((rounds, KEY_VALUE_HEADS, 8, 128), f32),
+            out((rows, model), f32),
+            out((rows, model)),
+            out((4,) + gains.shape, f32),
+            out((4, 8, rows, kv_width)),
+            out((3, 8, depth, width)),
+            out((3, 8, depth, output.shape[1])),
+            out((3, 8, depth, down.shape[1])),
+            out((3,) + dy.shape),
+        ],
+        [VMEM] * 7 + [ANY] * 5,
+        [VMEM] * 7 + [ANY] * 6,
+        [
+            pltpu.VMEM(query.shape, bf16),
+            pltpu.VMEM(key.shape, bf16),
+            pltpu.VMEM(value.shape, bf16),
+            pltpu.VMEM(output.shape, bf16),
+            pltpu.VMEM((3, 8, depth, width), bf16),
+            pltpu.VMEM((3, 8, depth, output.shape[1]), bf16),
+            pltpu.VMEM((4, 8, rows, kv_width), bf16),
+            pltpu.VMEM((rows, model), bf16),
+            dma((4,)),
+            dma((10,)),
+            dma((3,)),
+            dma((3,)),
+            dma((5, 5)),
+            dma((5, 3)),
+        ],
+        3 + 13 * 8,
+        0,
+        flops=10 * rows * model * model,
+    )(x, gains, cosine, sine, natural, begin, key_natural, query, key, value, output, down, dy)
 
 
 TILE = 256
@@ -606,29 +844,35 @@
     tiles = gates.shape[0]
     me, place = lax.axis_index("ctx"), lax.axis_index("fsdp")
     width = down_own.shape[1]
-    loads = []
-    for i in range(tiles):
-        cols = pl.ds(i * TILE, TILE)
-        loads.append(pltpu.make_async_copy(gate_ref.at[:, cols], gates.at[i], load_sem.at[0, i]))
-        loads.append(pltpu.make_async_copy(up_ref.at[:, cols], ups.at[i], load_sem.at[1, i]))
-    for j in range(tiles):
-        block = flip(me, j)
-        own_rows = pl.ds(pl.multiple_of(place * tiles * TILE + block * TILE, TILE), TILE)
+
+    def tile_loads(i, slot):
+        cols = pl.ds(pl.multiple_of(i * TILE, TILE), TILE)
+        copies = [
+            pltpu.make_async_copy(gate_ref.at[:, cols], gates.at[i], load_sem.at[0, i]),
+            pltpu.make_async_copy(up_ref.at[:, cols], ups.at[i], load_sem.at[1, i]),
+        ]
+        own_rows = pl.ds(pl.multiple_of(place * tiles * TILE + i * TILE, TILE), TILE)
         for d in range(4):
             cols = pl.ds(pl.multiple_of(flip(place, d) * width, width), width)
-            src = down_own.at[own_rows] if d == 0 else down_rest.at[d - 1, j]
-            loads.append(pltpu.make_async_copy(src, downs.at[block, :, cols], down_sem.at[j, d]))
-    for d in range(4):
-        src = dy_ref if d == 0 else dy_rest.at[d - 1]
-        loads.append(pltpu.make_async_copy(src, dys.at[d], dy_sem.at[d]))
-    for load in loads:
+            src = down_own.at[own_rows] if d == 0 else down_rest.at[d - 1, slot]
+            copies.append(pltpu.make_async_copy(src, downs.at[i, :, cols], down_sem.at[i, d]))
+        return copies
+
+    dy_copies = [
+        pltpu.make_async_copy(dy_ref if d == 0 else dy_rest.at[d - 1], dys.at[d], dy_sem.at[d])
+        for d in range(4)
+    ]
+    dy_copies[0].start()
+    for i in range(tiles):
+        for load in tile_loads(i, flip(me, i)):
+            load.start()
+    for load in dy_copies[1:]:
         load.start()
     greet((), (1, 2, 3))
     t = Transfers(send, recv)
     row = RowGather(h_ref, [None] + [hs.at[d] for d in range(3)], row_send, row_recv)
     row.begin()
-    for load in loads:
-        load.wait()
+    dy_copies[0].wait()
 
     def stage_copy(slot, k, part, i):
         out = (hid_out, dg_out, du_out)[k]
@@ -640,6 +884,9 @@
     def chunk(part, h):
         def step(i, carry):
             slot = lax.rem(i, 2)
+            if part == 0:
+                for load in tile_loads(i, 0):
+                    load.wait()
             gate, up, down = gates[i], ups[i], downs[i]
             g = jnp.dot(h[...], gate, preferred_element_type=f32)
             u = jnp.dot(h[...], up, preferred_element_type=f32)
@@ -697,6 +944,7 @@
         if part == 3:
             row.third()
         keep_h(part, h).start()
+        dy_copies[part].wait()
         chunk(part, h)
         back_send[part - 1] = back_acc[...].astype(bf16)
         backs.append(t.start(back_send.at[part - 1], back_land.at[part - 1], fsdp=part))
@@ -756,6 +1004,31 @@
     )(h, dy, dy_rest, gate, up, down_own, down_rest)
 
 
+class SmallReduce:
+    MASKS = ((0, 1), (0, 2), (2, 0), (4, 0), (1, 0))
+
+    def __init__(self, transfers, blocks, land, join):
+        self.t, self.blocks, self.land, self.join = transfers, blocks, land, join
+
+    def begin(self, step):
+        ctx, fsdp = self.MASKS[step]
+        self.copy = self.t.start(self.blocks.at[step], self.land.at[step], ctx=ctx, fsdp=fsdp)
+
+    def end(self, step):
+        self.copy.wait_recv()
+        self.blocks[step + 1] = self.join(self.blocks[step], self.land[step])
+
+    def on(self, step):
+        if 0 <= step - 1 < 5:
+            self.end(step - 1)
+        if step < 5:
+            self.begin(step)
+
+
+def small_scratch(shape):
+    return [pltpu.VMEM((6,) + shape, f32), pltpu.VMEM((5,) + shape, f32)]
+
+
 class PlaneSum:
     def __init__(self, transfers, cores, far, near, sums, total):
         self.t, self.cores, self.far, self.near = transfers, cores, far, near
@@ -800,21 +1073,21 @@
         return self.total[...] + self.near[0].astype(f32) + self.near[1].astype(f32)
 
 
-def plane_sum_scratch(count, rows, columns):
+def plane_sum_scratch(count, *shape):
     return [
-        pltpu.VMEM((count, 4, rows, columns), bf16),
-        pltpu.VMEM((count, rows, columns), bf16),
-        pltpu.VMEM((count, 2, rows, columns), bf16),
-        pltpu.VMEM((count, 3, rows, columns), bf16),
-        pltpu.VMEM((count, rows, columns), f32),
+        pltpu.VMEM((count, 4) + shape, bf16),
+        pltpu.VMEM((count,) + shape, bf16),
+        pltpu.VMEM((count, 2) + shape, bf16),
+        pltpu.VMEM((count, 3) + shape, bf16),
+        pltpu.VMEM((count,) + shape, f32),
     ]
 
 
 def grads_body(
-    h_ref, dg_ref, du_ref, hid_ref, dy_ref, dy_rest, y_rest,
-    gate_out, up_out, down_out, y_land,
+    h_ref, dg_ref, du_ref, hid_ref, dy_ref, dy_rest, y_rest, top_ref,
+    gate_out, up_out, down_out, y_land, top_out,
     left, rights, odd, cores, far, near, sums, totals, left_sem, right_sem, dy_sem, out_sem,
-    send, recv,
+    blocks, land, send, recv,
 ):
     me = lax.axis_index("ctx")
     rows = dy_ref.shape[0]
@@ -837,7 +1110,10 @@
     right_copies[1][0].start()
     greet((1, 2, 4), (1, 2, 3))
     t = Transfers(send, recv)
-    y_copies = [t.start(y_rest.at[d - 1], y_land.at[d - 1], fsdp=d) for d in (1, 2, 3)]
+    tops = SmallReduce(t, blocks, land, jnp.maximum)
+    blocks[0] = top_ref[...]
+    tops.on(0)
+    y_copies = []
     left_copies[0].wait()
     jobs, odd_copies, outs = [], {}, []
 
@@ -863,17 +1139,24 @@
                 left[:, block], rights[k % 2], OVER_ROWS, preferred_element_type=f32
             )
 
-        for j in (7, 5, 3, 1):
+        for i, j in enumerate((7, 5, 3, 1)):
             if j in odd_copies:
                 t.release(odd_copies[j])
             odd[j // 2] = partial(j).astype(bf16)
             odd_copies[j] = job.send_odd(j, odd.at[j // 2])
+            if k == 0:
+                tops.on(i + 1)
+            if k == 0 and i == 0:
+                for d in (1, 2, 3):
+                    y_copies.append(t.start(y_rest.at[d - 1], y_land.at[d - 1], fsdp=d))
         if k:
             jobs[k - 1].pass_on()
         for j in (6, 2, 4, 0):
             job.even(j, partial(j))
         if k:
             close(k - 1)
+    tops.on(5)
+    top_out[...] = blocks[5]
     jobs[2].pass_on()
     for copy in y_copies:
         copy.wait_recv()
@@ -883,34 +1166,36 @@
     t.finish()
 
 
-def grads_row(h, dg, du, hid, dy, dy_rest, y_rest):
+def grads_row(h, dg, du, hid, dy, dy_rest, y_rest, top):
     rows, model = dy.shape
     depth = model // 8
     dma = pltpu.SemaphoreType.DMA
     summed = jax.ShapeDtypeStruct((depth, dg.shape[1]), f32)
     return remote_call(
         grads_body,
-        [summed, summed, jax.ShapeDtypeStruct((depth, model), bf16), jax.ShapeDtypeStruct(y_rest.shape, bf16)],
-        [ANY, ANY, VMEM, ANY],
-        [ANY] * 7,
+        [summed, summed, jax.ShapeDtypeStruct((depth, model), bf16), jax.ShapeDtypeStruct(y_rest.shape, bf16)]
+        + [jax.ShapeDtypeStruct(top.shape, f32)],
+        [ANY, ANY, VMEM, ANY, VMEM],
+        [ANY] * 7 + [VMEM],
         [
             pltpu.VMEM(h.shape, bf16),
             pltpu.VMEM((2,) + h.shape, bf16),
             pltpu.VMEM((4, depth, model), bf16),
         ]
         + plane_sum_scratch(3, depth, model)
-        + [dma((2,)), dma((2,)), dma((4,)), dma((2,))],
-        3 + 3 * 10,
+        + [dma((2,)), dma((2,)), dma((4,)), dma((2,))]
+        + small_scratch(top.shape),
+        3 + 3 * 10 + 5,
         3,
         flops=6 * h.shape[0] * model * model,
-    )(h, dg, du, hid, dy, dy_rest, y_rest)
+    )(h, dg, du, hid, dy, dy_rest, y_rest, top)
 
 
 def kv_sum_body(
-    first_ref, rest_ref, cosine_ref, sine_ref, out_ref,
+    dkv_ref, cosine_ref, sine_ref, out_ref,
     evens, cores, far, near, sums, totals, even_sem, send, recv,
 ):
-    slots = [first_ref.at[0]] + [rest_ref.at[j] for j in range(7)]
+    slots = [dkv_ref.at[:, j] for j in range(8)]
     copies = {
         j: pltpu.make_async_copy(slots[j], evens.at[j // 2], even_sem.at[j // 2])
         for j in (6, 2, 4, 0)
@@ -928,40 +1213,47 @@
     job.pass_on()
     total = job.close()
     cosine, sine = cosine_ref[...], -sine_ref[...]
-    for h in range(total.shape[1] // (2 * HEAD_SIZE)):
-        first = 2 * h * HEAD_SIZE
-        middle = first + HEAD_SIZE
-        out_ref[:, first:middle] = rotate(total[:, first:middle], cosine, sine).astype(bf16)
-        out_ref[:, middle : middle + HEAD_SIZE] = total[:, middle : middle + HEAD_SIZE].astype(bf16)
+    parts, _, width = total.shape
+    for d in range(parts):
+        for h in range(width // (2 * HEAD_SIZE)):
+            first = 2 * h * HEAD_SIZE
+            middle = first + HEAD_SIZE
+            to = d * width + first
+            turned = rotate(total[d, :, first:middle], cosine, sine)
+            value = total[d, :, middle : middle + HEAD_SIZE]
+            out_ref[:, to : to + 2 * HEAD_SIZE] = jnp.concatenate([turned, value], 1).astype(bf16)
     t.finish()
 
 
-def kv_sum(first, rest, cosine, sine):
-    _, rows, width = first.shape
+def kv_sum(dkv, cosine, sine):
+    parts, _, rows, width = dkv.shape
     return remote_call(
         kv_sum_body,
-        jax.ShapeDtypeStruct((rows, width), bf16),
+        jax.ShapeDtypeStruct((rows, parts * width), bf16),
         VMEM,
-        [ANY, ANY, VMEM, VMEM],
-        [pltpu.VMEM((4, rows, width), bf16)]
-        + plane_sum_scratch(1, rows, width)
+        [ANY, VMEM, VMEM],
+        [pltpu.VMEM((4, parts, rows, width), bf16)]
+        + plane_sum_scratch(1, parts, rows, width)
         + [pltpu.SemaphoreType.DMA((4,))],
         10,
         4,
-    )(first, rest, cosine, sine)
+    )(dkv, cosine, sine)
 
 
 def unit_grads_body(
-    h_ref, dq_ref, dkv_ref, attended_ref, db_ref,
-    query_out, key_out, value_out, output_out,
+    h_ref, dq_ref, dkv_ref, attended_ref, db_ref, gain_ref,
+    query_out, key_out, value_out, output_out, gain_out,
     odd, cores, far, near, sums, totals, row_send, row_land,
-    send, recv,
+    blocks, land, send, recv,
 ):
     me, place = lax.axis_index("ctx"), lax.axis_index("fsdp")
     depth = cores.shape[2]
     width = row_land.shape[3]
     greet((1, 2, 4), (1, 2, 3))
     t = Transfers(send, recv)
+    gains = SmallReduce(t, blocks, land, jnp.add)
+    blocks[0] = gain_ref[...]
+    gains.on(0)
     pairs = ((attended_ref, db_ref), (h_ref, dq_ref), (h_ref, dkv_ref))
     jobs, odd_copies, over = [], {}, [None] * 3
 
@@ -988,17 +1280,21 @@
                 left[:, block], right[...], OVER_ROWS, preferred_element_type=f32
             )
 
-        for j in (7, 5, 3, 1):
+        for i, j in enumerate((7, 5, 3, 1)):
             if j in odd_copies:
                 t.release(odd_copies[j])
             odd[j // 2] = partial(j).astype(bf16)
             odd_copies[j] = job.send_odd(j, odd.at[j // 2])
+            if k == 0:
+                gains.on(i + 1)
         if k:
             jobs[k - 1].pass_on()
         for j in (6, 2, 4, 0):
             job.even(j, partial(j))
         if k:
             close(k - 1)
+    gains.on(5)
+    gain_out[...] = blocks[5]
     jobs[2].pass_on()
     close(2)
     for k in range(3):
@@ -1019,23 +1315,24 @@
     t.finish()
 
 
-def unit_grads(h, dq, dkv, attended, db):
+def unit_grads(h, dq, dkv, attended, db, gain_terms):
     rows, model = h.shape
     depth, width = model // 8, model // 4
     wide = jax.ShapeDtypeStruct((depth, width), f32)
     half = jax.ShapeDtypeStruct((depth, width // 2), f32)
     return remote_call(
         unit_grads_body,
-        [wide, half, half, wide],
-        [VMEM] * 4,
+        [wide, half, half, wide, jax.ShapeDtypeStruct(gain_terms.shape, f32)],
         [VMEM] * 5,
+        [VMEM] * 6,
         [pltpu.VMEM((4, depth, model), bf16)]
         + plane_sum_scratch(3, depth, model)
-        + [pltpu.VMEM((3, 3, depth, width), bf16)] * 2,
-        3 * (10 + 3),
+        + [pltpu.VMEM((3, 3, depth, width), bf16)] * 2
+        + small_scratch(gain_terms.shape),
+        3 * (10 + 3) + 5,
         5,
         flops=6 * rows * model * model,
-    )(h, dq, dkv, attended, db)
+    )(h, dq, dkv, attended, db, gain_terms)
 
 
 def unit_specs(depth, slots):
@@ -1051,64 +1348,6 @@
 
     widths = ((2 * HEAD_SIZE, 0), (HEAD_SIZE, 4), (HEAD_SIZE, 6))
     return [of_own(w) for w, _ in widths] + [of_rest(w, first) for w, first in widths]
-
-
-def unit_forward_body(
-    place_ref, h_ref, cosine_ref, sine_ref, q_own, k_own, v_own, q_rest, k_rest, v_rest,
-    unit_out, kv_out, total,
-):
-    d = pl.program_id(0)
-
-    @pl.when(d == 0)
-    def _():
-        weight = jnp.concatenate([q_own[...], k_own[...], v_own[...]], 1)
-        total[...] = jnp.dot(h_ref[...], weight, preferred_element_type=f32)
-
-    @pl.when(d > 0)
-    def _():
-        slots, depth = q_rest.shape[1], q_rest.shape[2]
-        value = None
-        for j in range(slots):
-            owner = place_ref[0] ^ j
-            part = h_ref[:, pl.ds(pl.multiple_of(owner * depth, depth), depth)]
-            weight = jnp.concatenate([q_rest[0, j], k_rest[0, j], v_rest[0, j]], 1)
-            term = jnp.dot(part, weight, preferred_element_type=f32)
-            value = term if value is None else value + term
-        total[...] = value
-
-    cosine, sine = cosine_ref[...], sine_ref[...]
-    turned = [
-        rotate(total[:, i * HEAD_SIZE : (i + 1) * HEAD_SIZE], cosine, sine).astype(bf16)
-        for i in range(REPEAT + 1)
-    ]
-    value = total[:, (REPEAT + 1) * HEAD_SIZE :].astype(bf16)
-    unit_out[...] = jnp.concatenate(turned + [value], 1)
-    kv_out[...] = jnp.concatenate([turned[REPEAT], value], 1)
-
-
-def unit_forward(places, h, cosine, sine, query, key, value, rest):
-    rows = h.shape[0]
-    heads = query.shape[1] // (REPEAT * HEAD_SIZE)
-    _, slots, depth, _ = rest.shape
-    whole = lambda a: pl.BlockSpec(a.shape, lambda d, h, p: (0, 0))
-    return pl.pallas_call(
-        unit_forward_body,
-        out_shape=[
-            jax.ShapeDtypeStruct((rows, 4 * heads * UNIT), bf16),
-            jax.ShapeDtypeStruct((rows, 4 * heads * 2 * HEAD_SIZE), bf16),
-        ],
-        grid_spec=pltpu.PrefetchScalarGridSpec(
-            num_scalar_prefetch=1,
-            grid=(4, heads),
-            in_specs=[whole(h), whole(cosine), whole(sine)] + unit_specs(depth, slots),
-            out_specs=[
-                pl.BlockSpec((rows, UNIT), lambda d, h, p: (0, d * heads + h)),
-                pl.BlockSpec((rows, 2 * HEAD_SIZE), lambda d, h, p: (0, d * heads + h)),
-            ],
-            scratch_shapes=[pltpu.VMEM((rows, UNIT), f32)],
-        ),
-        **params(8 * rows * h.shape[1] * heads * UNIT, 8 * h.shape[1] * heads * UNIT),
-    )(places, h, cosine, sine, query, key, value, rest, rest, rest)
 
 
 def unit_back_body(
@@ -1163,43 +1402,6 @@
         pl.BlockSpec(own.shape, lambda d, p: (0, 0)),
         pl.BlockSpec((1, slots, depth, width), lambda d, p: (jnp.maximum(d - 1, 0), 0, 0, 0)),
     ]
-
-
-def output_forward_body(place_ref, attended_ref, x_ref, own_ref, rest_ref, out_ref):
-    d = pl.program_id(0)
-    x = x_ref[...].astype(f32)
-
-    @pl.when(d == 0)
-    def _():
-        out_ref[...] = x + jnp.dot(attended_ref[...], own_ref[...], preferred_element_type=f32)
-
-    @pl.when(d > 0)
-    def _():
-        slots, depth = rest_ref.shape[1], rest_ref.shape[2]
-        value = x
-        for j in range(slots):
-            owner = place_ref[0] ^ j
-            part = attended_ref[:, pl.ds(pl.multiple_of(owner * depth, depth), depth)]
-            value = value + jnp.dot(part, rest_ref[0, j], preferred_element_type=f32)
-        out_ref[...] = value
-
-
-def output_forward(places, attended, x, own, rest):
-    rows, model = x.shape
-    width = own.shape[1]
-    tile = pl.BlockSpec((rows, width), lambda d, p: (0, p[1] ^ d))
-    return pl.pallas_call(
-        output_forward_body,
-        out_shape=jax.ShapeDtypeStruct((rows, model), f32),
-        grid_spec=pltpu.PrefetchScalarGridSpec(
-            num_scalar_prefetch=1,
-            grid=(4,),
-            in_specs=[pl.BlockSpec(attended.shape, lambda d, p: (0, 0)), tile]
-            + output_specs(own, rest),
-            out_specs=tile,
-        ),
-        **params(2 * rows * model * model, 2 * model * model),
-    )(places, attended, x, own, rest)
 
 
 def output_back_body(place_ref, db_ref, own_ref, rest_ref, out_ref, total):
@@ -1528,14 +1730,6 @@
     )
 
 
-def full_gains(first_gain, second_gain):
-    count, place = lax.axis_size("fsdp"), lax.axis_index("fsdp")
-    gains = jnp.stack([first_gain, second_gain])
-    parts = [gains] + [swap(gains, "fsdp", d) for d in range(1, count)]
-    gains = jnp.concatenate(by_place(parts, place), 1).astype(f32)
-    return gains[0], gains[1]
-
-
 def on_row_of_chips(
     hidden_in,
     out_grad,
@@ -1557,32 +1751,46 @@
     places = jnp.stack([me, place]).astype(jnp.int32)
     place_one = places[1:]
     natural, begin, key_natural, cosine, sine = attention_layout(seq_lengths, block_perm, rows)
-    first_full, second_full = full_gains(first_gain, second_gain)
     tokens_low = hidden_in.reshape(rows, model)
     grad_out = out_grad.reshape(rows, model)
-
-    unit_rest, output_rest, down_rest = weight_gather(
-        query_weight, key_matrix, value_matrix, output_weight, down_weight
-    )
+    gains = jnp.pad(jnp.stack([first_gain, second_gain]).astype(f32), ((0, 6), (0, 0)))
+    (
+        normalized,
+        qkv,
+        attended,
+        best,
+        residual,
+        normed_two,
+        all_gains,
+        kv_all,
+        unit_rest,
+        output_rest,
+        down_rest,
+        dy_rest,
+    ) = attention_row(
+        tokens_low,
+        gains,
+        cosine,
+        sine,
+        natural,
+        begin,
+        key_natural,
+        query_weight,
+        key_matrix,
+        value_matrix,
+        output_weight,
+        down_weight,
+        grad_out,
+    )
+    full = jnp.concatenate(by_place([all_gains[d] for d in range(4)], place), 1)
+    first_full, second_full = full[0], full[1]
     tokens = tokens_low.astype(f32)
     scale_one = rms_scale(tokens)
     unit_one = tokens * scale_one
-    normalized = (unit_one * first_full).astype(bf16)
-    qkv, kv_local = unit_forward(
-        places, normalized, cosine, sine, query_weight, key_matrix, value_matrix, unit_rest
-    )
-    kv_rest, dy_rest = kv_gather(kv_local, grad_out)
-    kv_slots = [kv_local[None], kv_rest]
-    attended, best = attend(place_one, natural, begin, key_natural, qkv, kv_slots)
-    head_max = jnp.max(best[:, :, :REPEAT, 0], 0).reshape(QUERY_HEADS)
-    for mask in (4, 2, 1):
-        head_max = jnp.maximum(head_max, swap(head_max, "ctx", mask))
-    for mask in (2, 1):
-        head_max = jnp.maximum(head_max, swap(head_max, "fsdp", mask))
-    residual = output_forward(places, attended, tokens_low, output_weight, output_rest)
     scale_two = rms_scale(residual)
     unit_two = residual * scale_two
-    normed_two = (unit_two * second_full).astype(bf16)
+    top = jnp.max(best[:, :, :REPEAT, 0], 0)
+    top = jnp.pad(top, ((0, 0), (0, 128 - REPEAT)))
 
     hid, dg, du, h_all, y_own, y_rest, grad_normed_two = feed_forward_row(
         normed_two, grad_out, dy_rest, gate_weight, up_weight, down_weight, down_rest
@@ -1592,33 +1800,42 @@
         grad_normed_two * second_full, unit_two, scale_two
     )
     grad_branch = grad_residual.astype(bf16)
-    gate_grad, up_grad, down_sum, y_land = grads_row(h_all, dg, du, hid, grad_out, dy_rest, y_rest)
+    gate_grad, up_grad, down_sum, y_land, top = grads_row(
+        h_all, dg, du, hid, grad_out, dy_rest, y_rest, top
+    )
+    head_max = top[:, :REPEAT].reshape(QUERY_HEADS)
     result = (residual + y_own + jnp.sum(y_land.astype(f32), 0)).astype(bf16)
     width = model // 4
-    moved = []
+    moved, pieces = [], []
     for k in range(4):
+        piece = lax.dynamic_slice_in_dim(down_sum, ((me % 4) ^ k) * width, width, 1)
+        pieces.append(piece)
+    (normalized, attended), pieces = lax.optimization_barrier(((normalized, attended), pieces))
+    for k, piece in enumerate(pieces):
         pairs = [
             (c * 4 + f, (2 * f + c // 4) * 4 + (c % 4 ^ k)) for c in range(8) for f in range(4)
         ]
-        piece = lax.dynamic_slice_in_dim(down_sum, ((me % 4) ^ k) * width, width, 1)
         moved.append(lax.ppermute(piece, ("ctx", "fsdp"), pairs))
     down_grad = jnp.concatenate(by_place(moved, place), 0).astype(f32)
 
     head_grad = output_back(places, grad_branch, output_weight, output_rest)
-    query_grad, dkv_first, dkv_rest = attend_back(
-        place_one, natural, begin, key_natural, cosine, sine, qkv, head_grad, kv_slots
-    )
-    dkv = kv_sum(dkv_first, dkv_rest, cosine, sine)
+    query_grad, dkv = attend_back(
+        place_one, natural, begin, key_natural, cosine, sine, qkv, head_grad, [kv_all]
+    )
+    dkv = kv_sum(dkv, cosine, sine)
     grad_normed_one = unit_back(
         places, query_grad, dkv, query_weight, key_matrix, value_matrix, unit_rest
     )
     first_term = jnp.sum(grad_normed_one * unit_one, 0)
     grad_input = grad_residual + norm_back(grad_normed_one * first_full, unit_one, scale_one)
-    query_out, key_out, value_out, output_out = unit_grads(
-        normalized, query_grad, dkv, attended, grad_branch
-    )
-    first_out = gain_sum(first_term, me, place, 8, 4)
-    second_out = gain_sum(second_term, me, place, 8, 4)
+    terms = jnp.concatenate([first_term, second_term]).reshape(-1, 128)
+    query_out, key_out, value_out, output_out, terms = unit_grads(
+        normalized, query_grad, dkv, attended, grad_branch, terms
+    )
+    terms = lax.dynamic_slice_in_dim(
+        terms.reshape(2, -1), (me * 4 + place) * (model // 32), model // 32, 1
+    )
+    first_out, second_out = terms[0], terms[1]
     multiplier = jnp.sqrt(clip_limit / jnp.maximum(head_max, clip_limit))
     key_ratio = jnp.min(multiplier.reshape(KEY_VALUE_HEADS, REPEAT), 1)
     return (

time: 903 us -> 758 us (0.84)
  Pallas kernels: 761 us -> 693 us
  starting transfers between devices: 40.6 us -> 8.75 us
  waiting for transfers between devices: 21.5 us -> 0.01 us
  other arithmetic: 41.2 us -> 27.2 us
    pallas_call x7 -> x3, Pallas kernels: 445 us -> 362 us  [the longest x1 180 us: attention_row(): remote_call(attention_row_body, [out((rows, model)), out((rows, 4 * width...]
    ppermute x18 -> x0, starting transfers between devices: 32.2 us -> none  [swap(): return lax.ppermute(value, axis, [(i, i ^ mask) for i in range(size)])]
    ppermute x18 -> x0, waiting for transfers between devices: 21.5 us -> none  [swap(): return lax.ppermute(value, axis, [(i, i ^ mask) for i in range(size)])]
    pallas_call x1, Pallas kernels: 154 us -> 165 us  [feed_forward_row(): remote_call(feed_forward_row_body, [wide, wide, wide, jax.ShapeDtypeStruc...]
    unnamed x98 -> x68, local copies, waits for them, and re-layouts: 18.7 us -> 11.3 us
  transfers between devices with their start and end apart: 22 -> 4, of which waited for: 12 -> 0; matrix products, arithmetic and copies ran while one was open for 4% -> 3% of each run, Pallas kernels for 15% -> 30%
where the time goes in v3:
time: 758 us; the launch traced here: 750 us
  Pallas kernels  693 us (91%)
  other arithmetic  27.2 us (4%)
  local copies, waits for them, and re-layouts  19.2 us (3%)
  starting transfers between devices  8.75 us (1%)
    pallas_call x1, Pallas kernels, attention_row(): remote_call(attention_row_body, [out((rows, model)), out((rows, 4 * width...  180 us
    pallas_call x1, Pallas kernels, feed_forward_row(): remote_call(feed_forward_row_body, [wide, wide, wide, jax.ShapeDtypeStruc...  165 us
    pallas_call x1, Pallas kernels, unit_grads(): remote_call(unit_grads_body, [wide, half, half, wide, jax.ShapeDtypeStruc...  137 us
    pallas_call x1, Pallas kernels, grads_row(): remote_call(grads_body, [summed, summed, jax.ShapeDtypeStruct((depth, mod...  122 us
    pallas_call x1, Pallas kernels, kv_sum(): remote_call(kv_sum_body, jax.ShapeDtypeStruct((rows, parts * width), bf16...  45.1 us
    pallas_call x1, Pallas kernels, attend_back(): pl.pallas_call(functools.partial(attend_back_body, len(slots)), out_shape...  24.1 us
  transfers between devices with their start and end apart: 4, of which 0 were waited for; matrix products, arithmetic and copies ran while one was open for 3% of the time, Pallas kernels for 30%

profile of v3, /device:TPU:0, one launch (start us, length us, event | category | flops | bytes accessed | tf_op | source)
XLA Modules:
  0.0 749.7 jit_solution(16340970879837165978)
XLA Ops:
  0.7 1.3 iota_reduce_fusion
  2.1 0.8 reduce-window.4
  5.3 0.8 copy.54.begin_ref.start_ref
  6.1 0.8 copy.53.natural_ref
  8.0 0.8 pad_maximum_fusion
  9.5 180.0 %shard_map.245 = (bf16[256,2048]{1,0:T(8,128)(2,1)}, bf16[256,4096]{1,0:T(8,128)(2,1)}, bf16[256,2048]{1,0:T(8,128)(2,1)}, f32[2,8,8,128]{3,2,1,0:T(8,128)}, f32...) custom-call(bf16[256,2048]{1,0:T(8,128)(2,1)} %bitcast.71, ...), custom_call_target="tpu_custom_call" | custom-call | flops 10737418240 | bytes 4194304 | tf_op jit(solution)/shard_map/pallas_call | solution.py:794
  189.5 0.9 slice_reduce_fusion
  191.0 164.6 %shard_map.246 = (bf16[1024,2048]{1,0:T(8,128)(2,1)}, bf16[1024,2048]{1,0:T(8,128)(2,1)}, bf16[1024,2048]{1,0:T(8,128)(2,1)}, bf16[1024,2048]{1,0:T(8,128)(2,1)}...) custom-call(bf16[256,2048]{1,0:T(8,128)(2,1)} %get-tuple-element.54.h_ref, ...), custom_call_target="tpu_custom_call" | custom-call | flops 51539607552 | bytes 4194304 | tf_op jit(solution)/shard_map/pallas_call | solution.py:973
  355.7 121.7 %shard_map.247 = (f32[256,2048]{1,0:T(8,128)}, f32[256,2048]{1,0:T(8,128)}, bf16[256,2048]{1,0:T(8,128)(2,1)}, bf16[3,256,2048]{2,1,0:T(8,128)(2,1)}, f32[8,128]{1,0:T(8,128)}) custom-call(bf16[1024,2048]{1,0:T(8,128)(2,1)} %get-tuple-element.58.h_ref, bf16[1024,2048]{1,0:T(8,128)(2,1)} %get-tuple-element.59.dg_ref, ...), custom_call_target="tpu_custom_call" | custom-call | flops 25769803776 | bytes 4194304 | tf_op jit(solution)/shard_map/pallas_call | solution.py:1174
  477.4 2.2 constant_dynamic-slice_fusion.1
  479.6 5.0 collective-permute-start
  484.6 1.9 collective-permute-start.1
  487.0 1.3 collective-permute-start.3
  489.0 1.2 copy-done.15
  491.0 0.9 copy-done.13
  492.9 0.8 copy-done.3
  493.8 6.9 shard_map.248.grad_ref
  500.7 24.1 %shard_map.249 = (bf16[256,2048]{1,0:T(8,128)(2,1)S(1)}, bf16[4,8,256,512]{3,2,1,0:T(8,128)(2,1)}) custom-call(s32[1]{0:T(128)} %bitcast.32.place_ref, s32[256,1]{1,0:T(8,128)S(1)} %copy-done.9, s32[256,1]{1,0:T(8,128)S(1)} %copy-done.8, s32[2,1,1024]{2,1,0:T(1,128)S(1)} %bitcast.70, f32[256,128]{1,0:T(8,128)S(1)} %copy-done.6, f32[256,128]{1,0:T(8,128)S(1)} %copy-done.7, ...), custom_call_target="tpu_custom_call" | custom-call | flops 5368709120 | bytes 20971520 | tf_op jit(solution)/shard_map/pallas_call | solution.py:331
  524.8 45.1 %shard_map.250.dkv_ref = bf16[256,2048]{1,0:T(8,128)(2,1)} custom-call(bf16[4,8,256,512]{3,2,1,0:T(8,128)(2,1)} %get-tuple-element.71.dkv_ref, f32[256,128]{1,0:T(8,128)} %get-tuple-element.142.cosine_ref, f32[256,128]{1,0:T(8,128)} %get-tuple-element.143.sine_ref), custom_call_target="tpu_custom_call" | custom-call | bytes 4194304 | tf_op jit(solution)/shard_map/pallas_call | solution.py:1230
  570.0 1.2 copy-done
  571.2 13.8 %shard_map.251 = f32[256,2048]{1,0:T(8,128)} custom-call(s32[2]{0:T(128)S(1)} %pad_add_fusion.place_ref, bf16[256,2048]{1,0:T(8,128)(2,1)S(1)} %get-tuple-element.70.dq_ref, bf16[256,2048]{1,0:T(8,128)(2,1)S(1)} %copy-done, bf16[2048,512]{1,0:T(8,128)(2,1)} %q_own.1, bf16[2048,256]{1,0:T(8,128)(2,1)S(1)} %copy-done.1, bf16[2048,256]{1,0:T(8,128)(2,1)S(1)} %copy-done.4, ...), custom_call_target="tpu_custom_call" | custom-call | flops 4294967296 | bytes 16777216 | tf_op jit(solution)/shard_map/pallas_call | solution.py:1386
  585.0 2.4 fusion.8
  587.5 2.0 convert_reduce_fusion
  590.3 136.8 %shard_map.252 = (f32[256,512]{1,0:T(8,128)}, f32[256,256]{1,0:T(8,128)}, f32[256,256]{1,0:T(8,128)}, f32[256,512]{1,0:T(8,128)}, f32[32,128]{1,0:T(8,128)}) custom-call(bf16[256,2048]{1,0:T(8,128)(2,1)} %get-tuple-element.76.h_ref, bf16[256,2048]{1,0:T(8,128)(2,1)} %copy-done.5, bf16[256,2048]{1,0:T(8,128)(2,1)} %shard_map.250.dkv_ref, ...), custom_call_target="tpu_custom_call" | custom-call | flops 6442450944 | bytes 4194304 | tf_op jit(solution)/shard_map/pallas_call | solution.py:1323
  728.1 1.2 multiply_convert_fusion.1
  729.3 3.5 multiply_convert_fusion
  732.7 6.3 fusion.11
  739.6 1.3 broadcast_select_fusion.7
  740.9 1.6 maximum_convert_fusion
  745.6 1.3 copy.67
  746.9 1.0 copy-done.21
  747.9 1.3 copy.68
  (105 shorter events, 13.2 us)
Async XLA Ops:
  355.7 132.7 %copy-start.16 = (bf16[1,256,2048]{2,1,0:T(8,128)(2,1)S(1)}, bf16[1,256,2048]{2,1,0:T(8,128)(2,1)}, u32[]{:S(2)}) copy-start(bf16[1,256,2048]{2,1,0:T(8,128)(2,1)} %param.14) | copy-start | bytes 3145732
  477.4 11.4 %copy-start.12 = (f32[256,2048]{1,0:T(8,128)S(1)}, f32[256,2048]{1,0:T(8,128)}, u32[]{:S(2)}) copy-start(f32[256,2048]{1,0:T(8,128)} %get-tuple-element.53) | copy-start | bytes 6291460
  479.6 9.4 %copy-start.27 = (f32[4,8,512]{2,1,0:T(8,128)S(1)}, f32[4,8,512]{2,1,0:T(8,128)}, u32[]{:S(2)}) copy-start(f32[4,8,512]{2,1,0:T(8,128)} %get-tuple-element.66) | copy-start | bytes 196612
  479.6 260.0 %collective-permute-start = (bf16[256,512]{1,0:T(8,128)(2,1)}, bf16[256,512]{1,0:T(8,128)(2,1)}, u32[]{:S(2)}, u32[]{:S(2)}) collective-permute-start(bf16[256,512]{1,0:T(8,128)(2,1)} %get-tuple-element.85), channel_id=1, source_target_pairs={{0,3},{1,11},{2,19},{3,27},{4,2},{5,10},{6,18},{7,26},{8,1},{9,9},... | collective-permute-start | bytes 786440 | tf_op jit(solution)/shard_map/ppermute | solution.py:1818
  484.6 254.9 %collective-permute-start.1 = (bf16[256,512]{1,0:T(8,128)(2,1)}, bf16[256,512]{1,0:T(8,128)(2,1)}, u32[]{:S(2)}, u32[]{:S(2)}) collective-permute-start(bf16[256,512]{1,0:T(8,128)(2,1)} %get-tuple-element.86), channel_id=1, source_target_pairs={{0,2},{1,10},{2,18},{3,26},{4,3},{5,11},{6,19},{7,27},{8,0},{9,8},... | collective-permute-start | bytes 786440 | tf_op jit(solution)/shard_map/ppermute | solution.py:1818
  486.5 253.1 %collective-permute-start.2 = (bf16[256,512]{1,0:T(8,128)(2,1)}, bf16[256,512]{1,0:T(8,128)(2,1)}, u32[]{:S(2)}, u32[]{:S(2)}) collective-permute-start(bf16[256,512]{1,0:T(8,128)(2,1)} %get-tuple-element.87), channel_id=1, source_target_pairs={{0,1},{1,9},{2,17},{3,25},{4,0},{5,8},{6,16},{7,24},{8,3},{9,11},{... | collective-permute-start | bytes 786440 | tf_op jit(solution)/shard_map/ppermute | solution.py:1818
  487.0 252.6 %collective-permute-start.3 = (bf16[256,512]{1,0:T(8,128)(2,1)S(1)}, bf16[256,512]{1,0:T(8,128)(2,1)}, u32[]{:S(2)}, u32[]{:S(2)}) collective-permute-start(bf16[256,512]{1,0:T(8,128)(2,1)S(1)} %get-tuple-element.88), channel_id=1, source_target_pairs={{0,0},{1,8},{2,16},{3,24},{4,1},{5,9},{6,17},{7,25},{8,2},{9,10},{... | collective-permute-start | bytes 786440 | tf_op jit(solution)/shard_map/ppermute | solution.py:1818
  488.7 1.6 copy-start.15
  490.3 1.9 copy-start.19
  492.8 7.8 %copy-start.2 = (bf16[256,2048]{1,0:T(8,128)(2,1)}, bf16[256,2048]{1,0:T(8,128)(2,1)S(1)}, u32[]{:S(2)}) copy-start(bf16[256,2048]{1,0:T(8,128)(2,1)S(1)} %fusion.28.db_ref) | copy-start | bytes 3145732
  493.7 6.9 copy-start.6
  493.7 6.9 copy-start.7
  493.7 7.0 copy-start.8
  493.7 7.0 copy-start.9
  493.7 7.0 copy-start.10
  493.7 7.0 copy-start.11
  524.8 45.2 %copy-start.5 = (bf16[256,2048]{1,0:T(8,128)(2,1)}, bf16[256,2048]{1,0:T(8,128)(2,1)S(1)}, u32[]{:S(2)}) copy-start(bf16[256,2048]{1,0:T(8,128)(2,1)S(1)} %get-tuple-element.70.dq_ref) | copy-start | bytes 3145732
  524.8 45.2 %copy-start.1 = (bf16[2048,256]{1,0:T(8,128)(2,1)S(1)}, bf16[2048,256]{1,0:T(8,128)(2,1)}, u32[]{:S(2)}) copy-start(bf16[2048,256]{1,0:T(8,128)(2,1)} %k_own.1) | copy-start | bytes 3145732
  524.8 45.2 %copy-start.4 = (bf16[2048,256]{1,0:T(8,128)(2,1)S(1)}, bf16[2048,256]{1,0:T(8,128)(2,1)}, u32[]{:S(2)}) copy-start(bf16[2048,256]{1,0:T(8,128)(2,1)} %v_own.1) | copy-start | bytes 3145732
  571.2 13.8 %copy-start.17 = (bf16[1,256,2048]{2,1,0:T(8,128)(2,1)S(1)}, bf16[1,256,2048]{2,1,0:T(8,128)(2,1)}, u32[]{:S(2)}) copy-start(bf16[1,256,2048]{2,1,0:T(8,128)(2,1)} %param.14) | copy-start | bytes 3145732
  585.0 2.5 copy-start.20
  587.5 2.0 copy-start.28
  587.5 2.0 copy-start.30
  589.5 137.6 %copy-start.29 = (f32[16]{0:T(128)}, f32[16]{0:T(128)S(1)}, u32[]{:S(2)}) copy-start(f32[16]{0:T(128)S(1)} %reshape.215) | copy-start | bytes 196
  729.3 3.5 copy-start.14
  729.3 3.5 copy-start.18
  740.9 1.7 copy-start.24
  740.9 2.4 copy-start.26
  740.9 3.1 copy-start.25
  740.9 3.8 copy-start.23
  742.5 3.0 copy-start.22
  745.6 2.3 copy-start.21
  (3 other events, 4.4 us)

commit v4 on v3

--- a/solution.py
+++ b/solution.py
@@ -408,7 +408,7 @@
         scratch_shapes=list(scratch)
         + [pltpu.SemaphoreType.DMA((transfers,)), pltpu.SemaphoreType.DMA((transfers,))],
         compiler_params=pltpu.CompilerParams(
-            vmem_limit_bytes=60 * 2**20, collective_id=number, has_side_effects=True
+            vmem_limit_bytes=62 * 2**20, collective_id=number, has_side_effects=True
         ),
         cost_estimate=pl.CostEstimate(flops=flops, bytes_accessed=moved, transcendentals=0),
     )
@@ -1191,258 +1191,319 @@
     )(h, dg, du, hid, dy, dy_rest, y_rest, top)
 
 
-def kv_sum_body(
-    dkv_ref, cosine_ref, sine_ref, out_ref,
-    evens, cores, far, near, sums, totals, even_sem, send, recv,
-):
-    slots = [dkv_ref.at[:, j] for j in range(8)]
-    copies = {
-        j: pltpu.make_async_copy(slots[j], evens.at[j // 2], even_sem.at[j // 2])
-        for j in (6, 2, 4, 0)
-    }
-    for copy in copies.values():
-        copy.start()
-    greet((1, 2, 4), ())
-    t = Transfers(send, recv)
-    job = PlaneSum(t, cores.at[0], far.at[0], near.at[0], sums.at[0], totals.at[0])
-    for j in (7, 3, 5, 1):
-        job.send_odd(j, slots[j])
-    for j in (6, 2, 4, 0):
-        copies[j].wait()
-        job.even(j, evens[j // 2].astype(f32))
-    job.pass_on()
-    total = job.close()
-    cosine, sine = cosine_ref[...], -sine_ref[...]
-    parts, _, width = total.shape
-    for d in range(parts):
-        for h in range(width // (2 * HEAD_SIZE)):
-            first = 2 * h * HEAD_SIZE
-            middle = first + HEAD_SIZE
-            to = d * width + first
-            turned = rotate(total[d, :, first:middle], cosine, sine)
-            value = total[d, :, middle : middle + HEAD_SIZE]
-            out_ref[:, to : to + 2 * HEAD_SIZE] = jnp.concatenate([turned, value], 1).astype(bf16)
-    t.finish()
-
-
-def kv_sum(dkv, cosine, sine):
-    parts, _, rows, width = dkv.shape
-    return remote_call(
-        kv_sum_body,
-        jax.ShapeDtypeStruct((rows, parts * width), bf16),
-        VMEM,
-        [ANY, VMEM, VMEM],
-        [pltpu.VMEM((4, parts, rows, width), bf16)]
-        + plane_sum_scratch(1, parts, rows, width)
-        + [pltpu.SemaphoreType.DMA((4,))],
-        10,
-        4,
-    )(dkv, cosine, sine)
-
-
-def unit_grads_body(
-    h_ref, dq_ref, dkv_ref, attended_ref, db_ref, gain_ref,
-    query_out, key_out, value_out, output_out, gain_out,
-    odd, cores, far, near, sums, totals, row_send, row_land,
-    blocks, land, send, recv,
+class RowSum:
+    def __init__(self, transfers, total, sent, landed, columns):
+        self.total, self.landed, self.columns = total, landed, columns
+        self.over = []
+        for d in (1, 2, 3):
+            sent[d - 1] = total[:, columns(d)].astype(bf16)
+            self.over.append(transfers.start(sent.at[d - 1], landed.at[d - 1], fsdp=d))
+
+    def close(self):
+        total = self.total[:, self.columns(0)]
+        for d in range(3):
+            self.over[d].wait_recv()
+            total = total + self.landed[d].astype(f32)
+        return total
+
+
+def attention_back_body(
+    db_ref, attended_ref, qkv_ref, cosine_ref, sine_ref, natural_ref, begin_ref, key_natural_ref,
+    kv_ref, o_ref, output_rest,
+    dq_out, dkv_out, output_out,
+    kvs, o_own, outputs, head_grad, odd,
+    cores, far, near, sums, totals,
+    kv_cores, kv_far, kv_near, kv_sums, kv_totals,
+    row_send, row_land, load_sem, send, recv,
 ):
     me, place = lax.axis_index("ctx"), lax.axis_index("fsdp")
+    rows, model = db_ref.shape
+    depth = cores.shape[2]
+    width = o_own.shape[1]
+    rounds = key_natural_ref.shape[0]
+    blk = rows // rounds
+    heads = kvs.shape[3] // (2 * HEAD_SIZE)
+    loads = [
+        pltpu.make_async_copy(src, dst, load_sem.at[i])
+        for i, (src, dst) in enumerate(((o_ref, o_own), (output_rest, outputs), (kv_ref, kvs)))
+    ]
+    for load in loads:
+        load.start()
+    greet((1, 2, 4), (1, 2, 3))
+    t = Transfers(send, recv)
+
+    def of_slot(j):
+        return pl.ds(pl.multiple_of(flip(me, j) * depth, depth), depth)
+
+    def shard(d):
+        return pl.ds(pl.multiple_of(flip(place, d) * width, width), width)
+
+    job = PlaneSum(t, cores.at[0], far.at[0], near.at[0], sums.at[0], totals.at[0])
+
+    def partial(j):
+        return lax.dot_general(
+            attended_ref[:, of_slot(j)], db_ref[...], OVER_ROWS, preferred_element_type=f32
+        )
+
+    for j in (7, 5, 3, 1):
+        odd[j // 2] = partial(j).astype(bf16)
+        job.send_odd(j, odd.at[j // 2])
+    for j in (6, 2, 4, 0):
+        job.even(j, partial(j))
+
+    loads[0].wait()
+    loads[1].wait()
+    for j in range(8):
+        total = lax.dot_general(
+            db_ref[:, shard(0)], o_own[of_slot(j)], OVER_COLUMNS, preferred_element_type=f32
+        )
+        for d in (1, 2, 3):
+            total += lax.dot_general(
+                db_ref[:, shard(d)], outputs[d - 1, j], OVER_COLUMNS, preferred_element_type=f32
+            )
+        head_grad[:, of_slot(j)] = total.astype(bf16)
+    loads[2].wait()
+    cosine, sine = cosine_ref[...], -sine_ref[...]
+
+    def attend_heads(d):
+        def step(i, carry):
+            r, h = lax.div(i, heads), lax.rem(i, heads)
+            here = pl.ds(pl.multiple_of(r * blk, blk), blk)
+            first = pl.multiple_of(d * heads * UNIT + h * UNIT, UNIT)
+            query = stacked_heads(qkv_ref[here, pl.ds(first, REPEAT * HEAD_SIZE)])
+            cols = pl.ds(pl.multiple_of(h * 2 * HEAD_SIZE, 2 * HEAD_SIZE), 2 * HEAD_SIZE)
+            both = kvs[d, :, here, cols].reshape(8 * blk, 2 * HEAD_SIZE)
+            keys, values = both[:, :HEAD_SIZE], both[:, HEAD_SIZE:]
+            natural = key_natural_ref[r]
+            allowed = (natural >= begin_ref[here]) & (natural <= natural_ref[here])
+            allowed = jnp.concatenate([allowed] * REPEAT, 0)
+            spot = flip(place, d) * heads + h
+            spot_cols = pl.ds(
+                pl.multiple_of(spot * REPEAT * HEAD_SIZE, REPEAT * HEAD_SIZE), REPEAT * HEAD_SIZE
+            )
+            grad = stacked_heads(head_grad[here, spot_cols])
+            probs, _ = probabilities(query, keys, allowed)
+            low = probs.astype(bf16)
+            grad_probs = lax.dot_general(grad, values, OVER_COLUMNS, preferred_element_type=f32)
+            delta = jnp.sum(low.astype(f32) * grad_probs, 1, keepdims=True)
+            score_grad = (probs * (grad_probs - delta)).astype(bf16)
+            query_grad = jnp.dot(score_grad, keys, preferred_element_type=f32) * SCALE
+            turn = cosine_ref[here], -sine_ref[here]
+            first = pl.multiple_of((d * heads + h) * REPEAT * HEAD_SIZE, REPEAT * HEAD_SIZE)
+            dq_out[here, pl.ds(first, REPEAT * HEAD_SIZE)] = jnp.concatenate(
+                [rotate(query_grad[i * blk : (i + 1) * blk], *turn) for i in range(REPEAT)], 1
+            ).astype(bf16)
+            key_grad = lax.dot_general(score_grad, query, OVER_ROWS, preferred_element_type=f32)
+            value_grad = lax.dot_general(low, grad, OVER_ROWS, preferred_element_type=f32)
+            both = jnp.concatenate([key_grad * SCALE, value_grad], 1).astype(bf16)
+            kvs[d, :, here, cols] = both.reshape(8, blk, 2 * HEAD_SIZE)
+            return carry
+
+        lax.fori_loop(0, rounds * heads, step, 0)
+
+    kv_jobs = [
+        PlaneSum(t, kv_cores.at[k], kv_far.at[k], kv_near.at[k], kv_sums.at[k], kv_totals.at[k])
+        for k in range(2)
+    ]
+
+    def send_half(k):
+        half = pl.ds(2 * k, 2)
+        for j in (7, 3, 5, 1):
+            kv_jobs[k].send_odd(j, kvs.at[half, j])
+        for j in (6, 2, 4, 0):
+            kv_jobs[k].even(j, kvs[half, j].astype(f32))
+
+    def take_half(k):
+        total = kv_jobs[k].close()
+        for i in range(2):
+            for h in range(heads):
+                first = 2 * h * HEAD_SIZE
+                middle = first + HEAD_SIZE
+                to = ((2 * k + i) * heads + h) * 2 * HEAD_SIZE
+                turned = rotate(total[i, :, first:middle], cosine, sine)
+                value = total[i, :, middle : middle + HEAD_SIZE]
+                dkv_out[:, to : to + 2 * HEAD_SIZE] = jnp.concatenate([turned, value], 1).astype(bf16)
+
+    attend_heads(0)
+    job.pass_on()
+    attend_heads(1)
+    send_half(0)
+    attend_heads(2)
+    kv_jobs[0].pass_on()
+    attend_heads(3)
+    send_half(1)
+    totals[0] = job.close()
+    row = RowSum(t, totals.at[0], row_send, row_land, shard)
+    kv_jobs[1].pass_on()
+    take_half(0)
+    output_out[...] = row.close()
+    take_half(1)
+    t.finish()
+
+
+def attention_back(db, attended, qkv, cosine, sine, natural, begin, key_natural, kv, output, output_rest):
+    rows, model = db.shape
+    depth, width = model // 8, output.shape[1]
+    kv_width = kv.shape[3]
+    return remote_call(
+        attention_back_body,
+        [
+            jax.ShapeDtypeStruct((rows, model), bf16),
+            jax.ShapeDtypeStruct((rows, 4 * kv_width), bf16),
+            jax.ShapeDtypeStruct((depth, width), f32),
+        ],
+        [VMEM] * 3,
+        [VMEM] * 8 + [ANY] * 3,
+        [
+            pltpu.VMEM(kv.shape, bf16),
+            pltpu.VMEM(output.shape, bf16),
+            pltpu.VMEM(output_rest.shape, bf16),
+            pltpu.VMEM((rows, model), bf16),
+            pltpu.VMEM((4, depth, model), bf16),
+        ]
+        + plane_sum_scratch(1, depth, model)
+        + plane_sum_scratch(2, 2, rows, kv_width)
+        + [pltpu.VMEM((3, depth, width), bf16)] * 2
+        + [pltpu.SemaphoreType.DMA((3,))],
+        3 * 10 + 3,
+        4,
+        flops=20 * rows * model * model,
+    )(db, attended, qkv, cosine, sine, natural, begin, key_natural, kv, output, output_rest)
+
+
+def unit_grads_body(
+    h_ref, dq_ref, dkv_ref, x_ref, term_ref, q_ref, k_ref, v_ref, unit_rest,
+    query_out, key_out, value_out, back_out, gain_out,
+    odd, q_own, k_own, v_own, units, cores, far, near, sums, totals, row_send, row_land,
+    blocks, land, load_sem, unit_sem, send, recv,
+):
+    me = lax.axis_index("ctx")
     depth = cores.shape[2]
     width = row_land.shape[3]
+    heads = k_own.shape[1] // HEAD_SIZE
+    loads = [
+        pltpu.make_async_copy(src, dst, load_sem.at[i])
+        for i, (src, dst) in enumerate(((q_ref, q_own), (k_ref, k_own), (v_ref, v_own)))
+    ]
+    unit_loads = [
+        pltpu.make_async_copy(unit_rest.at[d], units.at[d % 2], unit_sem.at[d]) for d in range(3)
+    ]
+    for load in loads + unit_loads[:2]:
+        load.start()
     greet((1, 2, 4), (1, 2, 3))
     t = Transfers(send, recv)
-    gains = SmallReduce(t, blocks, land, jnp.add)
-    blocks[0] = gain_ref[...]
-    gains.on(0)
-    pairs = ((attended_ref, db_ref), (h_ref, dq_ref), (h_ref, dkv_ref))
-    jobs, odd_copies, over = [], {}, [None] * 3
-
-    def columns(k, d):
-        if k == 0:
-            return pl.ds(pl.multiple_of(flip(place, d) * width, width), width)
-        return pl.ds(d * width, width)
-
-    def close(k):
-        totals[k] = jobs[k].close()
-        over[k] = []
-        for d in (1, 2, 3):
-            row_send[k, d - 1] = totals[k, :, columns(k, d)].astype(bf16)
-            over[k].append(t.start(row_send.at[k, d - 1], row_land.at[k, d - 1], fsdp=d))
-
-    for k in range(3):
-        left, right = pairs[k]
+    jobs, odd_copies = [], {}
+
+    def of_slot(j):
+        return pl.ds(pl.multiple_of(flip(me, j) * depth, depth), depth)
+
+    for k, right in enumerate((dq_ref, dkv_ref)):
         job = PlaneSum(t, cores.at[k], far.at[k], near.at[k], sums.at[k], totals.at[k])
         jobs.append(job)
 
         def partial(j):
-            block = pl.ds(pl.multiple_of(flip(me, j) * depth, depth), depth)
             return lax.dot_general(
-                left[:, block], right[...], OVER_ROWS, preferred_element_type=f32
+                h_ref[:, of_slot(j)], right[...], OVER_ROWS, preferred_element_type=f32
             )
 
-        for i, j in enumerate((7, 5, 3, 1)):
+        for j in (7, 5, 3, 1):
             if j in odd_copies:
                 t.release(odd_copies[j])
             odd[j // 2] = partial(j).astype(bf16)
             odd_copies[j] = job.send_odd(j, odd.at[j // 2])
-            if k == 0:
-                gains.on(i + 1)
-        if k:
-            jobs[k - 1].pass_on()
         for j in (6, 2, 4, 0):
             job.even(j, partial(j))
-        if k:
-            close(k - 1)
+
+    def grads(d):
+        query = dq_ref[:, d * width : (d + 1) * width]
+        pairs = dkv_ref[:, d * width : (d + 1) * width]
+        parts = [pairs[:, i * HEAD_SIZE : (i + 1) * HEAD_SIZE] for i in range(2 * heads)]
+        return jnp.concatenate([query] + parts[::2] + parts[1::2], 1)
+
+    def back(d):
+        grad = grads(d)
+        for j in range(8):
+            cols = of_slot(j)
+            if d == 0:
+                weight = jnp.concatenate([w[cols] for w in (q_own, k_own, v_own)], 1)
+                back_out[:, cols] = lax.dot_general(
+                    grad, weight, OVER_COLUMNS, preferred_element_type=f32
+                )
+            else:
+                back_out[:, cols] += lax.dot_general(
+                    grad, units[(d - 1) % 2, j], OVER_COLUMNS, preferred_element_type=f32
+                )
+
+    for load in loads:
+        load.wait()
+    back(0)
+    jobs[0].pass_on()
+    unit_loads[0].wait()
+    back(1)
+    unit_loads[2].start()
+    unit_loads[1].wait()
+    back(2)
+    jobs[1].pass_on()
+    unit_loads[2].wait()
+    back(3)
+    x = x_ref[...].astype(f32)
+    unit = x * lax.rsqrt(jnp.mean(x * x, 1, keepdims=True) + epsilon)
+    gains = SmallReduce(t, blocks, land, jnp.add)
+    blocks[0] = jnp.concatenate(
+        [jnp.sum(back_out[...] * unit, 0, keepdims=True), term_ref[1:8]], 0
+    )
+    gains.on(0)
+
+    def columns(d):
+        return pl.ds(d * width, width)
+
+    totals[0] = jobs[0].close()
+    gains.on(1)
+    first = RowSum(t, totals.at[0], row_send.at[0], row_land.at[0], columns)
+    gains.on(2)
+    totals[1] = jobs[1].close()
+    second = RowSum(t, totals.at[1], row_send.at[1], row_land.at[1], columns)
+    gains.on(3)
+    gains.on(4)
+    query_out[...] = first.close()
     gains.on(5)
     gain_out[...] = blocks[5]
-    jobs[2].pass_on()
-    close(2)
-    for k in range(3):
-        total = totals[k, :, columns(k, 0)]
-        for d in range(3):
-            over[k][d].wait_recv()
-            total = total + row_land[k, d].astype(f32)
-        if k == 0:
-            output_out[...] = total
-        elif k == 1:
-            query_out[...] = total
-        else:
-            for h in range(total.shape[1] // (2 * HEAD_SIZE)):
-                first = 2 * h * HEAD_SIZE
-                here = slice(h * HEAD_SIZE, (h + 1) * HEAD_SIZE)
-                key_out[:, here] = total[:, first : first + HEAD_SIZE]
-                value_out[:, here] = total[:, first + HEAD_SIZE : first + 2 * HEAD_SIZE]
+    total = second.close()
+    for h in range(heads):
+        start = 2 * h * HEAD_SIZE
+        here = slice(h * HEAD_SIZE, (h + 1) * HEAD_SIZE)
+        key_out[:, here] = total[:, start : start + HEAD_SIZE]
+        value_out[:, here] = total[:, start + HEAD_SIZE : start + 2 * HEAD_SIZE]
     t.finish()
 
 
-def unit_grads(h, dq, dkv, attended, db, gain_terms):
+def unit_grads(h, dq, dkv, x, terms, query, key, value, rest):
     rows, model = h.shape
     depth, width = model // 8, model // 4
     wide = jax.ShapeDtypeStruct((depth, width), f32)
     half = jax.ShapeDtypeStruct((depth, width // 2), f32)
+    dma = pltpu.SemaphoreType.DMA
     return remote_call(
         unit_grads_body,
-        [wide, half, half, wide, jax.ShapeDtypeStruct(gain_terms.shape, f32)],
+        [wide, half, half, jax.ShapeDtypeStruct((rows, model), f32)]
+        + [jax.ShapeDtypeStruct(terms.shape, f32)],
         [VMEM] * 5,
-        [VMEM] * 6,
-        [pltpu.VMEM((4, depth, model), bf16)]
-        + plane_sum_scratch(3, depth, model)
-        + [pltpu.VMEM((3, 3, depth, width), bf16)] * 2
-        + small_scratch(gain_terms.shape),
-        3 * (10 + 3) + 5,
+        [VMEM] * 5 + [ANY] * 4,
+        [
+            pltpu.VMEM((4, depth, model), bf16),
+            pltpu.VMEM(query.shape, bf16),
+            pltpu.VMEM(key.shape, bf16),
+            pltpu.VMEM(value.shape, bf16),
+            pltpu.VMEM((2,) + rest.shape[1:], bf16),
+        ]
+        + plane_sum_scratch(2, depth, model)
+        + [pltpu.VMEM((2, 3, depth, width), bf16)] * 2
+        + small_scratch(terms.shape)
+        + [dma((3,)), dma((3,))],
+        2 * (10 + 3) + 5,
         5,
-        flops=6 * rows * model * model,
-    )(h, dq, dkv, attended, db, gain_terms)
-
-
-def unit_specs(depth, slots):
-    def of_rest(width, first):
-        return pl.BlockSpec(
-            (1, slots, depth, width), lambda d, h, p: (jnp.maximum(d - 1, 0), 0, 0, first + h)
-        )
-
-    def of_own(width):
-        return pl.BlockSpec(
-            (slots * depth, width), lambda d, h, p: (0, jnp.where(d == 0, h, 1))
-        )
-
-    widths = ((2 * HEAD_SIZE, 0), (HEAD_SIZE, 4), (HEAD_SIZE, 6))
-    return [of_own(w) for w, _ in widths] + [of_rest(w, first) for w, first in widths]
-
-
-def unit_back_body(
-    place_ref, dq_ref, dkv_ref, q_own, k_own, v_own, q_rest, k_rest, v_rest, out_ref
-):
-    d, h = pl.program_id(0), pl.program_id(1)
-    grad = jnp.concatenate([dq_ref[...], dkv_ref[...]], 1)
-
-    @pl.when((d == 0) & (h == 0))
-    def _():
-        out_ref[...] = jnp.zeros_like(out_ref)
-
-    @pl.when(d == 0)
-    def _():
-        weight = jnp.concatenate([q_own[...], k_own[...], v_own[...]], 1)
-        out_ref[...] += lax.dot_general(grad, weight, OVER_COLUMNS, preferred_element_type=f32)
-
-    @pl.when(d > 0)
-    def _():
-        slots, depth = q_rest.shape[1], q_rest.shape[2]
-        for j in range(slots):
-            owner = place_ref[0] ^ j
-            cols = pl.ds(pl.multiple_of(owner * depth, depth), depth)
-            weight = jnp.concatenate([q_rest[0, j], k_rest[0, j], v_rest[0, j]], 1)
-            out_ref[:, cols] += lax.dot_general(
-                grad, weight, OVER_COLUMNS, preferred_element_type=f32
-            )
-
-
-def unit_back(places, dq, dkv, query, key, value, rest):
-    rows = dq.shape[0]
-    heads = query.shape[1] // (REPEAT * HEAD_SIZE)
-    _, slots, depth, _ = rest.shape
-    model = slots * depth
-    pair = pl.BlockSpec((rows, 2 * HEAD_SIZE), lambda d, h, p: (0, d * heads + h))
-    return pl.pallas_call(
-        unit_back_body,
-        out_shape=jax.ShapeDtypeStruct((rows, model), f32),
-        grid_spec=pltpu.PrefetchScalarGridSpec(
-            num_scalar_prefetch=1,
-            grid=(4, heads),
-            in_specs=[pair, pair] + unit_specs(depth, slots),
-            out_specs=pl.BlockSpec((rows, model), lambda d, h, p: (0, 0)),
-        ),
-        **params(8 * rows * model * heads * UNIT, 8 * model * heads * UNIT),
-    )(places, dq, dkv, query, key, value, rest, rest, rest)
-
-
-def output_specs(own, rest):
-    _, slots, depth, width = rest.shape
-    return [
-        pl.BlockSpec(own.shape, lambda d, p: (0, 0)),
-        pl.BlockSpec((1, slots, depth, width), lambda d, p: (jnp.maximum(d - 1, 0), 0, 0, 0)),
-    ]
-
-
-def output_back_body(place_ref, db_ref, own_ref, rest_ref, out_ref, total):
-    d = pl.program_id(0)
-    db = db_ref[...]
-
-    @pl.when(d == 0)
-    def _():
-        total[...] = lax.dot_general(db, own_ref[...], OVER_COLUMNS, preferred_element_type=f32)
-
-    @pl.when(d > 0)
-    def _():
-        slots, depth = rest_ref.shape[1], rest_ref.shape[2]
-        for j in range(slots):
-            owner = place_ref[0] ^ j
-            cols = pl.ds(pl.multiple_of(owner * depth, depth), depth)
-            total[:, cols] += lax.dot_general(
-                db, rest_ref[0, j], OVER_COLUMNS, preferred_element_type=f32
-            )
-
-    @pl.when(d == pl.num_programs(0) - 1)
-    def _():
-        out_ref[...] = total[...].astype(bf16)
-
-
-def output_back(places, db, own, rest):
-    rows, model = db.shape
-    height, width = own.shape
-    return pl.pallas_call(
-        output_back_body,
-        out_shape=jax.ShapeDtypeStruct((rows, height), bf16),
-        grid_spec=pltpu.PrefetchScalarGridSpec(
-            num_scalar_prefetch=1,
-            grid=(4,),
-            in_specs=[pl.BlockSpec((rows, width), lambda d, p: (0, p[1] ^ d))]
-            + output_specs(own, rest),
-            out_specs=pl.BlockSpec((rows, height), lambda d, p: (0, 0)),
-            scratch_shapes=[pltpu.VMEM((rows, height), f32)],
-        ),
-        **params(2 * rows * model * height, 2 * model * height),
-    )(places, db, own, rest)
+        flops=12 * rows * model * model,
+    )(h, dq, dkv, x, terms, query, key, value, rest)
 
 
 def token_layout(length_row, block_slots, block_size):
@@ -1748,8 +1809,6 @@
 ):
     rows, model = hidden_in.shape[1], hidden_in.shape[2]
     me, place = lax.axis_index("ctx"), lax.axis_index("fsdp")
-    places = jnp.stack([me, place]).astype(jnp.int32)
-    place_one = places[1:]
     natural, begin, key_natural, cosine, sine = attention_layout(seq_lengths, block_perm, rows)
     tokens_low = hidden_in.reshape(rows, model)
     grad_out = out_grad.reshape(rows, model)
@@ -1810,7 +1869,7 @@
     for k in range(4):
         piece = lax.dynamic_slice_in_dim(down_sum, ((me % 4) ^ k) * width, width, 1)
         pieces.append(piece)
-    (normalized, attended), pieces = lax.optimization_barrier(((normalized, attended), pieces))
+    attended, pieces = lax.optimization_barrier((attended, pieces))
     for k, piece in enumerate(pieces):
         pairs = [
             (c * 4 + f, (2 * f + c // 4) * 4 + (c % 4 ^ k)) for c in range(8) for f in range(4)
@@ -1818,22 +1877,34 @@
         moved.append(lax.ppermute(piece, ("ctx", "fsdp"), pairs))
     down_grad = jnp.concatenate(by_place(moved, place), 0).astype(f32)
 
-    head_grad = output_back(places, grad_branch, output_weight, output_rest)
-    query_grad, dkv = attend_back(
-        place_one, natural, begin, key_natural, cosine, sine, qkv, head_grad, [kv_all]
-    )
-    dkv = kv_sum(dkv, cosine, sine)
-    grad_normed_one = unit_back(
-        places, query_grad, dkv, query_weight, key_matrix, value_matrix, unit_rest
-    )
-    first_term = jnp.sum(grad_normed_one * unit_one, 0)
+    query_grad, dkv, output_out = attention_back(
+        grad_branch,
+        attended,
+        qkv,
+        cosine,
+        sine,
+        natural,
+        begin,
+        key_natural,
+        kv_all,
+        output_weight,
+        output_rest,
+    )
+    terms = jnp.pad(second_term[None], ((1, 6), (0, 0)))
+    query_out, key_out, value_out, grad_normed_one, terms = unit_grads(
+        normalized,
+        query_grad,
+        dkv,
+        tokens_low,
+        terms,
+        query_weight,
+        key_matrix,
+        value_matrix,
+        unit_rest,
+    )
     grad_input = grad_residual + norm_back(grad_normed_one * first_full, unit_one, scale_one)
-    terms = jnp.concatenate([first_term, second_term]).reshape(-1, 128)
-    query_out, key_out, value_out, output_out, terms = unit_grads(
-        normalized, query_grad, dkv, attended, grad_branch, terms
-    )
     terms = lax.dynamic_slice_in_dim(
-        terms.reshape(2, -1), (me * 4 + place) * (model // 32), model // 32, 1
+        terms[:2], (me * 4 + place) * (model // 32), model // 32, 1
     )
     first_out, second_out = terms[0], terms[1]
     multiplier = jnp.sqrt(clip_limit / jnp.maximum(head_max, clip_limit))

time: 758 us -> 738 us (0.974)
  Pallas kernels: 693 us -> 674 us
    pallas_call x5 -> x2, Pallas kernels: 227 us -> 208 us  [the longest x1 122 us: unit_grads(): remote_call(unit_grads_body, [wide, half, half, jax.ShapeDtypeStruct((row...]
    pallas_call x1, Pallas kernels: 122 us -> 130 us  [grads_row(): remote_call(grads_body, [summed, summed, jax.ShapeDtypeStruct((depth, mod...]
    pallas_call x1, Pallas kernels: 165 us -> 156 us  [feed_forward_row(): remote_call(feed_forward_row_body, [wide, wide, wide, jax.ShapeDtypeStruc...]
  transfers between devices with their start and end apart: 4 -> 4, of which waited for: 0 -> 0; matrix products, arithmetic and copies ran while one was open for 3% -> 3% of each run, Pallas kernels for 30% -> 29%
where the time goes in v4:
time: 738 us; the launch traced here: 728 us
  Pallas kernels  674 us (91%)
  other arithmetic  26.9 us (4%)
  local copies, waits for them, and re-layouts  17.5 us (2%)
  starting transfers between devices  8.74 us (1%)
    pallas_call x1, Pallas kernels, attention_row(): remote_call(attention_row_body, [out((rows, model)), out((rows, 4 * width...  180 us
    pallas_call x1, Pallas kernels, feed_forward_row(): remote_call(feed_forward_row_body, [wide, wide, wide, jax.ShapeDtypeStruc...  156 us
    pallas_call x1, Pallas kernels, grads_row(): remote_call(grads_body, [summed, summed, jax.ShapeDtypeStruct((depth, mod...  130 us
    pallas_call x1, Pallas kernels, unit_grads(): remote_call(unit_grads_body, [wide, half, half, jax.ShapeDtypeStruct((row...  122 us
    pallas_call x1, Pallas kernels, attention_back(): remote_call(attention_back_body, [jax.ShapeDtypeStruct((rows, model), bf1...  85.4 us
  transfers between devices with their start and end apart: 4, of which 0 were waited for; matrix products, arithmetic and copies ran while one was open for 3% of the time, Pallas kernels for 29%

profile of v4, /device:TPU:0, one launch (start us, length us, event | category | flops | bytes accessed | tf_op | source)
XLA Modules:
  0.0 728.3 jit_solution(16006453587393966961)
XLA Ops:
  0.6 1.3 iota_reduce_fusion
  2.1 0.8 reduce-window.4
  3.9 0.8 copy.53.natural_ref
  4.7 0.8 copy.54.begin_ref
  8.0 0.8 pad_maximum_fusion
  9.5 180.0 %shard_map.245 = (bf16[256,2048]{1,0:T(8,128)(2,1)}, bf16[256,4096]{1,0:T(8,128)(2,1)}, bf16[256,2048]{1,0:T(8,128)(2,1)}, f32[2,8,8,128]{3,2,1,0:T(8,128)}, f32...) custom-call(bf16[256,2048]{1,0:T(8,128)(2,1)} %bitcast.65, ...), custom_call_target="tpu_custom_call" | custom-call | flops 10737418240 | bytes 4194304 | tf_op jit(solution)/shard_map/pallas_call | solution.py:794
  189.5 0.9 slice_reduce_fusion
  191.0 156.3 %shard_map.246 = (bf16[1024,2048]{1,0:T(8,128)(2,1)}, bf16[1024,2048]{1,0:T(8,128)(2,1)}, bf16[1024,2048]{1,0:T(8,128)(2,1)}, bf16[1024,2048]{1,0:T(8,128)(2,1)}...) custom-call(bf16[256,2048]{1,0:T(8,128)(2,1)} %get-tuple-element.54.h_ref, ...), custom_call_target="tpu_custom_call" | custom-call | flops 51539607552 | bytes 4194304 | tf_op jit(solution)/shard_map/pallas_call | solution.py:973
  347.3 130.1 %shard_map.247 = (f32[256,2048]{1,0:T(8,128)}, f32[256,2048]{1,0:T(8,128)}, bf16[256,2048]{1,0:T(8,128)(2,1)}, bf16[3,256,2048]{2,1,0:T(8,128)(2,1)}, f32[8,128]{1,0:T(8,128)}) custom-call(bf16[1024,2048]{1,0:T(8,128)(2,1)} %get-tuple-element.58.h_ref, bf16[1024,2048]{1,0:T(8,128)(2,1)} %get-tuple-element.59.dg_ref, ...), custom_call_target="tpu_custom_call" | custom-call | flops 25769803776 | bytes 4194304 | tf_op jit(solution)/shard_map/pallas_call | solution.py:1174
  477.5 2.2 constant_dynamic-slice_fusion.1
  479.7 5.0 collective-permute-start
  484.7 1.9 collective-permute-start.1
  487.1 1.4 collective-permute-start.3
  489.1 1.3 copy-done.2
  491.6 1.6 fusion.26.db_ref
  493.9 85.4 %shard_map.248 = (bf16[256,2048]{1,0:T(8,128)(2,1)}, bf16[256,2048]{1,0:T(8,128)(2,1)}, f32[256,512]{1,0:T(8,128)}) custom-call(bf16[256,2048]{1,0:T(8,128)(2,1)} %fusion.26.db_ref, bf16[256,2048]{1,0:T(8,128)(2,1)} %get-tuple-element.70.attended_ref, bf16[256,4096]{1,0:T(8,128)(2,1)} %get-tuple-element.71.qkv_ref, ...), custom_call_target="tpu_custom_call" | custom-call | flops 21474836480 | bytes 4194304 | tf_op jit(solution)/shard_map/pallas_call | solution.py:1348
  579.3 122.2 %shard_map.249 = (f32[256,512]{1,0:T(8,128)}, f32[256,256]{1,0:T(8,128)}, f32[256,256]{1,0:T(8,128)}, f32[256,2048]{1,0:T(8,128)}, f32[8,2048]{1,0:T(8,128)}) custom-call(bf16[256,2048]{1,0:T(8,128)(2,1)} %get-tuple-element.67.h_ref, bf16[256,2048]{1,0:T(8,128)(2,1)} %get-tuple-element.74.dq_ref, bf16[256,2048]{1,0:T(8,128)(2,1)} %get-tuple-element.75.dkv_ref, ...), custom_call_target="tpu_custom_call" | custom-call | flops 12884901888 | bytes 4194304 | tf_op jit(solution)/shard_map/pallas_call | solution.py:1486
  701.5 2.2 fusion.2
  704.0 2.0 convert_reduce_fusion
  706.0 0.8 slice.88
  707.1 1.8 multiply_convert_fusion
  709.1 2.5 multiply_convert_fusion.1
  711.6 6.3 fusion.9
  718.5 1.3 broadcast_select_fusion.7
  719.9 1.6 maximum_convert_fusion
  721.5 0.8 copy.63
  722.3 0.7 copy.64
  723.0 0.7 copy.65
  723.7 0.8 copy.66
  724.5 1.3 copy.67
  725.8 1.0 copy-done.7
  726.8 1.3 copy.68
  (75 shorter events, 9.2 us)
Async XLA Ops:
  347.3 141.2 %copy-start.3 = (bf16[1,256,2048]{2,1,0:T(8,128)(2,1)S(1)}, bf16[1,256,2048]{2,1,0:T(8,128)(2,1)}, u32[]{:S(2)}) copy-start(bf16[1,256,2048]{2,1,0:T(8,128)(2,1)} %param.14) | copy-start | bytes 3145732
  477.5 11.3 %copy-start = (f32[256,2048]{1,0:T(8,128)S(1)}, f32[256,2048]{1,0:T(8,128)}, u32[]{:S(2)}) copy-start(f32[256,2048]{1,0:T(8,128)} %get-tuple-element.53) | copy-start | bytes 6291460
  479.7 9.3 %copy-start.14 = (f32[4,8,512]{2,1,0:T(8,128)S(1)}, f32[4,8,512]{2,1,0:T(8,128)}, u32[]{:S(2)}) copy-start(f32[4,8,512]{2,1,0:T(8,128)} %get-tuple-element.66) | copy-start | bytes 196612
  479.7 238.8 %collective-permute-start = (bf16[256,512]{1,0:T(8,128)(2,1)}, bf16[256,512]{1,0:T(8,128)(2,1)}, u32[]{:S(2)}, u32[]{:S(2)}) collective-permute-start(bf16[256,512]{1,0:T(8,128)(2,1)} %get-tuple-element.85), channel_id=1, source_target_pairs={{0,3},{1,11},{2,19},{3,27},{4,2},{5,10},{6,18},{7,26},{8,1},{9,9},... | collective-permute-start | bytes 786440 | tf_op jit(solution)/shard_map/ppermute | solution.py:1877
  484.7 233.8 %collective-permute-start.1 = (bf16[256,512]{1,0:T(8,128)(2,1)}, bf16[256,512]{1,0:T(8,128)(2,1)}, u32[]{:S(2)}, u32[]{:S(2)}) collective-permute-start(bf16[256,512]{1,0:T(8,128)(2,1)} %get-tuple-element.86), channel_id=1, source_target_pairs={{0,2},{1,10},{2,18},{3,26},{4,3},{5,11},{6,19},{7,27},{8,0},{9,8},... | collective-permute-start | bytes 786440 | tf_op jit(solution)/shard_map/ppermute | solution.py:1877
  486.6 231.9 %collective-permute-start.2 = (bf16[256,512]{1,0:T(8,128)(2,1)}, bf16[256,512]{1,0:T(8,128)(2,1)}, u32[]{:S(2)}, u32[]{:S(2)}) collective-permute-start(bf16[256,512]{1,0:T(8,128)(2,1)} %get-tuple-element.87), channel_id=1, source_target_pairs={{0,1},{1,9},{2,17},{3,25},{4,0},{5,8},{6,16},{7,24},{8,3},{9,11},{... | collective-permute-start | bytes 786440 | tf_op jit(solution)/shard_map/ppermute | solution.py:1877
  487.1 231.4 %collective-permute-start.3 = (bf16[256,512]{1,0:T(8,128)(2,1)S(1)}, bf16[256,512]{1,0:T(8,128)(2,1)}, u32[]{:S(2)}, u32[]{:S(2)}) collective-permute-start(bf16[256,512]{1,0:T(8,128)(2,1)S(1)} %get-tuple-element.88), channel_id=1, source_target_pairs={{0,0},{1,8},{2,16},{3,24},{4,1},{5,9},{6,17},{7,25},{8,2},{9,10},{... | collective-permute-start | bytes 786440 | tf_op jit(solution)/shard_map/ppermute | solution.py:1877
  488.8 1.6 copy-start.2
  490.4 1.2 copy-start.5
  579.3 122.2 %copy-start.4 = (bf16[1,256,2048]{2,1,0:T(8,128)(2,1)S(1)}, bf16[1,256,2048]{2,1,0:T(8,128)(2,1)}, u32[]{:S(2)}) copy-start(bf16[1,256,2048]{2,1,0:T(8,128)(2,1)} %param.14) | copy-start | bytes 3145732
  701.5 2.5 copy-start.6
  704.0 2.8 copy-start.15
  704.0 2.9 copy-start.17
  704.0 3.1 copy-start.9
  706.9 2.0 copy-start.16
  708.9 2.7 copy-start.1
  719.8 1.7 copy-start.11
  719.8 2.4 copy-start.13
  719.8 3.1 copy-start.12
  719.8 3.8 copy-start.10
  721.5 3.0 copy-start.8
  724.5 2.3 copy-start.7

commit v5 on v4

--- a/solution.py
+++ b/solution.py
@@ -345,6 +345,7 @@
 ANY = pl.BlockSpec(memory_space=pl.ANY)
 VMEM = pl.BlockSpec(memory_space=pltpu.VMEM)
 MESH = pl.DeviceIdType.MESH
+TILE = 256
 OVER_ROWS = (((0,), (0,)), ((), ()))
 OVER_COLUMNS = (((1,), (1,)), ((), ()))
 
@@ -371,32 +372,52 @@
     pl.semaphore_wait(barrier, len(partners))
 
 
+def stretch(place, size):
+    first = place * size
+    return pl.ds(first if isinstance(place, int) else pl.multiple_of(first, size), size)
+
+
 class Transfers:
     def __init__(self, send, recv):
         self.send, self.recv, self.count, self.open = send, recv, 0, {}
 
-    def start(self, src, dst, ctx=0, fsdp=0):
-        number = self.count
-        copy = pltpu.make_async_remote_copy(
-            src_ref=src,
-            dst_ref=dst,
-            send_sem=self.send.at[number],
-            recv_sem=self.recv.at[number],
-            device_id=device(ctx, fsdp),
+    def start(self, src, dst, ctx=0, fsdp=0, now=True):
+        copy = Transfer(self, self.count, src, dst, ctx, fsdp)
+        if now:
+            copy.made().start()
+        self.open[self.count] = copy
+        self.count += 1
+        return copy
+
+    def release(self, copy):
+        self.open.pop(copy.number).made().wait_send()
+
+    def finish(self):
+        for copy in list(self.open.values()):
+            self.release(copy)
+
+
+def part_of(ref):
+    return ref[0].at[ref[1]] if isinstance(ref, tuple) else ref
+
+
+class Transfer:
+    def __init__(self, transfers, number, src, dst, ctx, fsdp):
+        self.t, self.number, self.src, self.dst = transfers, number, src, dst
+        self.ctx, self.fsdp = ctx, fsdp
+
+    def made(self):
+        return pltpu.make_async_remote_copy(
+            src_ref=part_of(self.src),
+            dst_ref=part_of(self.dst),
+            send_sem=self.t.send.at[self.number],
+            recv_sem=self.t.recv.at[self.number],
+            device_id=device(self.ctx, self.fsdp),
             device_id_type=MESH,
         )
-        copy.start()
-        copy_key = id(copy)
-        self.open[copy_key] = copy
-        self.count += 1
-        return copy
-
-    def release(self, copy):
-        self.open.pop(id(copy)).wait_send()
-
-    def finish(self):
-        for copy in self.open.values():
-            copy.wait_send()
+
+    def wait_recv(self):
+        self.made().wait_recv()
 
 
 def remote_call(body, outs, out_specs, in_specs, scratch, transfers, number, flops=0, moved=2**22):
@@ -831,14 +852,177 @@
     )(x, gains, cosine, sine, natural, begin, key_natural, query, key, value, output, down, dy)
 
 
-TILE = 256
+class SmallReduce:
+    def __init__(self, transfers, blocks, land, join, masks):
+        self.t, self.blocks, self.land, self.join = transfers, blocks, land, join
+        self.masks = masks
+
+    def begin(self, step):
+        ctx, fsdp = self.masks[step]
+        self.copy = self.t.start(
+            (self.blocks, step), (self.land, step), ctx=ctx, fsdp=fsdp
+        )
+
+    def end(self, step):
+        self.copy.wait_recv()
+        self.blocks[step + 1] = self.join(self.blocks[step], self.land[step])
+
+    def on(self, step):
+        if 0 <= step - 1 < 5:
+            self.end(step - 1)
+        if step < 5:
+            self.begin(step)
+
+
+def small_scratch(shape):
+    return [pltpu.VMEM((6,) + shape, f32), pltpu.VMEM((5,) + shape, f32)]
+
+
+class PlaneSum:
+    def __init__(self, transfers, cores, far, near, sums, total, fetch=None):
+        self.t, self.cores, self.far, self.near = transfers, cores, far, near
+        self.sums, self.total, self.fetch = sums, total, fetch
+        self.half = cores.shape[1] // 2
+        self.over = {}
+
+    def arrive(self, j):
+        self.over[j].wait_recv()
+        if self.fetch is not None:
+            place, sems = self.fetch
+            slot = (j // 2) % 2
+            self.copy = pltpu.make_async_copy(
+                self.cores.at[j // 2], place.at[slot], sems.at[slot]
+            )
+            self.copy.start()
+
+    def send_odd(self, j, src):
+        self.over[j - 1] = self.t.start(src, self.cores.at[(j - 1) // 2], ctx=1)
+        return self.over[j - 1]
+
+    def even(self, j, value):
+        t, h = self.t, self.half
+        if self.fetch is None:
+            value = value + self.cores[j // 2].astype(f32)
+        else:
+            self.copy.wait()
+            value = value + self.fetch[0][(j // 2) % 2].astype(f32)
+        if j == 0:
+            self.total[...] = value
+            return
+        out = self.sums.at[(6, 2, 4).index(j)]
+        out[...] = value.astype(bf16)
+        if j == 6:
+            self.x6 = t.start(out.at[:h], self.far.at[:h], ctx=2)
+            self.y6 = t.start(out.at[h:], self.far.at[h:], ctx=4)
+        elif j == 2:
+            self.x2 = t.start(out.at[:h], self.near.at[0, :h], ctx=2)
+        else:
+            self.y4 = t.start(out.at[h:], self.near.at[1, h:], ctx=4)
+
+    def pass_on(self):
+        t, h = self.t, self.half
+        two, four = self.sums.at[1], self.sums.at[2]
+        self.y6.wait_recv()
+        two[h:] = (two[h:].astype(f32) + self.far[h:].astype(f32)).astype(bf16)
+        self.x2b = t.start(two.at[h:], self.near.at[0, h:], ctx=2)
+        self.x6.wait_recv()
+        four[:h] = (four[:h].astype(f32) + self.far[:h].astype(f32)).astype(bf16)
+        self.y4b = t.start(four.at[:h], self.near.at[1, :h], ctx=4)
+
+    def close(self):
+        for copy in (self.x2, self.x2b, self.y4, self.y4b):
+            copy.wait_recv()
+        return self.total[...] + self.near[0].astype(f32) + self.near[1].astype(f32)
+
+
+def plane_sum_scratch(count, *shape):
+    return [
+        pltpu.VMEM((count, 4) + shape, bf16),
+        pltpu.VMEM((count,) + shape, bf16),
+        pltpu.VMEM((count, 2) + shape, bf16),
+        pltpu.VMEM((count, 3) + shape, bf16),
+        pltpu.VMEM((count,) + shape, f32),
+    ]
 
 
 def feed_forward_row_body(
+    h_ref, dy_ref, dy_rest, gate_ref, up_ref, down_own, down_rest, top_ref,
+    hid_out, dg_out, du_out, h_out, y_out, y_rest, back_out,
+    cores, y_land, gate_out, up_out, down_out, top_out,
+    hs, back_send, back_land, far, near, blocks, land,
+    load_sem, down_sem, dy_sem, h_sem, stage_sem, y_sem, left_sem, right_sem, core_sem, out_sem,
+    row_send, row_recv, send, recv,
+):
+    greet((1, 2, 4), (1, 2, 3))
+    t = Transfers(send, recv)
+    row = RowGather(h_ref, [None] + [hs.at[d] for d in range(3)], row_send, row_recv)
+    row.begin()
+    blocks[0] = top_ref[...]
+    tops = SmallReduce(
+        t, blocks, land, jnp.maximum, ((2, 0), (4, 0), (1, 0), (0, 1), (0, 2))
+    )
+    rows, model = h_ref.shape
+    tiles = gate_ref.shape[1] // TILE
+    backs = []
+
+    def forward(gates, ups, downs, dys, y_acc, back_acc, y_send, stage):
+        feed_forward_parts(
+            t, row, tops, backs,
+            h_ref, dy_ref, dy_rest, gate_ref, up_ref, down_own, down_rest,
+            hid_out, dg_out, du_out, h_out, y_out, y_rest, back_out,
+            gates, ups, downs, hs, dys, y_acc, back_acc, back_send, back_land, y_send, stage,
+            load_sem, down_sem, dy_sem, h_sem, stage_sem, y_sem,
+        )
+
+    block = pltpu.VMEM((rows, model), f32)
+    pl.run_scoped(
+        forward,
+        pltpu.VMEM((tiles, model, TILE), bf16),
+        pltpu.VMEM((tiles, model, TILE), bf16),
+        pltpu.VMEM((tiles, TILE, model), bf16),
+        pltpu.VMEM((4, rows, model), bf16),
+        block,
+        block,
+        pltpu.VMEM((rows, model), bf16),
+        pltpu.VMEM((2, 3, rows, TILE), bf16),
+    )
+    y_copy = t.start((y_rest, 0), y_land, fsdp=1)
+
+    def grads(left, rights, odd, sums, totals, fetched):
+        feed_forward_grads(
+            t, h_out, dg_out, du_out, hid_out, dy_ref, dy_rest,
+            gate_out, up_out, down_out,
+            left, rights, odd, cores, far, near, sums, totals, fetched,
+            left_sem, right_sem, dy_sem, core_sem, out_sem,
+        )
+        t.finish()
+
+    depth = model // 8
+    pl.run_scoped(
+        grads,
+        pltpu.VMEM((4 * rows, model), bf16),
+        pltpu.VMEM((2, 4 * rows, model), bf16),
+        pltpu.VMEM((4, depth, model), bf16),
+        pltpu.VMEM((3, 3, depth, model), bf16),
+        pltpu.VMEM((3, depth, model), f32),
+        pltpu.VMEM((2, depth, model), bf16),
+    )
+    for d in range(3):
+        backs[d].wait_recv()
+        back_out[...] += back_land[d].astype(f32)
+    tops.on(5)
+    top_out[...] = blocks[5]
+    y_copy.wait_recv()
+    row.finish()
+    t.finish()
+
+
+def feed_forward_parts(
+    t, row, tops, backs,
     h_ref, dy_ref, dy_rest, gate_ref, up_ref, down_own, down_rest,
     hid_out, dg_out, du_out, h_out, y_out, y_rest, back_out,
     gates, ups, downs, hs, dys, y_acc, back_acc, back_send, back_land, y_send, stage,
-    load_sem, down_sem, dy_sem, h_sem, stage_sem, y_sem, row_send, row_recv, send, recv,
+    load_sem, down_sem, dy_sem, h_sem, stage_sem, y_sem,
 ):
     rows, model = h_ref.shape
     tiles = gates.shape[0]
@@ -846,14 +1030,14 @@
     width = down_own.shape[1]
 
     def tile_loads(i, slot):
-        cols = pl.ds(pl.multiple_of(i * TILE, TILE), TILE)
+        cols = stretch(i, TILE)
         copies = [
             pltpu.make_async_copy(gate_ref.at[:, cols], gates.at[i], load_sem.at[0, i]),
             pltpu.make_async_copy(up_ref.at[:, cols], ups.at[i], load_sem.at[1, i]),
         ]
-        own_rows = pl.ds(pl.multiple_of(place * tiles * TILE + i * TILE, TILE), TILE)
+        own_rows = stretch(place * tiles + i, TILE)
         for d in range(4):
-            cols = pl.ds(pl.multiple_of(flip(place, d) * width, width), width)
+            cols = stretch(flip(place, d), width)
             src = down_own.at[own_rows] if d == 0 else down_rest.at[d - 1, slot]
             copies.append(pltpu.make_async_copy(src, downs.at[i, :, cols], down_sem.at[i, d]))
         return copies
@@ -868,15 +1052,11 @@
             load.start()
     for load in dy_copies[1:]:
         load.start()
-    greet((), (1, 2, 3))
-    t = Transfers(send, recv)
-    row = RowGather(h_ref, [None] + [hs.at[d] for d in range(3)], row_send, row_recv)
-    row.begin()
     dy_copies[0].wait()
 
     def stage_copy(slot, k, part, i):
         out = (hid_out, dg_out, du_out)[k]
-        cols = pl.ds(pl.multiple_of(i * TILE, TILE), TILE)
+        cols = stretch(i, TILE)
         return pltpu.make_async_copy(
             stage.at[slot, k], out.at[pl.ds(part * rows, rows), cols], stage_sem.at[slot, k]
         )
@@ -932,11 +1112,15 @@
         return pltpu.make_async_copy(h, h_out.at[pl.ds(part * rows, rows)], h_sem.at[part])
 
     keep_h(0, h_ref).start()
+    tops.on(0)
     chunk(0, h_ref)
-    y_out[...] = y_acc[...]
+    y_copy = pltpu.make_async_copy(y_acc, y_out, y_sem.at[3])
+    y_copy.start()
     back_out[...] = back_acc[...]
     row.first()
-    backs, y_copy = [], None
+    tops.on(1)
+    y_copy.wait()
+    y_copy = None
     for part in (1, 2, 3):
         h = hs.at[part - 1]
         if part == 2:
@@ -947,151 +1131,34 @@
         dy_copies[part].wait()
         chunk(part, h)
         back_send[part - 1] = back_acc[...].astype(bf16)
-        backs.append(t.start(back_send.at[part - 1], back_land.at[part - 1], fsdp=part))
+        backs.append(
+            t.start((back_send, part - 1), (back_land, part - 1), fsdp=part, now=part > 1)
+        )
+        if part != 2:
+            @pl.when(row.inner == (part == 3))
+            def _():
+                backs[0].made().start()
+
         if y_copy is not None:
             y_copy.wait()
         y_send[...] = y_acc[...].astype(bf16)
         y_copy = pltpu.make_async_copy(y_send, y_rest.at[part - 1], y_sem.at[part - 1])
         y_copy.start()
+        tops.on(part + 1)
     y_copy.wait()
     for part in range(4):
         keep_h(part, h_ref if part == 0 else hs.at[part - 1]).wait()
-    for d in range(3):
-        backs[d].wait_recv()
-        back_out[...] += back_land[d].astype(f32)
-    row.finish()
-    t.finish()
-
-
-def feed_forward_row(h, dy, dy_rest, gate, up, down_own, down_rest):
-    rows, model = h.shape
-    units = gate.shape[1]
-    tiles = units // TILE
-    wide = jax.ShapeDtypeStruct((4 * rows, units), bf16)
-    block = pltpu.VMEM((rows, model), f32)
-    dma = pltpu.SemaphoreType.DMA
-    return remote_call(
-        feed_forward_row_body,
-        [wide, wide, wide, jax.ShapeDtypeStruct((4 * rows, model), bf16)]
-        + [jax.ShapeDtypeStruct((rows, model), f32), jax.ShapeDtypeStruct((3, rows, model), bf16)]
-        + [jax.ShapeDtypeStruct((rows, model), f32)],
-        [ANY] * 4 + [VMEM, ANY, VMEM],
-        [VMEM] + [ANY] * 6,
-        [
-            pltpu.VMEM((tiles, model, TILE), bf16),
-            pltpu.VMEM((tiles, model, TILE), bf16),
-            pltpu.VMEM((tiles, TILE, model), bf16),
-            pltpu.VMEM((3, rows, model), bf16),
-            pltpu.VMEM((4, rows, model), bf16),
-            block,
-            block,
-            pltpu.VMEM((3, rows, model), bf16),
-            pltpu.VMEM((3, rows, model), bf16),
-            pltpu.VMEM((rows, model), bf16),
-            pltpu.VMEM((2, 3, rows, TILE), bf16),
-            dma((2, tiles)),
-            dma((tiles, 4)),
-            dma((4,)),
-            dma((4,)),
-            dma((2, 3)),
-            dma((3,)),
-            dma((5,)),
-            dma((3,)),
-        ],
-        3,
-        2,
-        flops=48 * rows * model * units,
-    )(h, dy, dy_rest, gate, up, down_own, down_rest)
-
-
-class SmallReduce:
-    MASKS = ((0, 1), (0, 2), (2, 0), (4, 0), (1, 0))
-
-    def __init__(self, transfers, blocks, land, join):
-        self.t, self.blocks, self.land, self.join = transfers, blocks, land, join
-
-    def begin(self, step):
-        ctx, fsdp = self.MASKS[step]
-        self.copy = self.t.start(self.blocks.at[step], self.land.at[step], ctx=ctx, fsdp=fsdp)
-
-    def end(self, step):
-        self.copy.wait_recv()
-        self.blocks[step + 1] = self.join(self.blocks[step], self.land[step])
-
-    def on(self, step):
-        if 0 <= step - 1 < 5:
-            self.end(step - 1)
-        if step < 5:
-            self.begin(step)
-
-
-def small_scratch(shape):
-    return [pltpu.VMEM((6,) + shape, f32), pltpu.VMEM((5,) + shape, f32)]
-
-
-class PlaneSum:
-    def __init__(self, transfers, cores, far, near, sums, total):
-        self.t, self.cores, self.far, self.near = transfers, cores, far, near
-        self.sums, self.total = sums, total
-        self.half = cores.shape[1] // 2
-        self.over = {}
-
-    def send_odd(self, j, src):
-        self.over[j - 1] = self.t.start(src, self.cores.at[(j - 1) // 2], ctx=1)
-        return self.over[j - 1]
-
-    def even(self, j, value):
-        t, h = self.t, self.half
-        self.over[j].wait_recv()
-        value = value + self.cores[j // 2].astype(f32)
-        if j == 0:
-            self.total[...] = value
-            return
-        out = self.sums.at[(6, 2, 4).index(j)]
-        out[...] = value.astype(bf16)
-        if j == 6:
-            self.x6 = t.start(out.at[:h], self.far.at[:h], ctx=2)
-            self.y6 = t.start(out.at[h:], self.far.at[h:], ctx=4)
-        elif j == 2:
-            self.x2 = t.start(out.at[:h], self.near.at[0, :h], ctx=2)
-        else:
-            self.y4 = t.start(out.at[h:], self.near.at[1, h:], ctx=4)
-
-    def pass_on(self):
-        t, h = self.t, self.half
-        two, four = self.sums.at[1], self.sums.at[2]
-        self.y6.wait_recv()
-        two[h:] = (two[h:].astype(f32) + self.far[h:].astype(f32)).astype(bf16)
-        self.x2b = t.start(two.at[h:], self.near.at[0, h:], ctx=2)
-        self.x6.wait_recv()
-        four[:h] = (four[:h].astype(f32) + self.far[:h].astype(f32)).astype(bf16)
-        self.y4b = t.start(four.at[:h], self.near.at[1, :h], ctx=4)
-
-    def close(self):
-        for copy in (self.x2, self.x2b, self.y4, self.y4b):
-            copy.wait_recv()
-        return self.total[...] + self.near[0].astype(f32) + self.near[1].astype(f32)
-
-
-def plane_sum_scratch(count, *shape):
-    return [
-        pltpu.VMEM((count, 4) + shape, bf16),
-        pltpu.VMEM((count,) + shape, bf16),
-        pltpu.VMEM((count, 2) + shape, bf16),
-        pltpu.VMEM((count, 3) + shape, bf16),
-        pltpu.VMEM((count,) + shape, f32),
-    ]
-
-
-def grads_body(
-    h_ref, dg_ref, du_ref, hid_ref, dy_ref, dy_rest, y_rest, top_ref,
-    gate_out, up_out, down_out, y_land, top_out,
-    left, rights, odd, cores, far, near, sums, totals, left_sem, right_sem, dy_sem, out_sem,
-    blocks, land, send, recv,
+
+
+def feed_forward_grads(
+    t, h_ref, dg_ref, du_ref, hid_ref, dy_ref, dy_rest,
+    gate_out, up_out, down_out,
+    left, rights, odd, cores, far, near, sums, totals, fetched,
+    left_sem, right_sem, dy_sem, core_sem, out_sem,
 ):
     me = lax.axis_index("ctx")
     rows = dy_ref.shape[0]
-    depth = cores.shape[2]
+    depth = far.shape[1]
     dys = [dy_ref] + [dy_rest.at[d] for d in range(3)]
     right_copies = [
         [pltpu.make_async_copy(dg_ref, rights.at[0], right_sem.at[0])],
@@ -1108,12 +1175,6 @@
     left_copies[0].start()
     right_copies[0][0].start()
     right_copies[1][0].start()
-    greet((1, 2, 4), (1, 2, 3))
-    t = Transfers(send, recv)
-    tops = SmallReduce(t, blocks, land, jnp.maximum)
-    blocks[0] = top_ref[...]
-    tops.on(0)
-    y_copies = []
     left_copies[0].wait()
     jobs, odd_copies, outs = [], {}, []
 
@@ -1124,7 +1185,9 @@
         outs.append(out)
 
     for k in range(3):
-        job = PlaneSum(t, cores.at[k], far.at[k], near.at[k], sums.at[k], totals.at[k])
+        job = PlaneSum(
+            t, cores.at[k], far.at[k], near.at[k], sums.at[k], totals.at[k], (fetched, core_sem)
+        )
         jobs.append(job)
         if k == 2:
             for copy in [left_copies[1]] + right_copies[2]:
@@ -1134,61 +1197,73 @@
             copy.wait()
 
         def partial(j):
-            block = pl.ds(pl.multiple_of(flip(me, j) * depth, depth), depth)
+            block = stretch(flip(me, j), depth)
             return lax.dot_general(
                 left[:, block], rights[k % 2], OVER_ROWS, preferred_element_type=f32
             )
 
-        for i, j in enumerate((7, 5, 3, 1)):
+        for j in (7, 5, 3, 1):
             if j in odd_copies:
                 t.release(odd_copies[j])
             odd[j // 2] = partial(j).astype(bf16)
             odd_copies[j] = job.send_odd(j, odd.at[j // 2])
-            if k == 0:
-                tops.on(i + 1)
-            if k == 0 and i == 0:
-                for d in (1, 2, 3):
-                    y_copies.append(t.start(y_rest.at[d - 1], y_land.at[d - 1], fsdp=d))
         if k:
             jobs[k - 1].pass_on()
         for j in (6, 2, 4, 0):
+            job.arrive(j)
             job.even(j, partial(j))
         if k:
             close(k - 1)
-    tops.on(5)
-    top_out[...] = blocks[5]
     jobs[2].pass_on()
-    for copy in y_copies:
-        copy.wait_recv()
     down_out[...] = jobs[2].close().astype(bf16)
     for copy in outs:
         copy.wait()
-    t.finish()
-
-
-def grads_row(h, dg, du, hid, dy, dy_rest, y_rest, top):
-    rows, model = dy.shape
+
+
+def feed_forward_row(h, dy, dy_rest, gate, up, down_own, down_rest, top):
+    rows, model = h.shape
+    units = gate.shape[1]
+    tiles = units // TILE
     depth = model // 8
+    wide = jax.ShapeDtypeStruct((4 * rows, units), bf16)
+    low = jax.ShapeDtypeStruct((rows, model), bf16)
+    high = jax.ShapeDtypeStruct((rows, model), f32)
+    summed = jax.ShapeDtypeStruct((depth, units), f32)
     dma = pltpu.SemaphoreType.DMA
-    summed = jax.ShapeDtypeStruct((depth, dg.shape[1]), f32)
     return remote_call(
-        grads_body,
-        [summed, summed, jax.ShapeDtypeStruct((depth, model), bf16), jax.ShapeDtypeStruct(y_rest.shape, bf16)]
-        + [jax.ShapeDtypeStruct(top.shape, f32)],
-        [ANY, ANY, VMEM, ANY, VMEM],
-        [ANY] * 7 + [VMEM],
+        feed_forward_row_body,
+        [wide, wide, wide, jax.ShapeDtypeStruct((4 * rows, model), bf16)]
+        + [high, jax.ShapeDtypeStruct((3, rows, model), bf16), high]
+        + [jax.ShapeDtypeStruct((3, 4, depth, model), bf16), low, summed, summed]
+        + [jax.ShapeDtypeStruct((depth, model), bf16), jax.ShapeDtypeStruct(top.shape, f32)],
+        [ANY] * 6 + [VMEM] + [ANY] * 4 + [VMEM] * 2,
+        [VMEM] + [ANY] * 6 + [VMEM],
         [
-            pltpu.VMEM(h.shape, bf16),
-            pltpu.VMEM((2,) + h.shape, bf16),
-            pltpu.VMEM((4, depth, model), bf16),
+            pltpu.VMEM((3, rows, model), bf16),
+            pltpu.VMEM((3, rows, model), bf16),
+            pltpu.VMEM((3, rows, model), bf16),
+            pltpu.VMEM((3, depth, model), bf16),
+            pltpu.VMEM((3, 2, depth, model), bf16),
         ]
-        + plane_sum_scratch(3, depth, model)
-        + [dma((2,)), dma((2,)), dma((4,)), dma((2,))]
-        + small_scratch(top.shape),
-        3 + 3 * 10 + 5,
-        3,
-        flops=6 * h.shape[0] * model * model,
-    )(h, dg, du, hid, dy, dy_rest, y_rest, top)
+        + small_scratch(top.shape)
+        + [
+            dma((2, tiles)),
+            dma((tiles, 4)),
+            dma((4,)),
+            dma((4,)),
+            dma((2, 3)),
+            dma((4,)),
+            dma((2,)),
+            dma((2,)),
+            dma((2,)),
+            dma((2,)),
+            dma((5,)),
+            dma((3,)),
+        ],
+        3 + 5 + 1 + 3 * 10,
+        2,
+        flops=54 * rows * model * units,
+    )(h, dy, dy_rest, gate, up, down_own, down_rest, top)
 
 
 class RowSum:
@@ -1209,8 +1284,8 @@
 
 def attention_back_body(
     db_ref, attended_ref, qkv_ref, cosine_ref, sine_ref, natural_ref, begin_ref, key_natural_ref,
-    kv_ref, o_ref, output_rest,
-    dq_out, dkv_out, output_out,
+    kv_ref, o_ref, output_rest, y_ref,
+    dq_out, dkv_out, output_out, y_land,
     kvs, o_own, outputs, head_grad, odd,
     cores, far, near, sums, totals,
     kv_cores, kv_far, kv_near, kv_sums, kv_totals,
@@ -1238,6 +1313,7 @@
     def shard(d):
         return pl.ds(pl.multiple_of(flip(place, d) * width, width), width)
 
+    y_copy = t.start(y_ref.at[1], y_land, fsdp=2)
     job = PlaneSum(t, cores.at[0], far.at[0], near.at[0], sums.at[0], totals.at[0])
 
     def partial(j):
@@ -1249,6 +1325,7 @@
         odd[j // 2] = partial(j).astype(bf16)
         job.send_odd(j, odd.at[j // 2])
     for j in (6, 2, 4, 0):
+        job.arrive(j)
         job.even(j, partial(j))
 
     loads[0].wait()
@@ -1311,6 +1388,7 @@
         for j in (7, 3, 5, 1):
             kv_jobs[k].send_odd(j, kvs.at[half, j])
         for j in (6, 2, 4, 0):
+            kv_jobs[k].arrive(j)
             kv_jobs[k].even(j, kvs[half, j].astype(f32))
 
     def take_half(k):
@@ -1338,10 +1416,11 @@
     take_half(0)
     output_out[...] = row.close()
     take_half(1)
+    y_copy.wait_recv()
     t.finish()
 
 
-def attention_back(db, attended, qkv, cosine, sine, natural, begin, key_natural, kv, output, output_rest):
+def attention_back(db, attended, qkv, cosine, sine, natural, begin, key_natural, kv, output, output_rest, y_rest):
     rows, model = db.shape
     depth, width = model // 8, output.shape[1]
     kv_width = kv.shape[3]
@@ -1351,9 +1430,10 @@
             jax.ShapeDtypeStruct((rows, model), bf16),
             jax.ShapeDtypeStruct((rows, 4 * kv_width), bf16),
             jax.ShapeDtypeStruct((depth, width), f32),
+            jax.ShapeDtypeStruct((rows, model), bf16),
         ],
-        [VMEM] * 3,
-        [VMEM] * 8 + [ANY] * 3,
+        [VMEM] * 3 + [ANY],
+        [VMEM] * 8 + [ANY] * 4,
         [
             pltpu.VMEM(kv.shape, bf16),
             pltpu.VMEM(output.shape, bf16),
@@ -1365,15 +1445,15 @@
         + plane_sum_scratch(2, 2, rows, kv_width)
         + [pltpu.VMEM((3, depth, width), bf16)] * 2
         + [pltpu.SemaphoreType.DMA((3,))],
-        3 * 10 + 3,
+        3 * 10 + 3 + 1,
         4,
         flops=20 * rows * model * model,
-    )(db, attended, qkv, cosine, sine, natural, begin, key_natural, kv, output, output_rest)
+    )(db, attended, qkv, cosine, sine, natural, begin, key_natural, kv, output, output_rest, y_rest)
 
 
 def unit_grads_body(
-    h_ref, dq_ref, dkv_ref, x_ref, term_ref, q_ref, k_ref, v_ref, unit_rest,
-    query_out, key_out, value_out, back_out, gain_out,
+    h_ref, dq_ref, dkv_ref, x_ref, term_ref, q_ref, k_ref, v_ref, unit_rest, y_ref,
+    query_out, key_out, value_out, back_out, gain_out, y_land,
     odd, q_own, k_own, v_own, units, cores, far, near, sums, totals, row_send, row_land,
     blocks, land, load_sem, unit_sem, send, recv,
 ):
@@ -1392,6 +1472,7 @@
         load.start()
     greet((1, 2, 4), (1, 2, 3))
     t = Transfers(send, recv)
+    y_copy = t.start(y_ref.at[2], y_land, fsdp=3)
     jobs, odd_copies = [], {}
 
     def of_slot(j):
@@ -1412,6 +1493,7 @@
             odd[j // 2] = partial(j).astype(bf16)
             odd_copies[j] = job.send_odd(j, odd.at[j // 2])
         for j in (6, 2, 4, 0):
+            job.arrive(j)
             job.even(j, partial(j))
 
     def grads(d):
@@ -1448,7 +1530,9 @@
     back(3)
     x = x_ref[...].astype(f32)
     unit = x * lax.rsqrt(jnp.mean(x * x, 1, keepdims=True) + epsilon)
-    gains = SmallReduce(t, blocks, land, jnp.add)
+    gains = SmallReduce(
+        t, blocks, land, jnp.add, ((0, 1), (0, 2), (2, 0), (4, 0), (1, 0))
+    )
     blocks[0] = jnp.concatenate(
         [jnp.sum(back_out[...] * unit, 0, keepdims=True), term_ref[1:8]], 0
     )
@@ -1474,10 +1558,11 @@
         here = slice(h * HEAD_SIZE, (h + 1) * HEAD_SIZE)
         key_out[:, here] = total[:, start : start + HEAD_SIZE]
         value_out[:, here] = total[:, start + HEAD_SIZE : start + 2 * HEAD_SIZE]
+    y_copy.wait_recv()
     t.finish()
 
 
-def unit_grads(h, dq, dkv, x, terms, query, key, value, rest):
+def unit_grads(h, dq, dkv, x, terms, query, key, value, rest, y_rest):
     rows, model = h.shape
     depth, width = model // 8, model // 4
     wide = jax.ShapeDtypeStruct((depth, width), f32)
@@ -1486,9 +1571,9 @@
     return remote_call(
         unit_grads_body,
         [wide, half, half, jax.ShapeDtypeStruct((rows, model), f32)]
-        + [jax.ShapeDtypeStruct(terms.shape, f32)],
-        [VMEM] * 5,
-        [VMEM] * 5 + [ANY] * 4,
+        + [jax.ShapeDtypeStruct(terms.shape, f32), jax.ShapeDtypeStruct((rows, model), bf16)],
+        [VMEM] * 5 + [ANY],
+        [VMEM] * 5 + [ANY] * 5,
         [
             pltpu.VMEM((4, depth, model), bf16),
             pltpu.VMEM(query.shape, bf16),
@@ -1500,10 +1585,10 @@
         + [pltpu.VMEM((2, 3, depth, width), bf16)] * 2
         + small_scratch(terms.shape)
         + [dma((3,)), dma((3,))],
-        2 * (10 + 3) + 5,
+        2 * (10 + 3) + 5 + 1,
         5,
         flops=12 * rows * model * model,
-    )(h, dq, dkv, x, terms, query, key, value, rest)
+    )(h, dq, dkv, x, terms, query, key, value, rest, y_rest)
 
 
 def token_layout(length_row, block_slots, block_size):
@@ -1851,19 +1936,24 @@
     top = jnp.max(best[:, :, :REPEAT, 0], 0)
     top = jnp.pad(top, ((0, 0), (0, 128 - REPEAT)))
 
-    hid, dg, du, h_all, y_own, y_rest, grad_normed_two = feed_forward_row(
-        normed_two, grad_out, dy_rest, gate_weight, up_weight, down_weight, down_rest
-    )
+    _, _, _, _, y_own, y_rest, grad_normed_two, _, y_near, gate_grad, up_grad, down_sum, top = (
+        feed_forward_row(
+            normed_two,
+            grad_out,
+            dy_rest,
+            gate_weight,
+            up_weight,
+            down_weight,
+            down_rest,
+            top,
+        )
+    )
+    head_max = top[:, :REPEAT].reshape(QUERY_HEADS)
     second_term = jnp.sum(grad_normed_two * unit_two, 0)
     grad_residual = grad_out.astype(f32) + norm_back(
         grad_normed_two * second_full, unit_two, scale_two
     )
     grad_branch = grad_residual.astype(bf16)
-    gate_grad, up_grad, down_sum, y_land, top = grads_row(
-        h_all, dg, du, hid, grad_out, dy_rest, y_rest, top
-    )
-    head_max = top[:, :REPEAT].reshape(QUERY_HEADS)
-    result = (residual + y_own + jnp.sum(y_land.astype(f32), 0)).astype(bf16)
     width = model // 4
     moved, pieces = [], []
     for k in range(4):
@@ -1877,7 +1967,7 @@
         moved.append(lax.ppermute(piece, ("ctx", "fsdp"), pairs))
     down_grad = jnp.concatenate(by_place(moved, place), 0).astype(f32)
 
-    query_grad, dkv, output_out = attention_back(
+    query_grad, dkv, output_out, y_second = attention_back(
         grad_branch,
         attended,
         qkv,
@@ -1889,9 +1979,10 @@
         kv_all,
         output_weight,
         output_rest,
+        y_rest,
     )
     terms = jnp.pad(second_term[None], ((1, 6), (0, 0)))
-    query_out, key_out, value_out, grad_normed_one, terms = unit_grads(
+    query_out, key_out, value_out, grad_normed_one, terms, y_third = unit_grads(
         normalized,
         query_grad,
         dkv,
@@ -1901,7 +1992,10 @@
         key_matrix,
         value_matrix,
         unit_rest,
-    )
+        y_rest,
+    )
+    landed = y_near.astype(f32) + y_second.astype(f32) + y_third.astype(f32)
+    result = (residual + y_own + landed).astype(bf16)
     grad_input = grad_residual + norm_back(grad_normed_one * first_full, unit_one, scale_one)
     terms = lax.dynamic_slice_in_dim(
         terms[:2], (me * 4 + place) * (model // 32), model // 32, 1

time: 738 us -> 677 us (0.917)
  Pallas kernels: 674 us -> 616 us
    pallas_call x1 -> x0, Pallas kernels: 130 us -> none  [grads_row(): remote_call(grads_body, [summed, summed, jax.ShapeDtypeStruct((depth, mod...]
    pallas_call x1, Pallas kernels: 156 us -> 229 us  [feed_forward_row(): remote_call(feed_forward_row_body, [wide, wide, wide, jax.ShapeDtypeStruc...]
  transfers between devices with their start and end apart: 4 -> 4, of which waited for: 0 -> 0; matrix products, arithmetic and copies ran while one was open for 3% -> 3% of each run, Pallas kernels for 29% -> 31%
where the time goes in v5:
time: 677 us; the launch traced here: 667 us
  Pallas kernels  616 us (91%)
  other arithmetic  26.3 us (4%)
  local copies, waits for them, and re-layouts  15.6 us (2%)
  starting transfers between devices  7.84 us (1%)
    pallas_call x1, Pallas kernels, feed_forward_row(): remote_call(feed_forward_row_body, [wide, wide, wide, jax.ShapeDtypeStruc...  229 us
    pallas_call x1, Pallas kernels, attention_row(): remote_call(attention_row_body, [out((rows, model)), out((rows, 4 * width...  180 us
    pallas_call x1, Pallas kernels, unit_grads(): remote_call(unit_grads_body, [wide, half, half, jax.ShapeDtypeStruct((row...  122 us
    pallas_call x1, Pallas kernels, attention_back(): remote_call(attention_back_body, [jax.ShapeDtypeStruct((rows, model), bf1...  85.1 us
  transfers between devices with their start and end apart: 4, of which 0 were waited for; matrix products, arithmetic and copies ran while one was open for 3% of the time, Pallas kernels for 31%

profile of v5, /device:TPU:0, one launch (start us, length us, event | category | flops | bytes accessed | tf_op | source)
XLA Modules:
  0.0 667.1 jit_solution(10406023076404409994)
XLA Ops:
  0.7 1.3 iota_reduce_fusion
  2.1 0.8 reduce-window.4
  3.6 0.7 stack.36
  4.3 0.7 stack.37
  5.3 0.8 copy.54.begin_ref
  6.1 0.8 copy.53.natural_ref
  8.0 0.8 pad_maximum_fusion
  9.5 180.2 %shard_map.245 = (bf16[256,2048]{1,0:T(8,128)(2,1)}, bf16[256,4096]{1,0:T(8,128)(2,1)}, bf16[256,2048]{1,0:T(8,128)(2,1)}, f32[2,8,8,128]{3,2,1,0:T(8,128)}, f32...) custom-call(bf16[256,2048]{1,0:T(8,128)(2,1)} %bitcast.65, ...), custom_call_target="tpu_custom_call" | custom-call | flops 10737418240 | bytes 4194304 | tf_op jit(solution)/shard_map/pallas_call | solution.py:815
  189.7 0.9 slice_reduce_fusion
  191.3 229.0 %shard_map.246 = (bf16[1024,2048]{1,0:T(8,128)(2,1)}, bf16[1024,2048]{1,0:T(8,128)(2,1)}, bf16[1024,2048]{1,0:T(8,128)(2,1)}, bf16[1024,2048]{1,0:T(8,128)(2,1)}...) custom-call(bf16[256,2048]{1,0:T(8,128)(2,1)} %get-tuple-element.52., ...), custom_call_target="tpu_custom_call" | custom-call | flops 57982058496 | bytes 4194304 | tf_op jit(solution)/shard_map/pallas_call | solution.py:1233
  420.3 2.2 constant_dynamic-slice_fusion.1
  422.6 4.0 collective-permute-start
  426.6 1.9 collective-permute-start.1
  429.0 1.4 collective-permute-start.3
  431.3 2.2 multiply_reduce_fusion
  434.4 2.5 multiply_convert_fusion.1
  437.0 1.6 fusion.26.db_ref
  438.6 85.1 %shard_map.247 = (bf16[256,2048]{1,0:T(8,128)(2,1)}, bf16[256,2048]{1,0:T(8,128)(2,1)}, f32[256,512]{1,0:T(8,128)}, bf16[256,2048]{1,0:T(8,128)(2,1)}) custom-call(bf16[256,2048]{1,0:T(8,128)(2,1)} %fusion.26.db_ref, bf16[256,2048]{1,0:T(8,128)(2,1)} %get-tuple-element.62.attended_ref, bf16[256,4096]{1,0:T(8,128)(2,1)} %get-tuple-element.63.qkv_ref, ...), custom_call_target="tpu_custom_call" | custom-call | flops 21474836480 | bytes 4194304 | tf_op jit(solution)/shard_map/pallas_call | solution.py:1427
  523.7 121.6 %shard_map.248 = (f32[256,512]{1,0:T(8,128)}, f32[256,256]{1,0:T(8,128)}, f32[256,256]{1,0:T(8,128)}, f32[256,2048]{1,0:T(8,128)}, f32[8,2048]{1,0:T(8,128)}, /*index=5*/bf16[256,2048]{1,0:T(8,128)(2,1)}) custom-call(bf16[256,2048]{1,0:T(8,128)(2,1)} %get-tuple-element.68.h_ref, bf16[256,2048]{1,0:T(8,128)(2,1)} %get-tuple-element.69.dq_ref, ...), custom_call_target="tpu_custom_call" | custom-call | flops 12884901888 | bytes 4194304 | tf_op jit(solution)/shard_map/pallas_call | solution.py:1571
  645.4 2.2 fusion.2
  647.6 0.8 slice.88
  648.5 1.8 multiply_convert_fusion
  650.5 6.0 fusion.9
  657.1 1.3 broadcast_select_fusion.7
  658.4 1.6 maximum_convert_fusion
  660.0 0.8 copy.63
  660.8 0.7 copy.64
  661.5 0.7 copy.65
  662.2 0.8 copy.66
  663.0 1.3 copy.67
  664.3 1.0 copy-done.6
  665.3 1.3 copy.68
  (71 shorter events, 6.6 us)
Async XLA Ops:
  191.3 239.1 %copy-start.3 = (bf16[1,256,2048]{2,1,0:T(8,128)(2,1)S(1)}, bf16[1,256,2048]{2,1,0:T(8,128)(2,1)}, u32[]{:S(2)}) copy-start(bf16[1,256,2048]{2,1,0:T(8,128)(2,1)} %param.14) | copy-start | bytes 3145732
  420.3 10.5 %copy-start = (f32[256,2048]{1,0:T(8,128)S(1)}, f32[256,2048]{1,0:T(8,128)}, u32[]{:S(2)}) copy-start(f32[256,2048]{1,0:T(8,128)} %get-tuple-element.51) | copy-start | bytes 6291460
  422.5 8.4 %copy-start.14 = (f32[8,128]{1,0:T(8,128)S(1)}, f32[8,128]{1,0:T(8,128)}, u32[]{:S(2)}) copy-start(f32[8,128]{1,0:T(8,128)} %get-tuple-element.85) | copy-start | bytes 12292
  422.5 8.5 %copy-start.16 = (f32[16]{0:T(128)S(1)}, f32[16]{0:T(128)}, u32[]{:S(2)}) copy-start(f32[16]{0:T(128)} %param.27) | copy-start | bytes 196
  422.6 8.7 %copy-start.13 = (f32[4,8,512]{2,1,0:T(8,128)S(1)}, f32[4,8,512]{2,1,0:T(8,128)}, u32[]{:S(2)}) copy-start(f32[4,8,512]{2,1,0:T(8,128)} %get-tuple-element.59) | copy-start | bytes 196612
  422.6 234.5 %collective-permute-start = (bf16[256,512]{1,0:T(8,128)(2,1)}, bf16[256,512]{1,0:T(8,128)(2,1)}, u32[]{:S(2)}, u32[]{:S(2)}) collective-permute-start(bf16[256,512]{1,0:T(8,128)(2,1)} %get-tuple-element.81), channel_id=1, source_target_pairs={{0,3},{1,11},{2,19},{3,27},{4,2},{5,10},{6,18},{7,26},{8,1},{9,9},... | collective-permute-start | bytes 786440 | tf_op jit(solution)/shard_map/ppermute | solution.py:1967
  426.6 230.5 %collective-permute-start.1 = (bf16[256,512]{1,0:T(8,128)(2,1)}, bf16[256,512]{1,0:T(8,128)(2,1)}, u32[]{:S(2)}, u32[]{:S(2)}) collective-permute-start(bf16[256,512]{1,0:T(8,128)(2,1)} %get-tuple-element.82), channel_id=1, source_target_pairs={{0,2},{1,10},{2,18},{3,26},{4,3},{5,11},{6,19},{7,27},{8,0},{9,8},... | collective-permute-start | bytes 786440 | tf_op jit(solution)/shard_map/ppermute | solution.py:1967
  428.5 228.6 %collective-permute-start.2 = (bf16[256,512]{1,0:T(8,128)(2,1)}, bf16[256,512]{1,0:T(8,128)(2,1)}, u32[]{:S(2)}, u32[]{:S(2)}) collective-permute-start(bf16[256,512]{1,0:T(8,128)(2,1)} %get-tuple-element.83), channel_id=1, source_target_pairs={{0,1},{1,9},{2,17},{3,25},{4,0},{5,8},{6,16},{7,24},{8,3},{9,11},{... | collective-permute-start | bytes 786440 | tf_op jit(solution)/shard_map/ppermute | solution.py:1967
  429.0 228.0 %collective-permute-start.3 = (bf16[256,512]{1,0:T(8,128)(2,1)S(1)}, bf16[256,512]{1,0:T(8,128)(2,1)}, u32[]{:S(2)}, u32[]{:S(2)}) collective-permute-start(bf16[256,512]{1,0:T(8,128)(2,1)S(1)} %get-tuple-element.84), channel_id=1, source_target_pairs={{0,0},{1,8},{2,16},{3,24},{4,1},{5,9},{6,17},{7,25},{8,2},{9,10},{... | collective-permute-start | bytes 786440 | tf_op jit(solution)/shard_map/ppermute | solution.py:1967
  431.1 2.5 copy-start.15
  431.3 5.7 copy-start.5
  434.4 2.6 copy-start.2
  523.7 121.6 %copy-start.4 = (bf16[1,256,2048]{2,1,0:T(8,128)(2,1)S(1)}, bf16[1,256,2048]{2,1,0:T(8,128)(2,1)}, u32[]{:S(2)}) copy-start(bf16[1,256,2048]{2,1,0:T(8,128)(2,1)} %param.14) | copy-start | bytes 3145732
  645.4 3.1 copy-start.8
  648.5 2.0 copy-start.1
  658.3 1.7 copy-start.10
  658.4 2.4 copy-start.12
  658.4 3.1 copy-start.11
  658.4 3.8 copy-start.9
  660.0 3.0 copy-start.7
  663.0 2.3 copy-start.6

commit v6 on v5

--- a/solution.py
+++ b/solution.py
@@ -852,6 +852,9 @@
     )(x, gains, cosine, sine, natural, begin, key_natural, query, key, value, output, down, dy)
 
 
+SLOTS = (7, 3, 6, 5, 2, 1, 4, 0)
+
+
 class SmallReduce:
     def __init__(self, transfers, blocks, land, join, masks):
         self.t, self.blocks, self.land, self.join = transfers, blocks, land, join
@@ -1002,10 +1005,10 @@
         grads,
         pltpu.VMEM((4 * rows, model), bf16),
         pltpu.VMEM((2, 4 * rows, model), bf16),
-        pltpu.VMEM((4, depth, model), bf16),
-        pltpu.VMEM((3, 3, depth, model), bf16),
-        pltpu.VMEM((3, depth, model), f32),
-        pltpu.VMEM((2, depth, model), bf16),
+        pltpu.VMEM((4, depth, model // 2), bf16),
+        pltpu.VMEM((6, 3, depth, model // 2), bf16),
+        pltpu.VMEM((6, depth, model // 2), f32),
+        pltpu.VMEM((2, depth, model // 2), bf16),
     )
     for d in range(3):
         backs[d].wait_recv()
@@ -1176,46 +1179,62 @@
     right_copies[0][0].start()
     right_copies[1][0].start()
     left_copies[0].wait()
+    half = far.shape[2]
+    count = far.shape[0]
     jobs, odd_copies, outs = [], {}, []
 
-    def close(k):
-        totals[k] = jobs[k].close()
-        out = pltpu.make_async_copy(totals.at[k], (gate_out, up_out)[k], out_sem.at[k])
-        out.start()
-        outs.append(out)
-
-    for k in range(3):
+    def close(n):
+        cols = slice((n % 2) * half, (n % 2 + 1) * half)
+        if n < 4:
+            totals[n] = jobs[n].close()
+            out = pltpu.make_async_copy(
+                totals.at[n], (gate_out, up_out)[n // 2].at[:, cols], out_sem.at[n]
+            )
+            out.start()
+            outs.append(out)
+        else:
+            down_out[:, cols] = jobs[n].close().astype(bf16)
+
+    for n in range(count):
+        k = n // 2
+        cols = slice((n % 2) * half, (n % 2 + 1) * half)
         job = PlaneSum(
-            t, cores.at[k], far.at[k], near.at[k], sums.at[k], totals.at[k], (fetched, core_sem)
+            t, cores.at[n], far.at[n], near.at[n], sums.at[n], totals.at[n], (fetched, core_sem)
         )
         jobs.append(job)
-        if k == 2:
-            for copy in [left_copies[1]] + right_copies[2]:
+        if n == 2:
+            for copy in right_copies[2]:
                 copy.start()
+        if n == 4:
+            left_copies[1].start()
             left_copies[1].wait()
-        for copy in right_copies[k]:
-            copy.wait()
+        if n % 2 == 0:
+            for copy in right_copies[k]:
+                copy.wait()
 
         def partial(j):
-            block = stretch(flip(me, j), depth)
             return lax.dot_general(
-                left[:, block], rights[k % 2], OVER_ROWS, preferred_element_type=f32
+                left[:, stretch(flip(me, j), depth)],
+                rights[k % 2, :, cols],
+                OVER_ROWS,
+                preferred_element_type=f32,
             )
 
-        for j in (7, 5, 3, 1):
-            if j in odd_copies:
-                t.release(odd_copies[j])
-            odd[j // 2] = partial(j).astype(bf16)
-            odd_copies[j] = job.send_odd(j, odd.at[j // 2])
-        if k:
-            jobs[k - 1].pass_on()
-        for j in (6, 2, 4, 0):
-            job.arrive(j)
-            job.even(j, partial(j))
-        if k:
-            close(k - 1)
-    jobs[2].pass_on()
-    down_out[...] = jobs[2].close().astype(bf16)
+        for i, j in enumerate(SLOTS):
+            if i == 2 and n:
+                jobs[n - 1].pass_on()
+            if j % 2:
+                if j in odd_copies:
+                    t.release(odd_copies[j])
+                odd[j // 2] = partial(j).astype(bf16)
+                odd_copies[j] = job.send_odd(j, odd.at[j // 2])
+            else:
+                job.arrive(j)
+                job.even(j, partial(j))
+        if n:
+            close(n - 1)
+    jobs[count - 1].pass_on()
+    close(count - 1)
     for copy in outs:
         copy.wait()
 
@@ -1234,7 +1253,7 @@
         feed_forward_row_body,
         [wide, wide, wide, jax.ShapeDtypeStruct((4 * rows, model), bf16)]
         + [high, jax.ShapeDtypeStruct((3, rows, model), bf16), high]
-        + [jax.ShapeDtypeStruct((3, 4, depth, model), bf16), low, summed, summed]
+        + [jax.ShapeDtypeStruct((6, 4, depth, model // 2), bf16), low, summed, summed]
         + [jax.ShapeDtypeStruct((depth, model), bf16), jax.ShapeDtypeStruct(top.shape, f32)],
         [ANY] * 6 + [VMEM] + [ANY] * 4 + [VMEM] * 2,
         [VMEM] + [ANY] * 6 + [VMEM],
@@ -1242,8 +1261,8 @@
             pltpu.VMEM((3, rows, model), bf16),
             pltpu.VMEM((3, rows, model), bf16),
             pltpu.VMEM((3, rows, model), bf16),
-            pltpu.VMEM((3, depth, model), bf16),
-            pltpu.VMEM((3, 2, depth, model), bf16),
+            pltpu.VMEM((6, depth, model // 2), bf16),
+            pltpu.VMEM((6, 2, depth, model // 2), bf16),
         ]
         + small_scratch(top.shape)
         + [
@@ -1256,11 +1275,11 @@
             dma((2,)),
             dma((2,)),
             dma((2,)),
-            dma((2,)),
+            dma((4,)),
             dma((5,)),
             dma((3,)),
         ],
-        3 + 5 + 1 + 3 * 10,
+        3 + 5 + 1 + 6 * 10,
         2,
         flops=54 * rows * model * units,
     )(h, dy, dy_rest, gate, up, down_own, down_rest, top)
@@ -1321,12 +1340,13 @@
             attended_ref[:, of_slot(j)], db_ref[...], OVER_ROWS, preferred_element_type=f32
         )
 
-    for j in (7, 5, 3, 1):
-        odd[j // 2] = partial(j).astype(bf16)
-        job.send_odd(j, odd.at[j // 2])
-    for j in (6, 2, 4, 0):
-        job.arrive(j)
-        job.even(j, partial(j))
+    for j in SLOTS:
+        if j % 2:
+            odd[j // 2] = partial(j).astype(bf16)
+            job.send_odd(j, odd.at[j // 2])
+        else:
+            job.arrive(j)
+            job.even(j, partial(j))
 
     loads[0].wait()
     loads[1].wait()
@@ -1478,23 +1498,45 @@
     def of_slot(j):
         return pl.ds(pl.multiple_of(flip(me, j) * depth, depth), depth)
 
-    for k, right in enumerate((dq_ref, dkv_ref)):
-        job = PlaneSum(t, cores.at[k], far.at[k], near.at[k], sums.at[k], totals.at[k])
+    half = cores.shape[3]
+    order = ((1, 1), (0, 1), (0, 0), (1, 0))
+    over = []
+
+    def close(n):
+        k, p = order[n]
+        totals[n] = jobs[n].close()
+        for d in (2 * p, 2 * p + 1):
+            if d:
+                first = (d % 2) * width
+                row_send[k, d - 1] = totals[n, :, first : first + width].astype(bf16)
+                over.append(t.start(row_send.at[k, d - 1], row_land.at[k, d - 1], fsdp=d))
+
+    for n, (k, p) in enumerate(order):
+        right = (dq_ref, dkv_ref)[k]
+        job = PlaneSum(t, cores.at[n], far.at[n], near.at[n], sums.at[n], totals.at[n])
         jobs.append(job)
 
         def partial(j):
             return lax.dot_general(
-                h_ref[:, of_slot(j)], right[...], OVER_ROWS, preferred_element_type=f32
+                h_ref[:, of_slot(j)],
+                right[:, p * half : (p + 1) * half],
+                OVER_ROWS,
+                preferred_element_type=f32,
             )
 
-        for j in (7, 5, 3, 1):
-            if j in odd_copies:
-                t.release(odd_copies[j])
-            odd[j // 2] = partial(j).astype(bf16)
-            odd_copies[j] = job.send_odd(j, odd.at[j // 2])
-        for j in (6, 2, 4, 0):
-            job.arrive(j)
-            job.even(j, partial(j))
+        for j in SLOTS:
+            if j % 2:
+                if j in odd_copies:
+                    t.release(odd_copies[j])
+                odd[j // 2] = partial(j).astype(bf16)
+                odd_copies[j] = job.send_odd(j, odd.at[j // 2])
+            else:
+                job.arrive(j)
+                job.even(j, partial(j))
+        if n:
+            jobs[n - 1].pass_on()
+        if n > 1:
+            close(n - 2)
 
     def grads(d):
         query = dq_ref[:, d * width : (d + 1) * width]
@@ -1519,13 +1561,12 @@
     for load in loads:
         load.wait()
     back(0)
-    jobs[0].pass_on()
+    jobs[3].pass_on()
     unit_loads[0].wait()
     back(1)
     unit_loads[2].start()
     unit_loads[1].wait()
     back(2)
-    jobs[1].pass_on()
     unit_loads[2].wait()
     back(3)
     x = x_ref[...].astype(f32)
@@ -1537,22 +1578,25 @@
         [jnp.sum(back_out[...] * unit, 0, keepdims=True), term_ref[1:8]], 0
     )
     gains.on(0)
-
-    def columns(d):
-        return pl.ds(d * width, width)
-
-    totals[0] = jobs[0].close()
+    close(2)
     gains.on(1)
-    first = RowSum(t, totals.at[0], row_send.at[0], row_land.at[0], columns)
     gains.on(2)
-    totals[1] = jobs[1].close()
-    second = RowSum(t, totals.at[1], row_send.at[1], row_land.at[1], columns)
+    close(3)
     gains.on(3)
     gains.on(4)
-    query_out[...] = first.close()
     gains.on(5)
     gain_out[...] = blocks[5]
-    total = second.close()
+    for copy in over:
+        copy.wait_recv()
+
+    def whole(n, k):
+        total = totals[n, :, :width]
+        for d in range(3):
+            total = total + row_land[k, d].astype(f32)
+        return total
+
+    query_out[...] = whole(2, 0)
+    total = whole(3, 1)
     for h in range(heads):
         start = 2 * h * HEAD_SIZE
         here = slice(h * HEAD_SIZE, (h + 1) * HEAD_SIZE)
@@ -1575,17 +1619,17 @@
         [VMEM] * 5 + [ANY],
         [VMEM] * 5 + [ANY] * 5,
         [
-            pltpu.VMEM((4, depth, model), bf16),
+            pltpu.VMEM((4, depth, model // 2), bf16),
             pltpu.VMEM(query.shape, bf16),
             pltpu.VMEM(key.shape, bf16),
             pltpu.VMEM(value.shape, bf16),
             pltpu.VMEM((2,) + rest.shape[1:], bf16),
         ]
-        + plane_sum_scratch(2, depth, model)
+        + plane_sum_scratch(4, depth, model // 2)
         + [pltpu.VMEM((2, 3, depth, width), bf16)] * 2
         + small_scratch(terms.shape)
         + [dma((3,)), dma((3,))],
-        2 * (10 + 3) + 5 + 1,
+        4 * 10 + 6 + 5 + 1,
         5,
         flops=12 * rows * model * model,
     )(h, dq, dkv, x, terms, query, key, value, rest, y_rest)

time: 677 us -> 667 us (0.985)
  Pallas kernels: 616 us -> 606 us
    pallas_call x1, Pallas kernels: 122 us -> 114 us  [unit_grads(): remote_call(unit_grads_body, [wide, half, half, jax.ShapeDtypeStruct((row...]
  transfers between devices with their start and end apart: 4 -> 4, of which waited for: 0 -> 0; matrix products, arithmetic and copies ran while one was open for 3% -> 3% of each run, Pallas kernels for 31% -> 30%
where the time goes in v6:
time: 667 us; the launch traced here: 658 us
  Pallas kernels  606 us (91%)
  other arithmetic  26.3 us (4%)
  local copies, waits for them, and re-layouts  15.6 us (2%)
  starting transfers between devices  7.9 us (1%)
    pallas_call x1, Pallas kernels, feed_forward_row(): remote_call(feed_forward_row_body, [wide, wide, wide, jax.ShapeDtypeStruc...  226 us
    pallas_call x1, Pallas kernels, attention_row(): remote_call(attention_row_body, [out((rows, model)), out((rows, 4 * width...  180 us
    pallas_call x1, Pallas kernels, unit_grads(): remote_call(unit_grads_body, [wide, half, half, jax.ShapeDtypeStruct((row...  114 us
    pallas_call x1, Pallas kernels, attention_back(): remote_call(attention_back_body, [jax.ShapeDtypeStruct((rows, model), bf1...  85.6 us
  transfers between devices with their start and end apart: 4, of which 0 were waited for; matrix products, arithmetic and copies ran while one was open for 3% of the time, Pallas kernels for 30%

profile of v6, /device:TPU:0, one launch (start us, length us, event | category | flops | bytes accessed | tf_op | source)
XLA Modules:
  0.0 657.6 jit_solution(4254925674253897331)
XLA Ops:
  0.7 1.3 iota_reduce_fusion
  2.1 0.8 reduce-window.4
  3.6 0.7 stack.36
  4.3 0.7 stack.37
  5.3 0.8 copy.54.begin_ref
  6.1 0.8 copy.53.natural_ref
  8.0 0.8 pad_maximum_fusion
  9.5 180.2 %shard_map.245 = (bf16[256,2048]{1,0:T(8,128)(2,1)}, bf16[256,4096]{1,0:T(8,128)(2,1)}, bf16[256,2048]{1,0:T(8,128)(2,1)}, f32[2,8,8,128]{3,2,1,0:T(8,128)}, f32...) custom-call(bf16[256,2048]{1,0:T(8,128)(2,1)} %bitcast.65, ...), custom_call_target="tpu_custom_call" | custom-call | flops 10737418240 | bytes 4194304 | tf_op jit(solution)/shard_map/pallas_call | solution.py:815
  189.7 0.9 slice_reduce_fusion
  191.3 226.2 %shard_map.246 = (bf16[1024,2048]{1,0:T(8,128)(2,1)}, bf16[1024,2048]{1,0:T(8,128)(2,1)}, bf16[1024,2048]{1,0:T(8,128)(2,1)}, bf16[1024,2048]{1,0:T(8,128)(2,1)}...) custom-call(bf16[256,2048]{1,0:T(8,128)(2,1)} %get-tuple-element.52., ...), custom_call_target="tpu_custom_call" | custom-call | flops 57982058496 | bytes 4194304 | tf_op jit(solution)/shard_map/pallas_call | solution.py:1252
  417.4 2.2 constant_dynamic-slice_fusion.1
  419.7 4.2 collective-permute-start
  423.9 1.9 collective-permute-start.1
  426.1 1.5 collective-permute-start.3
  428.6 2.2 multiply_reduce_fusion
  431.7 2.5 multiply_convert_fusion.1
  434.2 1.6 fusion.26.db_ref
  435.8 85.6 %shard_map.247 = (bf16[256,2048]{1,0:T(8,128)(2,1)}, bf16[256,2048]{1,0:T(8,128)(2,1)}, f32[256,512]{1,0:T(8,128)}, bf16[256,2048]{1,0:T(8,128)(2,1)}) custom-call(bf16[256,2048]{1,0:T(8,128)(2,1)} %fusion.26.db_ref, bf16[256,2048]{1,0:T(8,128)(2,1)} %get-tuple-element.62.attended_ref, bf16[256,4096]{1,0:T(8,128)(2,1)} %get-tuple-element.63.qkv_ref, ...), custom_call_target="tpu_custom_call" | custom-call | flops 21474836480 | bytes 4194304 | tf_op jit(solution)/shard_map/pallas_call | solution.py:1447
  521.4 114.3 %shard_map.248 = (f32[256,512]{1,0:T(8,128)}, f32[256,256]{1,0:T(8,128)}, f32[256,256]{1,0:T(8,128)}, f32[256,2048]{1,0:T(8,128)}, f32[8,2048]{1,0:T(8,128)}, /*index=5*/bf16[256,2048]{1,0:T(8,128)(2,1)}) custom-call(bf16[256,2048]{1,0:T(8,128)(2,1)} %get-tuple-element.68.h_ref, bf16[256,2048]{1,0:T(8,128)(2,1)} %get-tuple-element.69.dq_ref, ...), custom_call_target="tpu_custom_call" | custom-call | flops 12884901888 | bytes 4194304 | tf_op jit(solution)/shard_map/pallas_call | solution.py:1615
  635.8 2.2 fusion.2
  638.0 0.8 slice.88
  638.9 1.8 multiply_convert_fusion
  640.8 6.0 fusion.9
  647.4 1.3 broadcast_select_fusion.7
  648.8 1.6 maximum_convert_fusion
  650.4 0.8 copy.63
  651.2 0.7 copy.64
  651.9 0.7 copy.65
  652.6 0.8 copy.66
  653.4 1.3 copy.67
  654.7 1.0 copy-done.6
  655.7 1.3 copy.68
  (71 shorter events, 6.3 us)
Async XLA Ops:
  191.3 236.4 %copy-start.3 = (bf16[1,256,2048]{2,1,0:T(8,128)(2,1)S(1)}, bf16[1,256,2048]{2,1,0:T(8,128)(2,1)}, u32[]{:S(2)}) copy-start(bf16[1,256,2048]{2,1,0:T(8,128)(2,1)} %param.14) | copy-start | bytes 3145732
  417.4 10.5 %copy-start = (f32[256,2048]{1,0:T(8,128)S(1)}, f32[256,2048]{1,0:T(8,128)}, u32[]{:S(2)}) copy-start(f32[256,2048]{1,0:T(8,128)} %get-tuple-element.51) | copy-start | bytes 6291460
  419.7 8.5 %copy-start.14 = (f32[8,128]{1,0:T(8,128)S(1)}, f32[8,128]{1,0:T(8,128)}, u32[]{:S(2)}) copy-start(f32[8,128]{1,0:T(8,128)} %get-tuple-element.85) | copy-start | bytes 12292
  419.7 8.6 %copy-start.16 = (f32[16]{0:T(128)S(1)}, f32[16]{0:T(128)}, u32[]{:S(2)}) copy-start(f32[16]{0:T(128)} %param.27) | copy-start | bytes 196
  419.7 8.8 %copy-start.13 = (f32[4,8,512]{2,1,0:T(8,128)S(1)}, f32[4,8,512]{2,1,0:T(8,128)}, u32[]{:S(2)}) copy-start(f32[4,8,512]{2,1,0:T(8,128)} %get-tuple-element.59) | copy-start | bytes 196612
  419.7 227.7 %collective-permute-start = (bf16[256,512]{1,0:T(8,128)(2,1)}, bf16[256,512]{1,0:T(8,128)(2,1)}, u32[]{:S(2)}, u32[]{:S(2)}) collective-permute-start(bf16[256,512]{1,0:T(8,128)(2,1)} %get-tuple-element.81), channel_id=1, source_target_pairs={{0,3},{1,11},{2,19},{3,27},{4,2},{5,10},{6,18},{7,26},{8,1},{9,9},... | collective-permute-start | bytes 786440 | tf_op jit(solution)/shard_map/ppermute | solution.py:2011
  423.9 223.5 %collective-permute-start.1 = (bf16[256,512]{1,0:T(8,128)(2,1)}, bf16[256,512]{1,0:T(8,128)(2,1)}, u32[]{:S(2)}, u32[]{:S(2)}) collective-permute-start(bf16[256,512]{1,0:T(8,128)(2,1)} %get-tuple-element.82), channel_id=1, source_target_pairs={{0,2},{1,10},{2,18},{3,26},{4,3},{5,11},{6,19},{7,27},{8,0},{9,8},... | collective-permute-start | bytes 786440 | tf_op jit(solution)/shard_map/ppermute | solution.py:2011
  425.8 221.6 %collective-permute-start.2 = (bf16[256,512]{1,0:T(8,128)(2,1)}, bf16[256,512]{1,0:T(8,128)(2,1)}, u32[]{:S(2)}, u32[]{:S(2)}) collective-permute-start(bf16[256,512]{1,0:T(8,128)(2,1)} %get-tuple-element.83), channel_id=1, source_target_pairs={{0,1},{1,9},{2,17},{3,25},{4,0},{5,8},{6,16},{7,24},{8,3},{9,11},{... | collective-permute-start | bytes 786440 | tf_op jit(solution)/shard_map/ppermute | solution.py:2011
  426.1 221.3 %collective-permute-start.3 = (bf16[256,512]{1,0:T(8,128)(2,1)S(1)}, bf16[256,512]{1,0:T(8,128)(2,1)}, u32[]{:S(2)}, u32[]{:S(2)}) collective-permute-start(bf16[256,512]{1,0:T(8,128)(2,1)S(1)} %get-tuple-element.84), channel_id=1, source_target_pairs={{0,0},{1,8},{2,16},{3,24},{4,1},{5,9},{6,17},{7,25},{8,2},{9,10},{... | collective-permute-start | bytes 786440 | tf_op jit(solution)/shard_map/ppermute | solution.py:2011
  428.3 2.5 copy-start.15
  428.5 5.7 copy-start.5
  431.6 2.6 copy-start.2
  521.4 114.3 %copy-start.4 = (bf16[1,256,2048]{2,1,0:T(8,128)(2,1)S(1)}, bf16[1,256,2048]{2,1,0:T(8,128)(2,1)}, u32[]{:S(2)}) copy-start(bf16[1,256,2048]{2,1,0:T(8,128)(2,1)} %param.14) | copy-start | bytes 3145732
  635.7 3.1 copy-start.8
  638.9 2.0 copy-start.1
  648.7 1.7 copy-start.10
  648.7 2.4 copy-start.12
  648.7 3.1 copy-start.11
  648.8 3.8 copy-start.9
  650.4 3.0 copy-start.7
  653.4 2.3 copy-start.6

commit v7 on v6

--- a/solution.py
+++ b/solution.py
@@ -699,6 +699,7 @@
     output_row.first()
     for row in unit_rows:
         row.third()
+    dy_row.begin()
     unit_plane[3].begin()
     downs = []
     for d in (1, 2, 3):
@@ -708,7 +709,6 @@
                 down_ref.at[pl.ds(pl.multiple_of(row, depth), depth)], down_out.at[d - 1, 0], fsdp=d
             )
         )
-    dy_row.begin()
     unit_plane[2].middle()
     unit_plane[1].end()
     output_row.second()
@@ -725,13 +725,13 @@
     unit_plane[3].end()
     kv_plane[0].ready()
     attend_heads(0)
+    dy_row.first()
     unit_plane[3].ready()
     project(3)
     kv_plane[3].begin()
     kv_plane[2].middle()
     kv_plane[1].end()
     output_plane[1].begin()
-    dy_row.first()
     kv_plane[3].middle()
     kv_plane[2].end()
     output_plane[2].begin()
@@ -742,11 +742,11 @@
     output_plane[3].begin()
     kv_plane[2].ready()
     attend_heads(2)
+    dy_row.second()
     output_plane[2].middle()
     output_plane[1].end()
     downs[0].wait_recv()
     down_plane[1].begin()
-    dy_row.second()
     kv_plane[3].ready()
     attend_heads(3)
     output_plane[3].middle()
@@ -989,7 +989,9 @@
         pltpu.VMEM((rows, model), bf16),
         pltpu.VMEM((2, 3, rows, TILE), bf16),
     )
-    y_copy = t.start((y_rest, 0), y_land, fsdp=1)
+    y_copies = [
+        t.start((y_rest, d - 1), (y_land, d // 2), fsdp=d) for d in (1, 3)
+    ]
 
     def grads(left, rights, odd, sums, totals, fetched):
         feed_forward_grads(
@@ -1015,7 +1017,8 @@
         back_out[...] += back_land[d].astype(f32)
     tops.on(5)
     top_out[...] = blocks[5]
-    y_copy.wait_recv()
+    for copy in y_copies:
+        copy.wait_recv()
     row.finish()
     t.finish()
 
@@ -1245,7 +1248,6 @@
     tiles = units // TILE
     depth = model // 8
     wide = jax.ShapeDtypeStruct((4 * rows, units), bf16)
-    low = jax.ShapeDtypeStruct((rows, model), bf16)
     high = jax.ShapeDtypeStruct((rows, model), f32)
     summed = jax.ShapeDtypeStruct((depth, units), f32)
     dma = pltpu.SemaphoreType.DMA
@@ -1253,7 +1255,8 @@
         feed_forward_row_body,
         [wide, wide, wide, jax.ShapeDtypeStruct((4 * rows, model), bf16)]
         + [high, jax.ShapeDtypeStruct((3, rows, model), bf16), high]
-        + [jax.ShapeDtypeStruct((6, 4, depth, model // 2), bf16), low, summed, summed]
+        + [jax.ShapeDtypeStruct((6, 4, depth, model // 2), bf16)]
+        + [jax.ShapeDtypeStruct((2, rows, model), bf16), summed, summed]
         + [jax.ShapeDtypeStruct((depth, model), bf16), jax.ShapeDtypeStruct(top.shape, f32)],
         [ANY] * 6 + [VMEM] + [ANY] * 4 + [VMEM] * 2,
         [VMEM] + [ANY] * 6 + [VMEM],
@@ -1279,7 +1282,7 @@
             dma((5,)),
             dma((3,)),
         ],
-        3 + 5 + 1 + 6 * 10,
+        3 + 5 + 2 + 6 * 10,
         2,
         flops=54 * rows * model * units,
     )(h, dy, dy_rest, gate, up, down_own, down_rest, top)
@@ -1472,8 +1475,8 @@
 
 
 def unit_grads_body(
-    h_ref, dq_ref, dkv_ref, x_ref, term_ref, q_ref, k_ref, v_ref, unit_rest, y_ref,
-    query_out, key_out, value_out, back_out, gain_out, y_land,
+    h_ref, dq_ref, dkv_ref, x_ref, term_ref, q_ref, k_ref, v_ref, unit_rest,
+    query_out, key_out, value_out, back_out, gain_out,
     odd, q_own, k_own, v_own, units, cores, far, near, sums, totals, row_send, row_land,
     blocks, land, load_sem, unit_sem, send, recv,
 ):
@@ -1492,7 +1495,6 @@
         load.start()
     greet((1, 2, 4), (1, 2, 3))
     t = Transfers(send, recv)
-    y_copy = t.start(y_ref.at[2], y_land, fsdp=3)
     jobs, odd_copies = [], {}
 
     def of_slot(j):
@@ -1602,11 +1604,10 @@
         here = slice(h * HEAD_SIZE, (h + 1) * HEAD_SIZE)
         key_out[:, here] = total[:, start : start + HEAD_SIZE]
         value_out[:, here] = total[:, start + HEAD_SIZE : start + 2 * HEAD_SIZE]
-    y_copy.wait_recv()
     t.finish()
 
 
-def unit_grads(h, dq, dkv, x, terms, query, key, value, rest, y_rest):
+def unit_grads(h, dq, dkv, x, terms, query, key, value, rest):
     rows, model = h.shape
     depth, width = model // 8, model // 4
     wide = jax.ShapeDtypeStruct((depth, width), f32)
@@ -1615,9 +1616,9 @@
     return remote_call(
         unit_grads_body,
         [wide, half, half, jax.ShapeDtypeStruct((rows, model), f32)]
-        + [jax.ShapeDtypeStruct(terms.shape, f32), jax.ShapeDtypeStruct((rows, model), bf16)],
-        [VMEM] * 5 + [ANY],
-        [VMEM] * 5 + [ANY] * 5,
+        + [jax.ShapeDtypeStruct(terms.shape, f32)],
+        [VMEM] * 5,
+        [VMEM] * 5 + [ANY] * 4,
         [
             pltpu.VMEM((4, depth, model // 2), bf16),
             pltpu.VMEM(query.shape, bf16),
@@ -1629,10 +1630,10 @@
         + [pltpu.VMEM((2, 3, depth, width), bf16)] * 2
         + small_scratch(terms.shape)
         + [dma((3,)), dma((3,))],
-        4 * 10 + 6 + 5 + 1,
+        4 * 10 + 6 + 5,
         5,
         flops=12 * rows * model * model,
-    )(h, dq, dkv, x, terms, query, key, value, rest, y_rest)
+    )(h, dq, dkv, x, terms, query, key, value, rest)
 
 
 def token_layout(length_row, block_slots, block_size):
@@ -2026,7 +2027,7 @@
         y_rest,
     )
     terms = jnp.pad(second_term[None], ((1, 6), (0, 0)))
-    query_out, key_out, value_out, grad_normed_one, terms, y_third = unit_grads(
+    query_out, key_out, value_out, grad_normed_one, terms = unit_grads(
         normalized,
         query_grad,
         dkv,
@@ -2036,9 +2037,8 @@
         key_matrix,
         value_matrix,
         unit_rest,
-        y_rest,
-    )
-    landed = y_near.astype(f32) + y_second.astype(f32) + y_third.astype(f32)
+    )
+    landed = y_near[0].astype(f32) + y_second.astype(f32) + y_near[1].astype(f32)
     result = (residual + y_own + landed).astype(bf16)
     grad_input = grad_residual + norm_back(grad_normed_one * first_full, unit_one, scale_one)
     terms = lax.dynamic_slice_in_dim(

time: 667 us -> 656 us (0.984)
  Pallas kernels: 606 us -> 595 us
    pallas_call x1, Pallas kernels: 114 us -> 104 us  [unit_grads(): remote_call(unit_grads_body, [wide, half, half, jax.ShapeDtypeStruct((row...]
  transfers between devices with their start and end apart: 4 -> 4, of which waited for: 0 -> 0; matrix products, arithmetic and copies ran while one was open for 3% -> 3% of each run, Pallas kernels for 30% -> 29%
where the time goes in v7:
time: 656 us; the launch traced here: 647 us
  Pallas kernels  595 us (91%)
  other arithmetic  26.1 us (4%)
  local copies, waits for them, and re-layouts  15.7 us (2%)
  starting transfers between devices  7.93 us (1%)
    pallas_call x1, Pallas kernels, feed_forward_row(): remote_call(feed_forward_row_body, [wide, wide, wide, jax.ShapeDtypeStruc...  226 us
    pallas_call x1, Pallas kernels, attention_row(): remote_call(attention_row_body, [out((rows, model)), out((rows, 4 * width...  180 us
    pallas_call x1, Pallas kernels, unit_grads(): remote_call(unit_grads_body, [wide, half, half, jax.ShapeDtypeStruct((row...  104 us
    pallas_call x1, Pallas kernels, attention_back(): remote_call(attention_back_body, [jax.ShapeDtypeStruct((rows, model), bf1...  85.5 us
  transfers between devices with their start and end apart: 4, of which 0 were waited for; matrix products, arithmetic and copies ran while one was open for 3% of the time, Pallas kernels for 29%

profile of v7, /device:TPU:0, one launch (start us, length us, event | category | flops | bytes accessed | tf_op | source)
XLA Modules:
  0.0 646.6 jit_solution(1448411932375587095)
XLA Ops:
  0.7 1.3 iota_reduce_fusion
  2.1 0.8 reduce-window.4
  3.6 0.7 stack.36
  4.3 0.7 stack.37
  5.3 0.8 copy.54.begin_ref
  6.1 0.8 copy.53.natural_ref
  8.0 0.8 pad_maximum_fusion
  9.5 180.0 %shard_map.245 = (bf16[256,2048]{1,0:T(8,128)(2,1)}, bf16[256,4096]{1,0:T(8,128)(2,1)}, bf16[256,2048]{1,0:T(8,128)(2,1)}, f32[2,8,8,128]{3,2,1,0:T(8,128)}, f32...) custom-call(bf16[256,2048]{1,0:T(8,128)(2,1)} %bitcast.71, ...), custom_call_target="tpu_custom_call" | custom-call | flops 10737418240 | bytes 4194304 | tf_op jit(solution)/shard_map/pallas_call | solution.py:815
  189.5 0.9 slice_reduce_fusion
  191.1 226.2 %shard_map.246 = (bf16[1024,2048]{1,0:T(8,128)(2,1)}, bf16[1024,2048]{1,0:T(8,128)(2,1)}, bf16[1024,2048]{1,0:T(8,128)(2,1)}, bf16[1024,2048]{1,0:T(8,128)(2,1)}...) custom-call(bf16[256,2048]{1,0:T(8,128)(2,1)} %get-tuple-element.51., ...), custom_call_target="tpu_custom_call" | custom-call | flops 57982058496 | bytes 4194304 | tf_op jit(solution)/shard_map/pallas_call | solution.py:1254
  417.3 2.2 constant_dynamic-slice_fusion.1
  419.6 4.2 collective-permute-start
  423.7 1.9 collective-permute-start.1
  426.0 1.5 collective-permute-start.3
  428.4 2.2 multiply_reduce_fusion
  431.6 2.5 multiply_convert_fusion.1
  434.1 1.6 fusion.28.db_ref
  435.7 85.5 %shard_map.247 = (bf16[256,2048]{1,0:T(8,128)(2,1)}, bf16[256,2048]{1,0:T(8,128)(2,1)}, f32[256,512]{1,0:T(8,128)}, bf16[256,2048]{1,0:T(8,128)(2,1)}) custom-call(bf16[256,2048]{1,0:T(8,128)(2,1)} %fusion.28.db_ref, bf16[256,2048]{1,0:T(8,128)(2,1)} %get-tuple-element.61.attended_ref, bf16[256,4096]{1,0:T(8,128)(2,1)} %get-tuple-element.62.qkv_ref, ...), custom_call_target="tpu_custom_call" | custom-call | flops 21474836480 | bytes 4194304 | tf_op jit(solution)/shard_map/pallas_call | solution.py:1450
  521.2 103.6 %shard_map.248 = (f32[256,512]{1,0:T(8,128)}, f32[256,256]{1,0:T(8,128)}, f32[256,256]{1,0:T(8,128)}, f32[256,2048]{1,0:T(8,128)}, f32[8,2048]{1,0:T(8,128)}) custom-call(bf16[256,2048]{1,0:T(8,128)(2,1)} %get-tuple-element.67.h_ref, bf16[256,2048]{1,0:T(8,128)(2,1)} %get-tuple-element.68.dq_ref, bf16[256,2048]{1,0:T(8,128)(2,1)} %get-tuple-element.69.dkv_ref, ...), custom_call_target="tpu_custom_call" | custom-call | flops 12884901888 | bytes 4194304 | tf_op jit(solution)/shard_map/pallas_call | solution.py:1616
  624.8 1.0 slice.96
  625.8 2.1 fusion.2
  627.9 1.8 multiply_convert_fusion
  629.9 6.0 fusion.11
  636.5 1.3 broadcast_select_fusion.7
  637.8 1.6 maximum_convert_fusion
  639.4 0.8 copy.63
  640.2 0.7 copy.64
  640.9 0.7 copy.65
  641.6 0.8 copy.66
  642.4 1.3 copy.67
  643.8 1.0 copy-done.6
  644.8 1.3 copy.68
  (71 shorter events, 6.4 us)
Async XLA Ops:
  191.1 236.5 %copy-start.3 = (bf16[1,256,2048]{2,1,0:T(8,128)(2,1)S(1)}, bf16[1,256,2048]{2,1,0:T(8,128)(2,1)}, u32[]{:S(2)}) copy-start(bf16[1,256,2048]{2,1,0:T(8,128)(2,1)} %param.14) | copy-start | bytes 3145732
  417.3 10.6 %copy-start = (f32[256,2048]{1,0:T(8,128)S(1)}, f32[256,2048]{1,0:T(8,128)}, u32[]{:S(2)}) copy-start(f32[256,2048]{1,0:T(8,128)} %get-tuple-element.50) | copy-start | bytes 6291460
  419.5 8.6 %copy-start.14 = (f32[8,128]{1,0:T(8,128)S(1)}, f32[8,128]{1,0:T(8,128)}, u32[]{:S(2)}) copy-start(f32[8,128]{1,0:T(8,128)} %get-tuple-element.83) | copy-start | bytes 12292
  419.5 8.6 %copy-start.16 = (f32[16]{0:T(128)S(1)}, f32[16]{0:T(128)}, u32[]{:S(2)}) copy-start(f32[16]{0:T(128)} %param.27) | copy-start | bytes 196
  419.5 8.8 %copy-start.13 = (f32[4,8,512]{2,1,0:T(8,128)S(1)}, f32[4,8,512]{2,1,0:T(8,128)}, u32[]{:S(2)}) copy-start(f32[4,8,512]{2,1,0:T(8,128)} %get-tuple-element.58) | copy-start | bytes 196612
  419.6 216.9 %collective-permute-start = (bf16[256,512]{1,0:T(8,128)(2,1)}, bf16[256,512]{1,0:T(8,128)(2,1)}, u32[]{:S(2)}, u32[]{:S(2)}) collective-permute-start(bf16[256,512]{1,0:T(8,128)(2,1)} %get-tuple-element.79), channel_id=1, source_target_pairs={{0,3},{1,11},{2,19},{3,27},{4,2},{5,10},{6,18},{7,26},{8,1},{9,9},... | collective-permute-start | bytes 786440 | tf_op jit(solution)/shard_map/ppermute | solution.py:2012
  423.7 212.7 %collective-permute-start.1 = (bf16[256,512]{1,0:T(8,128)(2,1)}, bf16[256,512]{1,0:T(8,128)(2,1)}, u32[]{:S(2)}, u32[]{:S(2)}) collective-permute-start(bf16[256,512]{1,0:T(8,128)(2,1)} %get-tuple-element.80), channel_id=1, source_target_pairs={{0,2},{1,10},{2,18},{3,26},{4,3},{5,11},{6,19},{7,27},{8,0},{9,8},... | collective-permute-start | bytes 786440 | tf_op jit(solution)/shard_map/ppermute | solution.py:2012
  425.7 210.8 %collective-permute-start.2 = (bf16[256,512]{1,0:T(8,128)(2,1)}, bf16[256,512]{1,0:T(8,128)(2,1)}, u32[]{:S(2)}, u32[]{:S(2)}) collective-permute-start(bf16[256,512]{1,0:T(8,128)(2,1)} %get-tuple-element.81), channel_id=1, source_target_pairs={{0,1},{1,9},{2,17},{3,25},{4,0},{5,8},{6,16},{7,24},{8,3},{9,11},{... | collective-permute-start | bytes 786440 | tf_op jit(solution)/shard_map/ppermute | solution.py:2012
  426.0 210.5 %collective-permute-start.3 = (bf16[256,512]{1,0:T(8,128)(2,1)S(1)}, bf16[256,512]{1,0:T(8,128)(2,1)}, u32[]{:S(2)}, u32[]{:S(2)}) collective-permute-start(bf16[256,512]{1,0:T(8,128)(2,1)S(1)} %get-tuple-element.82), channel_id=1, source_target_pairs={{0,0},{1,8},{2,16},{3,24},{4,1},{5,9},{6,17},{7,25},{8,2},{9,10},{... | collective-permute-start | bytes 786440 | tf_op jit(solution)/shard_map/ppermute | solution.py:2012
  428.2 2.5 copy-start.15
  428.4 5.7 copy-start.5
  431.5 2.6 copy-start.2
  521.2 104.6 %copy-start.4 = (bf16[1,256,2048]{2,1,0:T(8,128)(2,1)S(1)}, bf16[1,256,2048]{2,1,0:T(8,128)(2,1)}, u32[]{:S(2)}) copy-start(bf16[1,256,2048]{2,1,0:T(8,128)(2,1)} %param.14) | copy-start | bytes 3145732
  624.8 3.1 copy-start.8
  627.9 2.0 copy-start.1
  637.8 1.7 copy-start.10
  637.8 2.4 copy-start.12
  637.8 3.1 copy-start.11
  637.8 3.8 copy-start.9
  639.4 3.0 copy-start.7
  642.4 2.3 copy-start.6
